TPU v7x, 128 devices: a whole 4x4x4 slice. The times are simulated.
128 devices in a mesh: span: 4 (over z), dom: 32 (over y, x, core).
Axes of the slice: x: 4, y: 4, z: 4, core: 2. Of those that a mesh axis runs over, the one named last changes fastest.
Arguments:
- adjoint_rhs: float32 [6, 128, 32768], P(None, 'span', 'dom'), may hold values from -6 to 6
- block_inverse: float32 [6, 6, 128, 32768], P(None, None, 'span', 'dom')
- coupling: float32 [4, 128, 32768], P(None, 'span', 'dom'), may hold values from 0.05 to 0.25
- distance_grad: float32 [1, 128, 32768], P(None, 'span', 'dom'), may hold values from -6 to 6
- slot_cell: int32 [4, 32, 65536], P('span', 'dom'), may hold values from 0 to 32768, as said below
- slot_face: int32 [4, 32, 65536], P('span', 'dom'), may hold values from 0 to 8192, as said below
- area_grad: float32 [3, 4, 262144], P(None, None, 'dom'), may hold values from -6 to 6
- face_nodes: int32 [4, 262144], P(None, 'dom'), may hold values from 0 to 131071, as said below
Outputs:
- adjoint: float32 [6, 128, 32768], P(None, 'span', 'dom')
- face_sens: float32 [262144], P('dom')
- node_sens: float32 [3, 131072], P(None, 'dom')
Inputs may be any that keep to these rules, and one draw needn't show every extreme that they name: `slot_cell`: entry [s, i, j * 2048 + k] is a local cell of device (s, i) sent to face owner j, or the pad 32768; each owner's live slots come first, every local cell stands in exactly one slot, and one owner has all 2048 slots live from every device. `slot_face`: entry [s, j, i * 2048 + k] is the owner-local wall face of owner j nearest to the cell in slot j * 2048 + k of device (s, i), and is the pad 8192 exactly where that slot is a pad. `face_nodes`: node n is owned by dom index n // 4096; the nodes of face g are owned by dom index i = g // 8192, by one of its two neighbours, or by the index i + 16, all counted periodically along dom.
All inputs are finite; a program needn't handle non-finite values.
Results may differ from a plain program's by a relative error of at most 0.00011.
Values sent between devices are 32-bit elements; how exact they have to be, the bound alone decides.
No kernel may reach another device: no remote copies, remote signals or barrier semaphores. Data moves between devices by JAX's collectives and lax.ppermute only.
A program may use at most 192 MiB of HBM per device.

v0:
```python
import jax
import jax.numpy as jnp
from jax import lax
from jax.sharding import PartitionSpec as P

NVAR = 6
SWEEPS = 4
FACE_DEV = 8192
NODE_DEV = 4096


def with_halo(cells, sides, width, closed):
    for axis, dim in sides:
        count = lax.axis_size(axis)
        ends = count if closed else count - 1
        head = lax.slice_in_dim(cells, 0, width, axis=dim)
        tail = lax.slice_in_dim(cells, cells.shape[dim] - width, cells.shape[dim], axis=dim)
        cells = jnp.concatenate(
            [
                lax.ppermute(tail, axis, [(i, (i + 1) % count) for i in range(ends)]),
                cells,
                lax.ppermute(head, axis, [((i + 1) % count, i) for i in range(ends)]),
            ],
            axis=dim,
        )
    return cells


def apply_inverse(inverse, vector):
    return jnp.einsum("baxy,bxy->axy", inverse, vector, precision=lax.Precision.HIGHEST)


def relax_sweep(field, coupling, inverse, objective):
    total = (coupling[1:2] * field)[:, 2:, 1:-1] + (coupling[0:1] * field)[:, :-2, 1:-1]
    total = total + (coupling[3:4] * field)[:, 1:-1, 2:] + (coupling[2:3] * field)[:, 1:-1, :-2]
    return apply_inverse(inverse, objective - total)


def rimmed(field, width):
    spanwise = with_halo(field, (("span", 1),), width, False)
    return with_halo(spanwise, (("dom", 2),), width, True)


def node_sums(contrib, node_index, count):
    flat_index = node_index.reshape(-1)
    return jax.vmap(lambda part: jax.ops.segment_sum(part.reshape(-1), flat_index, count))(contrib)


def shards(
    adjoint_rhs, block_inverse, coupling, distance_grad, slot_cell, slot_face, area_grad, face_nodes
):
    coupling_ext = rimmed(coupling, 1)
    adjoint = apply_inverse(block_inverse, adjoint_rhs)
    for sweep in range(SWEEPS):
        adjoint = relax_sweep(rimmed(adjoint, 1), coupling_ext, block_inverse, adjoint_rhs)
    cell_sens = (distance_grad[0] * adjoint[NVAR - 1]).reshape(-1)
    owners = lax.axis_size("dom")
    padded = jnp.concatenate([cell_sens, jnp.zeros((1,), jnp.float32)])
    send_list = slot_cell.reshape(-1)
    slot_vals = padded[send_list].reshape(owners, send_list.shape[0] // owners)
    received = lax.all_to_all(slot_vals, "dom", split_axis=0, concat_axis=0, tiled=True)
    face_part = jax.ops.segment_sum(received.reshape(-1), slot_face.reshape(-1), FACE_DEV + 1)[
        :FACE_DEV
    ]
    face_sens = lax.psum(face_part, "span")
    contrib = area_grad * face_sens[None, None, :]
    dense = node_sums(contrib, face_nodes, NODE_DEV * owners)
    node_sens = lax.psum_scatter(dense, "dom", scatter_dimension=1, tiled=True)
    return (adjoint, face_sens, node_sens)


def solution(mesh):
    in_specs = (
        P(None, "span", "dom"),
        P(None, None, "span", "dom"),
        P(None, "span", "dom"),
        P(None, "span", "dom"),
        P("span", "dom", None),
        P("span", "dom", None),
        P(None, None, "dom"),
        P(None, "dom"),
    )
    out_specs = (P(None, "span", "dom"), P("dom"), P(None, "dom"))
    return jax.shard_map(shards, mesh=mesh, in_specs=in_specs, out_specs=out_specs, check_vma=False)
```

profile of v0, /device:TPU:0, one launch (start us, length us, event | category | flops | bytes accessed | tf_op | source)
XLA Modules:
  0.0 1939.0 jit_solution(13456986044448331289)
XLA Ops:
  7.2 1.1 fusion.38
  8.2 3.9 collective-permute-start
  12.1 1.3 collective-permute-start.1
  13.4 3.3 multiply_reduce_fusion.4
  16.8 4.5 collective-permute-start.4
  21.3 1.3 collective-permute-start.5
  22.9 4.1 collective-permute-start.3
  26.9 2.1 collective-permute-done.3
  29.0 5.1 collective-permute-done.2
  34.1 1.1 concatenate.34
  36.1 1.2 slice_bitcast_fusion.2
  38.0 5.4 collective-permute-done.6
  43.4 1.5 concatenate.36
  44.9 0.7 fusion.23
  45.6 3.1 multiply_reduce_fusion.3
  48.8 4.3 collective-permute-start.8
  53.1 1.3 collective-permute-start.9
  54.6 4.2 collective-permute-done.9
  59.6 1.9 collective-permute-done.11
  61.5 5.4 collective-permute-done.10
  66.9 1.5 concatenate.38
  68.4 0.7 fusion.18
  69.1 3.1 multiply_reduce_fusion.2
  72.3 3.6 collective-permute-start.12
  75.9 1.3 collective-permute-start.13
  77.4 4.2 collective-permute-done.13
  82.5 1.9 collective-permute-done.15
  84.4 5.4 collective-permute-done.14
  89.8 1.5 concatenate.40
  91.3 0.7 fusion.13
  92.0 3.1 multiply_reduce_fusion.1
  95.2 3.5 collective-permute-start.16
  98.7 1.3 collective-permute-start.17
  100.3 4.1 collective-permute-done.17
  105.8 0.7 broadcast_clamp_fusion
  106.5 11.1 sort
  118.3 1.7 concatenate.42
  120.0 0.7 fusion.8
  120.7 3.1 multiply_reduce_fusion
  124.0 639.6 %gather_fusion = f32[65536]{0:T(1024)} fusion(f32[32769]{0:T(1024)S(1)} %pad_maximum_fusion.5, s32[65536]{0:T(1024)S(1)} %copy-done.2), kind=kCustom, calls=%fused_computation | custom fusion | bytes 786432 | tf_op jit(solution)/shard_map/gather | solution.py:60
  763.5 6.3 all-to-all-start
  769.9 8.8 all-to-all-done
  778.7 370.7 %scatter_custom_fusion = f32[8193]{0:T(1024)S(1)} fusion(s32[65536]{0:T(1024)} %bitcast.63, f32[65536]{0:T(1024)S(1)} %bitcast.61, f32[]{:T(128)} %constant.4.clone.1), kind=kCustom, calls=%fused_computation.64 | custom fusion | flops 65536 | bytes 33284 | tf_op jit(solution)/shard_map/scatter-add | solution.py:62
  1149.5 14.7 psum.7
  1164.3 8.1 copy.50
  1172.4 390.2 %scatter_custom_fusion.1 = f32[3,131072]{0,1:T(8,128)} fusion(s32[32768]{0:T(1024)} %get-tuple-element.9, f32[]{:T(128)} %constant.4.clone.1, f32[32768,3]{1,0:T(8,128)} %bitcast.47, s32[32768]{0:T(1024)S(1)} %broadcast_clamp_fusion.1), kind=kCustom, calls=%fused_computation.4 | custom fusion | flops 98304 | bytes 1573376 | tf_op jit(solution)/shard_map/vmap()/scatter-add | solution.py:46
  1562.6 366.4 %reduce-scatter.2.cloned.1.call-done = f32[3,4096]{0,1:T(8,128)} async-done(((f32[3,131072]{0,1:T(8,128)}), f32[3,4096]{0,1:T(8,128)}) %reduce-scatter.2.cloned.1.call-update) | async-done | bytes 49168 | tf_op jit(solution)/shard_map/reduce_scatter | solution.py:68
  1929.1 2.8 copy.14
  (68 shorter events, 6.3 us)
Async XLA Ops:
  7.2 15.5 copy-start.3
  8.2 14.4 collective-permute-start
  12.1 10.5 collective-permute-start.1
  16.8 18.5 collective-permute-start.4
  21.3 13.9 collective-permute-start.5
  22.8 22.1 %copy-start = (f32[6,32,1024]{2,1,0:T(8,128)S(1)}, f32[6,32,1024]{2,1,0:T(8,128)}, u32[]{:S(2)}) copy-start(f32[6,32,1024]{2,1,0:T(8,128)} %param.8) | copy-start | bytes 2359300
  22.9 6.1 collective-permute-start.3
  26.9 7.2 collective-permute-start.2
  35.5 2.5 collective-permute-start.7
  35.6 7.8 collective-permute-start.6
  48.8 5.8 collective-permute-start.8
  53.1 5.7 collective-permute-start.9
  59.0 2.5 collective-permute-start.11
  59.1 7.8 collective-permute-start.10
  72.3 5.2 collective-permute-start.12
  75.9 5.7 collective-permute-start.13
  81.9 2.5 collective-permute-start.15
  82.0 7.8 collective-permute-start.14
  91.3 8.8 copy-start.5
  92.0 14.5 copy-start.8
  95.2 5.1 collective-permute-start.16
  98.7 5.7 collective-permute-start.17
  104.7 12.9 collective-permute-start.19
  105.3 13.0 collective-permute-start.18
  117.6 0.6 copy-start.9
  120.0 3.9 copy-start.6
  120.7 3.2 copy-start.2
  123.9 639.7 %copy-start.1 = (f32[32,1024,6]{1,0,2:T(8,128)}, f32[32,1024,6]{1,0,2:T(8,128)S(1)}, u32[]{:S(2)}) copy-start(f32[32,1024,6]{1,0,2:T(8,128)S(1)} %multiply_reduce_fusion) | copy-start | bytes 2359300
  124.0 1040.2 %copy-start.4 = (f32[3,4,8192]{2,1,0:T(4,128)S(1)}, f32[3,4,8192]{2,1,0:T(4,128)}, u32[]{:S(2)}) copy-start(f32[3,4,8192]{2,1,0:T(4,128)} %param.14) | copy-start | bytes 1179652
  763.5 15.2 all-to-all-start
  769.8 1159.2 %reduce-scatter.2.cloned.1.call-start = ((), (), s32[]{:S(2)}) async-start(), calls=%async_computation.2 | async-start | bytes 69206016 | tf_op jit(solution)/shard_map/reduce_scatter | solution.py:68
  1164.2 8.2 copy-start.7
Sparse Core Ops, SparseCore 0:
  1562.8 366.2 reduce-scatter.1
where the time goes:
time: 1950 us; the launch traced here: 1940 us
  other arithmetic  792 us (41%)
  local copies, waits for them, and re-layouts  662 us (34%)
  waiting for transfers between devices  416 us (21%)
  starting transfers between devices  39.5 us (2%)
    gather x1, local copies, waits for them, and re-layouts, shards(): slot_vals = padded[send_list].reshape(owners, send_list.shape[0] // owners)  640 us
    scatter-add x3, other arithmetic, node_sums(): jax.ops.segment_sum(part.reshape(-1), flat_index, count)  401 us
    scatter-add x1, other arithmetic, shards(): jax.ops.segment_sum(received.reshape(-1), slot_face.reshape(-1), FACE_DEV...  371 us
    reduce_scatter x1, waiting for transfers between devices, shards(): node_sens = lax.psum_scatter(dense, 'dom', scatter_dimension=1, tiled=True)  366 us
  transfers between devices with their start and end apart: 22, of which 15 were waited for; matrix products, arithmetic and copies ran while one was open for 1% of the time, Pallas kernels for 0%

commit v1 on v0

v1 whole, which is shorter than its diff:
```python
import jax
import jax.numpy as jnp
from jax import lax
from jax.experimental import pallas as pl
from jax.experimental.pallas import tpu as pltpu
from jax.sharding import PartitionSpec as P

NVAR = 6
SWEEPS = 4
CX = 32
CY = 1024
CELLS = 32768
CAP = 2048
FACE_DEV = 8192
NODE_DEV = 4096
N_SPAN = 4
N_DOM = 32
LANES = 128
TILES = CY // LANES
SLOT_ROWS = CAP // LANES
CHUNK_ROWS = 4
CHUNK = CHUNK_ROWS * LANES
FACE_HI = FACE_DEV // LANES
NODE_HI = NODE_DEV // LANES

VMEM = pl.BlockSpec(memory_space=pltpu.VMEM)
SMEM = pl.BlockSpec(memory_space=pltpu.SMEM)
PARAMS = pltpu.CompilerParams(vmem_limit_bytes=40 << 20)
BF = jnp.bfloat16
F32 = jnp.float32


def f32(*shape):
    return jax.ShapeDtypeStruct(shape, F32)


def lane_tile(k):
    return slice(k * LANES, (k + 1) * LANES)


def product(inverse, terms, k):
    out = []
    for a in range(NVAR):
        total = inverse[0, a, :, lane_tile(k)] * terms[0]
        for b in range(1, NVAR):
            total = total + inverse[b, a, :, lane_tile(k)] * terms[b]
        out.append(total)
    return out


def store_edges(values, coupling, k, low, high, left, right):
    for a in range(NVAR):
        low[a : a + 1, lane_tile(k)] = coupling[1, 0:1, lane_tile(k)] * values[a][0:1]
        high[a : a + 1, lane_tile(k)] = coupling[0, CX - 1 : CX, lane_tile(k)] * values[a][CX - 1 :]
    lane = lax.broadcasted_iota(jnp.int32, (CX, LANES), 1)
    if k == 0:
        total = jnp.zeros((CX, LANES), F32)
        for a in range(NVAR):
            edge = coupling[3, :, lane_tile(k)] * values[a]
            total = jnp.where(lane == a, pltpu.roll(edge, a, 1) if a else edge, total)
        left[...] = total
    if k == TILES - 1:
        total = jnp.zeros((CX, LANES), F32)
        for a in range(NVAR):
            edge = coupling[2, :, lane_tile(k)] * values[a]
            total = jnp.where(lane == a, pltpu.roll(edge, a + 1, 1), total)
        right[...] = total


def first_kernel(rhs, inverse, coupling, out, low, high, left, right):
    for edge in (low, high):
        edge[...] = jnp.zeros_like(edge)
    for k in range(TILES):
        values = product(inverse, [rhs[b, :, lane_tile(k)] for b in range(NVAR)], k)
        for a in range(NVAR):
            out[a, :, lane_tile(k)] = values[a]
        store_edges(values, coupling, k, low, high, left, right)


def neighbour_terms(rhs, coupling, field, above, below, after, before):
    at = lax.axis_index("span")
    row = lax.broadcasted_iota(jnp.int32, (CX, LANES), 0)
    lane = lax.broadcasted_iota(jnp.int32, (CX, LANES), 1)
    after_rolled = {}
    before_rolled = {}

    def roll_back(k, b):
        if (k, b) not in after_rolled:
            if k == TILES:
                after_rolled[k, b] = pltpu.roll(after[...], LANES - 1 - b, 1)
            else:
                part = coupling[3, :, lane_tile(k)] * field[b, :, lane_tile(k)]
                after_rolled[k, b] = pltpu.roll(part, LANES - 1, 1)
        return after_rolled[k, b]

    def roll_on(k, b):
        if (k, b) not in before_rolled:
            if k < 0:
                before_rolled[k, b] = pltpu.roll(before[...], LANES - b, 1) if b else before[...]
            else:
                part = coupling[2, :, lane_tile(k)] * field[b, :, lane_tile(k)]
                before_rolled[k, b] = pltpu.roll(part, 1, 1)
        return before_rolled[k, b]

    def tile(k):
        terms = []
        for b in range(NVAR):
            value = field[b, :, lane_tile(k)]
            up = pltpu.roll(coupling[1, :, lane_tile(k)] * value, CX - 1, 0)
            edge = jnp.where(at == N_SPAN - 1, 0.0, above[b : b + 1, lane_tile(k)])
            total = jnp.where(row == CX - 1, edge, up)
            down = pltpu.roll(coupling[0, :, lane_tile(k)] * value, 1, 0)
            edge = jnp.where(at == 0, 0.0, below[b : b + 1, lane_tile(k)])
            total = total + jnp.where(row == 0, edge, down)
            total = total + jnp.where(lane == LANES - 1, roll_back(k + 1, b), roll_back(k, b))
            total = total + jnp.where(lane == 0, roll_on(k - 1, b), roll_on(k, b))
            terms.append(rhs[b, :, lane_tile(k)] - total)
        return terms

    return tile


def sweep_kernel(
    rhs, inverse, coupling, field, above, below, after, before, out, low, high, left, right
):
    for edge in (low, high):
        edge[...] = jnp.zeros_like(edge)
    terms = neighbour_terms(rhs, coupling, field, above, below, after, before)
    for k in range(TILES):
        values = product(inverse, terms(k), k)
        for a in range(NVAR):
            out[a, :, lane_tile(k)] = values[a]
        store_edges(values, coupling, k, low, high, left, right)


def last_kernel(rhs, inverse, coupling, field, above, below, after, before, grad, out, sens):
    terms = neighbour_terms(rhs, coupling, field, above, below, after, before)
    for k in range(TILES):
        values = product(inverse, terms(k), k)
        for a in range(NVAR):
            out[a, :, lane_tile(k)] = values[a]
        sens[:, lane_tile(k)] = grad[0, :, lane_tile(k)] * values[NVAR - 1]


EDGES = (f32(8, CY), f32(8, CY), f32(CX, LANES), f32(CX, LANES))


def shifted(axis, size, step):
    return [(i, (i + step) % size) for i in range(size)]


def exchange(low, high, left, right):
    above = lax.ppermute(low, "span", shifted("span", N_SPAN, -1))
    below = lax.ppermute(high, "span", shifted("span", N_SPAN, 1))
    after = lax.ppermute(left, "dom", shifted("dom", N_DOM, -1))
    before = lax.ppermute(right, "dom", shifted("dom", N_DOM, 1))
    return above, below, after, before


def relax(rhs, inverse, coupling, grad):
    whole = f32(NVAR, CX, CY)
    field, *edges = pl.pallas_call(
        first_kernel,
        out_shape=(whole, *EDGES),
        in_specs=[VMEM] * 3,
        out_specs=[VMEM] * 5,
        compiler_params=PARAMS,
        name="first_product",
    )(rhs, inverse, coupling)
    for sweep in range(SWEEPS - 1):
        field, *edges = pl.pallas_call(
            sweep_kernel,
            out_shape=(whole, *EDGES),
            in_specs=[VMEM] * 8,
            out_specs=[VMEM] * 5,
            compiler_params=PARAMS,
            name="sweep",
        )(rhs, inverse, coupling, field, *exchange(*edges))
    return pl.pallas_call(
        last_kernel,
        out_shape=(whole, f32(CX, CY)),
        in_specs=[VMEM] * 9,
        out_specs=[VMEM] * 2,
        compiler_params=PARAMS,
        name="last_sweep",
    )(rhs, inverse, coupling, field, *exchange(*edges), grad)


def two_parts(value):
    high = value.astype(BF).astype(F32)
    return high, value - high


def rows_of(ref, first, count):
    return jnp.concatenate([ref[pl.ds(first + i, 1), :] for i in range(count)], axis=1)


def sixteen(row):
    return jnp.broadcast_to(row, (16, row.shape[1])).astype(BF)


def matches(index, count):
    index = sixteen(index.astype(F32))
    first = lax.broadcasted_iota(jnp.int32, index.shape, 0)
    return [(first + 16 * k).astype(F32).astype(BF) == index for k in range(count // 16)]


def one_hot(index, count):
    return jnp.concatenate(
        [jnp.where(m, jnp.array(1, BF), jnp.array(0, BF)) for m in matches(index, count)], axis=0
    )


def weighted(index, count, values):
    masks = matches(index, count)
    parts = []
    for value in values:
        for part in two_parts(value):
            part = sixteen(part)
            parts += [jnp.where(m, part, jnp.array(0, BF)) for m in masks]
    return jnp.concatenate(parts, axis=0)


def outer_sum(left, right):
    return lax.dot_general(left, right, (((1,), (1,)), ((), ())), preferred_element_type=F32)


def gather_kernel(live, sens, slots, out, table):
    cells = jnp.concatenate([sens[:, lane_tile(k)] for k in range(TILES)], axis=0).T
    for part, half in enumerate(two_parts(cells)):
        table[part * LANES : (part + 1) * LANES, :] = half.astype(BF)
    place = lax.broadcasted_iota(jnp.int32, (LANES, CHUNK), 0)
    out[...] = jnp.zeros_like(out)

    @pl.loop(0, N_DOM)
    def owner(j):
        @pl.loop(0, live[j])
        def chunk(k):
            first = j * SLOT_ROWS + k * CHUNK_ROWS
            slot = rows_of(slots, first, CHUNK_ROWS)
            high = jnp.where(slot < CELLS, ((slot >> 7) & (TILES - 1)) * CX + (slot >> 10), 512)
            picked = jnp.dot(table[...], one_hot(high, 256), preferred_element_type=F32)
            picked = picked[:LANES] + picked[LANES:]
            value = jnp.sum(
                jnp.where(place == (slot & (LANES - 1)), picked, 0.0), axis=0, keepdims=True
            )
            for i in range(CHUNK_ROWS):
                out[pl.ds(first + i, 1), :] = value[:, lane_tile(i)]


def gather(sens, slots):
    live = jnp.sum(
        (slots.reshape(N_DOM, CAP // CHUNK, CHUNK)[:, :, 0] < CELLS).astype(jnp.int32), axis=1
    )
    return pl.pallas_call(
        gather_kernel,
        out_shape=f32(N_DOM * SLOT_ROWS, LANES),
        in_specs=[SMEM, VMEM, VMEM],
        out_specs=VMEM,
        scratch_shapes=[pltpu.VMEM((2 * LANES, 2 * LANES), BF)],
        compiler_params=PARAMS,
        name="gather_slots",
    )(live, sens, slots)


def face_kernel(values, faces, out, total):
    total[...] = jnp.zeros_like(total)

    @pl.loop(0, N_DOM)
    def sender(j):
        part = None
        for k in range(CAP // CHUNK):
            first = j * SLOT_ROWS + k * CHUNK_ROWS
            face = rows_of(faces, first, CHUNK_ROWS)
            value = rows_of(values, first, CHUNK_ROWS)
            step = outer_sum(
                weighted(face >> 7, FACE_HI, [value]), one_hot(face & (LANES - 1), LANES)
            )
            part = step if part is None else part + step
        total[...] += part

    out[...] = total[:FACE_HI] + total[FACE_HI:]


def face_sums(values, faces):
    return pl.pallas_call(
        face_kernel,
        out_shape=f32(FACE_HI, LANES),
        in_specs=[VMEM] * 2,
        out_specs=VMEM,
        scratch_shapes=[pltpu.VMEM((2 * FACE_HI, LANES), F32)],
        compiler_params=PARAMS,
        name="face_sums",
    )(values, faces)


def node_kernel(part0, part1, part2, part3, grad, nodes, faces, out, total):
    at = lax.axis_index("span")
    offset = jnp.where(at == 0, 0, jnp.where(at == 1, 1, jnp.where(at == 2, N_DOM - 1, N_DOM // 2)))
    base = lax.rem(lax.axis_index("dom") + offset, N_DOM) * NODE_DEV
    faces[...] = (part0[...] + part1[...]) + (part2[...] + part3[...])
    total[...] = jnp.zeros_like(total)

    @pl.loop(0, FACE_DEV // CHUNK)
    def chunk(g):
        sens = rows_of(faces, g * CHUNK_ROWS, CHUNK_ROWS)
        columns = pl.ds(pl.multiple_of(g * CHUNK, CHUNK), CHUNK)
        part = None
        for k in range(4):
            node = nodes[k : k + 1, columns] - base
            values = [grad[c, k : k + 1, columns] * sens for c in range(3)]
            step = outer_sum(
                weighted(node >> 7, NODE_HI, values), one_hot(node & (LANES - 1), LANES)
            )
            part = step if part is None else part + step
        total[...] += part

    for c in range(3):
        high = total[(2 * c) * NODE_HI : (2 * c + 1) * NODE_HI]
        out[c] = high + total[(2 * c + 1) * NODE_HI : (2 * c + 2) * NODE_HI]


def node_sums(parts, grad, nodes):
    return pl.pallas_call(
        node_kernel,
        out_shape=(f32(FACE_HI, LANES), f32(3, NODE_HI, LANES)),
        in_specs=[VMEM] * 6,
        out_specs=[VMEM] * 2,
        scratch_shapes=[pltpu.VMEM((6 * NODE_HI, LANES), F32)],
        compiler_params=PARAMS,
        name="node_sums",
    )(*parts, grad, nodes)


def to_node_owners(turn):
    offsets = (0, 1, N_DOM - 1, N_DOM // 2)
    return [
        (s * N_DOM + d, (s + turn) % N_SPAN * N_DOM + (d + offsets[s]) % N_DOM)
        for s in range(N_SPAN)
        for d in range(N_DOM)
    ]


def shards(
    adjoint_rhs, block_inverse, coupling, distance_grad, slot_cell, slot_face, area_grad, face_nodes
):
    adjoint, cell_sens = relax(adjoint_rhs, block_inverse, coupling, distance_grad)
    slot_vals = gather(cell_sens, slot_cell.reshape(N_DOM * SLOT_ROWS, LANES))
    received = lax.all_to_all(slot_vals, "dom", split_axis=0, concat_axis=0, tiled=True)
    face_part = face_sums(received, slot_face.reshape(N_DOM * SLOT_ROWS, LANES))
    parts = [face_part] + [
        lax.ppermute(face_part, "span", shifted("span", N_SPAN, turn)) for turn in range(1, N_SPAN)
    ]
    face_sens, part = node_sums(parts, area_grad, face_nodes)
    node_sens = sum(
        lax.ppermute(part, ("span", "dom"), to_node_owners(turn)) for turn in range(N_SPAN)
    )
    return (adjoint, face_sens.reshape(FACE_DEV), node_sens.reshape(3, NODE_DEV))


def solution(mesh):
    in_specs = (
        P(None, "span", "dom"),
        P(None, None, "span", "dom"),
        P(None, "span", "dom"),
        P(None, "span", "dom"),
        P("span", "dom", None),
        P("span", "dom", None),
        P(None, None, "dom"),
        P(None, "dom"),
    )
    out_specs = (P(None, "span", "dom"), P("dom"), P(None, "dom"))
    return jax.shard_map(shards, mesh=mesh, in_specs=in_specs, out_specs=out_specs, check_vma=False)
```

time: 1950 us -> 131 us (0.07)
  other arithmetic: 792 us -> 1.93 us
  local copies, waits for them, and re-layouts: 662 us -> 8.14 us
  waiting for transfers between devices: 416 us -> 33.5 us
  Pallas kernels: 0 us -> 43.4 us
    scatter-add x4 -> x0, other arithmetic: 772 us -> none  [the longest x3 401 us: node_sums(): jax.ops.segment_sum(part.reshape(-1), flat_index, count)]
    gather x1 -> x0, local copies, waits for them, and re-layouts: 640 us -> none  [shards(): slot_vals = padded[send_list].reshape(owners, send_list.shape[0] // owners)]
    reduce_scatter x1 -> x0, waiting for transfers between devices: 366 us -> none  [shards(): node_sens = lax.psum_scatter(dense, 'dom', scatter_dimension=1, tiled=True)]
    pallas_call x0 -> x8, Pallas kernels: none -> 43.4 us  [the longest x1 20.2 us: gather(): pl.pallas_call(gather_kernel, out_shape=f32(N_DOM * SLOT_ROWS, LANES), in...]
    ppermute x20 -> x23, waiting for transfers between devices: 40.5 us -> 33.5 us  [the longest x4 19.2 us: exchange(): before = lax.ppermute(right, 'dom', shifted('dom', N_DOM, 1))]
  transfers between devices with their start and end apart: 22 -> 23, of which waited for: 15 -> 13; matrix products, arithmetic and copies ran while one was open for 1% -> 2% of each run, Pallas kernels for 0% -> 0%
where the time goes in v1:
time: 131 us
  Pallas kernels  43.4 us (33%)
  waiting for transfers between devices  33.5 us (26%)
  starting transfers between devices  31 us (24%)
  blocking collectives  11.9 us (9%)
  local copies, waits for them, and re-layouts  8.14 us (6%)
  other arithmetic  1.93 us (1%)
    pallas_call x1, Pallas kernels, gather(): pl.pallas_call(gather_kernel, out_shape=f32(N_DOM * SLOT_ROWS, LANES), in...  20.2 us
    ppermute x4, waiting for transfers between devices, exchange(): before = lax.ppermute(right, 'dom', shifted('dom', N_DOM, 1))  19.2 us
    ppermute x4, starting transfers between devices, exchange(): above = lax.ppermute(low, 'span', shifted('span', N_SPAN, -1))  13.8 us
    all_to_all x1, blocking collectives, shards(): lax.all_to_all(slot_vals, 'dom', split_axis=0, concat_axis=0, tiled=True)  11.9 us
    pallas_call x1, Pallas kernels, face_sums(): pl.pallas_call(face_kernel, out_shape=f32(FACE_HI, LANES), in_specs=[VMEM...  10.5 us
    unnamed x24, local copies, waits for them, and re-layouts  8.05 us
    ppermute x4, waiting for transfers between devices, shards(): lax.ppermute(part, ('span', 'dom'), to_node_owners(turn))  7.5 us
    ppermute x4, starting transfers between devices, shards(): lax.ppermute(part, ('span', 'dom'), to_node_owners(turn))  6.83 us
  transfers between devices with their start and end apart: 23, of which 13 were waited for; matrix products, arithmetic and copies ran while one was open for 2% of the time, Pallas kernels for 0%

profile of v1, /device:TPU:0, one launch (start us, length us, event | category | flops | bytes accessed | tf_op | source)
XLA Modules:
  0.0 130.7 jit_solution(10759384865314917693)
XLA Ops:
  0.6 0.0 copy-start
  0.6 2.3 %copy-done = f32[6,6,32,1024]{3,2,1,0:T(8,128)S(1)} copy-done((f32[6,6,32,1024]{3,2,1,0:T(8,128)S(1)}, f32[6,6,32,1024]{3,2,1,0:T(8,128)}, u32[]{:S(2)}) %copy-start) | copy-done | bytes 4718616
  3.0 1.1 copy-done.2
  4.1 1.0 copy-done.4
  5.1 0.6 first_product.1
  5.7 4.2 %collective-permute-start = (f32[8,1024]{1,0:T(8,128)S(1)}, f32[8,1024]{1,0:T(8,128)S(1)}, u32[]{:S(2)}, u32[]{:S(2)}) collective-permute-start(f32[8,1024]{1,0:T(8,128)S(1)} %get-tuple-element.28), channel_id=1, source_target_pairs={{0,96},{32,0},{64,32},{96,64},{1,97},{33,1},{65,33},{97,65},{2,98}... | collective-permute-start | bytes 98312 | tf_op jit(solution)/shard_map/ppermute | solution.py:153
  9.9 4.4 %collective-permute-start.2 = (f32[32,128]{1,0:T(8,128)S(1)}, f32[32,128]{1,0:T(8,128)S(1)}, u32[]{:S(2)}, u32[]{:S(2)}) collective-permute-start(f32[32,128]{1,0:T(8,128)S(1)} %get-tuple-element.30), channel_id=1, source_target_pairs={{0,31},{1,0},{2,1},{3,2},{4,3},{5,4},{6,5},{7,6},{8,7},{9,8},{10,9... | collective-permute-start | bytes 49160 | tf_op jit(solution)/shard_map/ppermute | solution.py:155
  14.3 1.4 %collective-permute-done.2.after = f32[32,128]{1,0:T(8,128)S(1)} collective-permute-done((f32[32,128]{1,0:T(8,128)S(1)}, f32[32,128]{1,0:T(8,128)S(1)}, u32[]{:S(2)}, u32[]{:S(2)}) %collective-permute-start.2) | collective-permute-done | bytes 16416 | tf_op jit(solution)/shard_map/ppermute | solution.py:155
  15.7 5.0 %collective-permute-done.3.before = f32[32,128]{1,0:T(8,128)S(1)} collective-permute-done((f32[32,128]{1,0:T(8,128)S(1)}, f32[32,128]{1,0:T(8,128)S(1)}, u32[]{:S(2)}, u32[]{:S(2)}) %collective-permute-start.3) | collective-permute-done | bytes 16416 | tf_op jit(solution)/shard_map/ppermute | solution.py:156
  20.8 1.2 sweep.3
  22.0 3.0 %collective-permute-start.4 = (f32[8,1024]{1,0:T(8,128)S(1)}, f32[8,1024]{1,0:T(8,128)S(1)}, u32[]{:S(2)}, u32[]{:S(2)}) collective-permute-start(f32[8,1024]{1,0:T(8,128)S(1)} %get-tuple-element.33), channel_id=1, source_target_pairs={{0,96},{32,0},{64,32},{96,64},{1,97},{33,1},{65,33},{97,65},{2,98}... | collective-permute-start | bytes 98312 | tf_op jit(solution)/shard_map/ppermute | solution.py:153
  25.1 0.5 collective-permute-start.7
  25.6 0.9 collective-permute-done.6.after
  26.5 5.0 %collective-permute-done.7.before = f32[32,128]{1,0:T(8,128)S(1)} collective-permute-done((f32[32,128]{1,0:T(8,128)S(1)}, f32[32,128]{1,0:T(8,128)S(1)}, u32[]{:S(2)}, u32[]{:S(2)}) %collective-permute-start.7) | collective-permute-done | bytes 16416 | tf_op jit(solution)/shard_map/ppermute | solution.py:156
  31.6 1.2 sweep.4
  32.8 3.3 %collective-permute-start.8 = (f32[8,1024]{1,0:T(8,128)S(1)}, f32[8,1024]{1,0:T(8,128)S(1)}, u32[]{:S(2)}, u32[]{:S(2)}) collective-permute-start(f32[8,1024]{1,0:T(8,128)S(1)} %get-tuple-element.38), channel_id=1, source_target_pairs={{0,96},{32,0},{64,32},{96,64},{1,97},{33,1},{65,33},{97,65},{2,98}... | collective-permute-start | bytes 98312 | tf_op jit(solution)/shard_map/ppermute | solution.py:153
  36.1 0.5 collective-permute-start.11
  36.6 0.5 broadcast.5
  37.1 1.3 reduce.4
  38.4 0.1 reshape_reshape.3
  38.5 4.1 %collective-permute-done.11.before = f32[32,128]{1,0:T(8,128)S(1)} collective-permute-done((f32[32,128]{1,0:T(8,128)S(1)}, f32[32,128]{1,0:T(8,128)S(1)}, u32[]{:S(2)}, u32[]{:S(2)}) %collective-permute-start.11) | collective-permute-done | bytes 16416 | tf_op jit(solution)/shard_map/ppermute | solution.py:156
  42.6 0.0 copy-start.1
  42.6 2.3 %copy-done.1 = f32[6,6,32,1024]{3,2,1,0:T(8,128)S(1)} copy-done((f32[6,6,32,1024]{3,2,1,0:T(8,128)S(1)}, f32[6,6,32,1024]{3,2,1,0:T(8,128)}, u32[]{:S(2)}) %copy-start.1) | copy-done | bytes 4718616
  44.9 1.2 sweep.5
  46.2 3.3 %collective-permute-start.12 = (f32[8,1024]{1,0:T(8,128)S(1)}, f32[8,1024]{1,0:T(8,128)S(1)}, u32[]{:S(2)}, u32[]{:S(2)}) collective-permute-start(f32[8,1024]{1,0:T(8,128)S(1)} %get-tuple-element.43), channel_id=1, source_target_pairs={{0,96},{32,0},{64,32},{96,64},{1,97},{33,1},{65,33},{97,65},{2,98}... | collective-permute-start | bytes 98312 | tf_op jit(solution)/shard_map/ppermute | solution.py:153
  49.5 0.2 collective-permute-start.14
  49.7 0.3 collective-permute-start.15
  50.0 0.7 convert_reduce_fusion.live
  50.6 0.5 collective-permute-done.14.after
  51.1 5.0 %collective-permute-done.15.before = f32[32,128]{1,0:T(8,128)S(1)} collective-permute-done((f32[32,128]{1,0:T(8,128)S(1)}, f32[32,128]{1,0:T(8,128)S(1)}, u32[]{:S(2)}, u32[]{:S(2)}) %collective-permute-start.15) | collective-permute-done | bytes 16416 | tf_op jit(solution)/shard_map/ppermute | solution.py:156
  56.2 2.0 %last_sweep.1 = (f32[6,32,1024]{2,1,0:T(8,128)}, f32[32,1024]{1,0:T(8,128)S(1)}) custom-call(f32[6,32,1024]{2,1,0:T(8,128)S(1)} %copy-done.3, f32[6,6,32,1024]{3,2,1,0:T(8,128)S(1)} %copy-done.1, f32[4,32,1024]{2,1,0:T(8,128)S(1)} %copy-done.5, f32[6,32,1024]{2,1,0:T(8,128)S(1)} %get-tuple-element.42.field, f32[8,1024]{1,0:T(8,128)S(1)} %collective-permute-done.12.above, ...), custom_call_target="tpu_custom_call" | custom-call | tf_op jit(solution)/shard_map/last_sweep/pallas_call | solution.py:179
  58.2 20.2 %gather_slots.1 = f32[512,128]{1,0:T(8,128)S(1)} custom-call(s32[32]{0:T(128)S(1)} %convert_reduce_fusion.live, f32[32,1024]{1,0:T(8,128)S(1)} %get-tuple-element.48.sens, s32[512,128]{1,0:T(8,128)S(1)} %bitcast.10), custom_call_target="tpu_custom_call" | custom-call | tf_op jit(solution)/shard_map/gather_slots/pallas_call | solution.py:255
  78.4 11.9 %all_to_all.11 = f32[32,16,128]{2,1,0:T(8,128)S(1)} all-to-all(f32[32,16,128]{2,1,0:T(8,128)S(1)} %bitcast.11), channel_id=1, replica_groups=mesh['span'=4,'dom'=32] {'dom'}, dimensions={0} | all-to-all | bytes 524288 | tf_op jit(solution)/shard_map/all_to_all | solution.py:349
  90.3 10.5 %face_sums.1.part0 = f32[64,128]{1,0:T(8,128)S(1)} custom-call(f32[512,128]{1,0:T(8,128)S(1)} %bitcast.12, s32[512,128]{1,0:T(8,128)S(1)} %bitcast.13), custom_call_target="tpu_custom_call" | custom-call | tf_op jit(solution)/shard_map/face_sums/pallas_call | solution.py:286
  100.8 0.1 collective-permute-start.16
  100.9 4.4 %collective-permute-start.17 = (f32[64,128]{1,0:T(8,128)S(1)}, f32[64,128]{1,0:T(8,128)S(1)}, u32[]{:S(2)}, u32[]{:S(2)}) collective-permute-start(f32[64,128]{1,0:T(8,128)S(1)} %face_sums.1.part0), channel_id=1, source_target_pairs={{0,64},{32,96},{64,0},{96,32},{1,65},{33,97},{65,1},{97,33},{2,66}... | collective-permute-start | bytes 98312 | tf_op jit(solution)/shard_map/ppermute | solution.py:352
  105.2 0.7 collective-permute-done.16.part1
  106.0 1.5 %collective-permute-done.17.part2 = f32[64,128]{1,0:T(8,128)S(1)} collective-permute-done((f32[64,128]{1,0:T(8,128)S(1)}, f32[64,128]{1,0:T(8,128)S(1)}, u32[]{:S(2)}, u32[]{:S(2)}) %collective-permute-start.17) | collective-permute-done | bytes 32800 | tf_op jit(solution)/shard_map/ppermute | solution.py:352
  107.5 1.7 %collective-permute-done.18.part3 = f32[64,128]{1,0:T(8,128)S(1)} collective-permute-done((f32[64,128]{1,0:T(8,128)S(1)}, f32[64,128]{1,0:T(8,128)S(1)}, u32[]{:S(2)}, u32[]{:S(2)}) %collective-permute-start.18) | collective-permute-done | bytes 32800 | tf_op jit(solution)/shard_map/ppermute | solution.py:352
  109.2 6.5 %node_sums.1 = (f32[64,128]{1,0:T(8,128)}, f32[3,32,128]{2,1,0:T(8,128)S(1)}) custom-call(f32[64,128]{1,0:T(8,128)S(1)} %face_sums.1.part0, f32[64,128]{1,0:T(8,128)S(1)} %collective-permute-done.16.part1, f32[64,128]{1,0:T(8,128)S(1)} %collective-permute-done.17.part2, f32[64,128]{1,0:T(8,128)S(1)} %collective-permute-done.18.part3, ...), custom_call_target="tpu_custom_call" | custom-call | tf_op jit(solution)/shard_map/node_sums/pallas_call | solution.py:324
  115.7 0.7 collective-permute-start.19
  116.3 1.1 collective-permute-start.20
  117.4 4.9 %collective-permute-start.21 = (f32[3,32,128]{2,1,0:T(8,128)S(1)}, f32[3,32,128]{2,1,0:T(8,128)S(1)}, u32[]{:S(2)}, u32[]{:S(2)}) collective-permute-start(f32[3,32,128]{2,1,0:T(8,128)S(1)} %get-tuple-element.50), channel_id=1, source_target_pairs={{0,64},{1,65},{2,66},{3,67},{4,68},{5,69},{6,70},{7,71},{8,72},{9,... | collective-permute-start | bytes 147464 | tf_op jit(solution)/shard_map/ppermute | solution.py:356
  122.3 0.2 collective-permute-start.22
  122.5 2.3 %collective-permute-done.20 = f32[3,32,128]{2,1,0:T(8,128)S(1)} collective-permute-done((f32[3,32,128]{2,1,0:T(8,128)S(1)}, f32[3,32,128]{2,1,0:T(8,128)S(1)}, u32[]{:S(2)}, u32[]{:S(2)}) %collective-permute-start.20) | collective-permute-done | bytes 49184 | tf_op jit(solution)/shard_map/ppermute | solution.py:356
  124.8 0.2 collective-permute-done.21
  125.0 5.0 %collective-permute-done.22 = f32[3,32,128]{2,1,0:T(8,128)S(1)} collective-permute-done((f32[3,32,128]{2,1,0:T(8,128)S(1)}, f32[3,32,128]{2,1,0:T(8,128)S(1)}, u32[]{:S(2)}, u32[]{:S(2)}) %collective-permute-start.22) | collective-permute-done | bytes 49184 | tf_op jit(solution)/shard_map/ppermute | solution.py:356
  130.0 0.7 copy.13
  (35 shorter events, 0.1 us)
Async XLA Ops:
  0.6 2.3 %copy-start = (f32[6,6,32,1024]{3,2,1,0:T(8,128)S(1)}, f32[6,6,32,1024]{3,2,1,0:T(8,128)}, u32[]{:S(2)}) copy-start(f32[6,6,32,1024]{3,2,1,0:T(8,128)} %inverse.9) | copy-start | bytes 14155780
  3.0 1.1 copy-start.2
  4.1 1.0 copy-start.4
  5.7 15.0 %collective-permute-start = (f32[8,1024]{1,0:T(8,128)S(1)}, f32[8,1024]{1,0:T(8,128)S(1)}, u32[]{:S(2)}, u32[]{:S(2)}) collective-permute-start(f32[8,1024]{1,0:T(8,128)S(1)} %get-tuple-element.28), channel_id=1, source_target_pairs={{0,96},{32,0},{64,32},{96,64},{1,97},{33,1},{65,33},{97,65},{2,98}... | collective-permute-start | bytes 98312 | tf_op jit(solution)/shard_map/ppermute | solution.py:153
  9.9 10.9 %collective-permute-start.1 = (f32[8,1024]{1,0:T(8,128)S(1)}, f32[8,1024]{1,0:T(8,128)S(1)}, u32[]{:S(2)}, u32[]{:S(2)}) collective-permute-start(f32[8,1024]{1,0:T(8,128)S(1)} %get-tuple-element.29), channel_id=1, source_target_pairs={{0,32},{32,64},{64,96},{96,0},{1,33},{33,65},{65,97},{97,1},{2,34}... | collective-permute-start | bytes 98312 | tf_op jit(solution)/shard_map/ppermute | solution.py:154
  9.9 5.8 %collective-permute-start.2 = (f32[32,128]{1,0:T(8,128)S(1)}, f32[32,128]{1,0:T(8,128)S(1)}, u32[]{:S(2)}, u32[]{:S(2)}) collective-permute-start(f32[32,128]{1,0:T(8,128)S(1)} %get-tuple-element.30), channel_id=1, source_target_pairs={{0,31},{1,0},{2,1},{3,2},{4,3},{5,4},{6,5},{7,6},{8,7},{9,8},{10,9... | collective-permute-start | bytes 49160 | tf_op jit(solution)/shard_map/ppermute | solution.py:155
  14.3 6.5 %collective-permute-start.3 = (f32[32,128]{1,0:T(8,128)S(1)}, f32[32,128]{1,0:T(8,128)S(1)}, u32[]{:S(2)}, u32[]{:S(2)}) collective-permute-start(f32[32,128]{1,0:T(8,128)S(1)} %get-tuple-element.31), channel_id=1, source_target_pairs={{0,1},{1,2},{2,3},{3,4},{4,5},{5,6},{6,7},{7,8},{8,9},{9,10},{10,1... | collective-permute-start | bytes 49160 | tf_op jit(solution)/shard_map/ppermute | solution.py:156
  22.0 15.1 %copy-start.6 = (s32[1,1,65536]{2,1,0:T(1,128)S(1)}, s32[1,1,65536]{2,1,0:T(1,128)}, u32[]{:S(2)}) copy-start(s32[1,1,65536]{2,1,0:T(1,128)} %param.12) | copy-start | bytes 786436
  22.0 20.5 %copy-start.3 = (f32[6,32,1024]{2,1,0:T(8,128)S(1)}, f32[6,32,1024]{2,1,0:T(8,128)}, u32[]{:S(2)}) copy-start(f32[6,32,1024]{2,1,0:T(8,128)} %rhs.13) | copy-start | bytes 2359300
  22.0 20.5 %copy-start.5 = (f32[4,32,1024]{2,1,0:T(8,128)S(1)}, f32[4,32,1024]{2,1,0:T(8,128)}, u32[]{:S(2)}) copy-start(f32[4,32,1024]{2,1,0:T(8,128)} %coupling.9) | copy-start | bytes 1572868
  22.0 9.5 %collective-permute-start.4 = (f32[8,1024]{1,0:T(8,128)S(1)}, f32[8,1024]{1,0:T(8,128)S(1)}, u32[]{:S(2)}, u32[]{:S(2)}) collective-permute-start(f32[8,1024]{1,0:T(8,128)S(1)} %get-tuple-element.33), channel_id=1, source_target_pairs={{0,96},{32,0},{64,32},{96,64},{1,97},{33,1},{65,33},{97,65},{2,98}... | collective-permute-start | bytes 98312 | tf_op jit(solution)/shard_map/ppermute | solution.py:153
  25.1 6.5 %collective-permute-start.5 = (f32[8,1024]{1,0:T(8,128)S(1)}, f32[8,1024]{1,0:T(8,128)S(1)}, u32[]{:S(2)}, u32[]{:S(2)}) collective-permute-start(f32[8,1024]{1,0:T(8,128)S(1)} %get-tuple-element.34), channel_id=1, source_target_pairs={{0,32},{32,64},{64,96},{96,0},{1,33},{33,65},{65,97},{97,1},{2,34}... | collective-permute-start | bytes 98312 | tf_op jit(solution)/shard_map/ppermute | solution.py:154
  25.1 1.4 %collective-permute-start.6 = (f32[32,128]{1,0:T(8,128)S(1)}, f32[32,128]{1,0:T(8,128)S(1)}, u32[]{:S(2)}, u32[]{:S(2)}) collective-permute-start(f32[32,128]{1,0:T(8,128)S(1)} %get-tuple-element.35), channel_id=1, source_target_pairs={{0,31},{1,0},{2,1},{3,2},{4,3},{5,4},{6,5},{7,6},{8,7},{9,8},{10,9... | collective-permute-start | bytes 49160 | tf_op jit(solution)/shard_map/ppermute | solution.py:155
  25.1 6.5 %collective-permute-start.7 = (f32[32,128]{1,0:T(8,128)S(1)}, f32[32,128]{1,0:T(8,128)S(1)}, u32[]{:S(2)}, u32[]{:S(2)}) collective-permute-start(f32[32,128]{1,0:T(8,128)S(1)} %get-tuple-element.36), channel_id=1, source_target_pairs={{0,1},{1,2},{2,3},{3,4},{4,5},{5,6},{6,7},{7,8},{8,9},{9,10},{10,1... | collective-permute-start | bytes 49160 | tf_op jit(solution)/shard_map/ppermute | solution.py:156
  32.8 23.4 %copy-start.9 = (f32[1,32,1024]{2,1,0:T(8,128)S(1)}, f32[1,32,1024]{2,1,0:T(8,128)}, u32[]{:S(2)}) copy-start(f32[1,32,1024]{2,1,0:T(8,128)} %grad.2) | copy-start | bytes 393220
  32.8 9.8 %collective-permute-start.8 = (f32[8,1024]{1,0:T(8,128)S(1)}, f32[8,1024]{1,0:T(8,128)S(1)}, u32[]{:S(2)}, u32[]{:S(2)}) collective-permute-start(f32[8,1024]{1,0:T(8,128)S(1)} %get-tuple-element.38), channel_id=1, source_target_pairs={{0,96},{32,0},{64,32},{96,64},{1,97},{33,1},{65,33},{97,65},{2,98}... | collective-permute-start | bytes 98312 | tf_op jit(solution)/shard_map/ppermute | solution.py:153
  36.1 6.5 %collective-permute-start.9 = (f32[8,1024]{1,0:T(8,128)S(1)}, f32[8,1024]{1,0:T(8,128)S(1)}, u32[]{:S(2)}, u32[]{:S(2)}) collective-permute-start(f32[8,1024]{1,0:T(8,128)S(1)} %get-tuple-element.39), channel_id=1, source_target_pairs={{0,32},{32,64},{64,96},{96,0},{1,33},{33,65},{65,97},{97,1},{2,34}... | collective-permute-start | bytes 98312 | tf_op jit(solution)/shard_map/ppermute | solution.py:154
  36.1 2.4 %collective-permute-start.10 = (f32[32,128]{1,0:T(8,128)S(1)}, f32[32,128]{1,0:T(8,128)S(1)}, u32[]{:S(2)}, u32[]{:S(2)}) collective-permute-start(f32[32,128]{1,0:T(8,128)S(1)} %get-tuple-element.40), channel_id=1, source_target_pairs={{0,31},{1,0},{2,1},{3,2},{4,3},{5,4},{6,5},{7,6},{8,7},{9,8},{10,9... | collective-permute-start | bytes 49160 | tf_op jit(solution)/shard_map/ppermute | solution.py:155
  36.1 6.5 %collective-permute-start.11 = (f32[32,128]{1,0:T(8,128)S(1)}, f32[32,128]{1,0:T(8,128)S(1)}, u32[]{:S(2)}, u32[]{:S(2)}) collective-permute-start(f32[32,128]{1,0:T(8,128)S(1)} %get-tuple-element.41), channel_id=1, source_target_pairs={{0,1},{1,2},{2,3},{3,4},{4,5},{5,6},{6,7},{7,8},{8,9},{9,10},{10,1... | collective-permute-start | bytes 49160 | tf_op jit(solution)/shard_map/ppermute | solution.py:156
  42.6 2.3 %copy-start.1 = (f32[6,6,32,1024]{3,2,1,0:T(8,128)S(1)}, f32[6,6,32,1024]{3,2,1,0:T(8,128)}, u32[]{:S(2)}) copy-start(f32[6,6,32,1024]{3,2,1,0:T(8,128)} %inverse.9) | copy-start | bytes 14155780
  46.1 44.1 %copy-start.8 = (s32[1,1,65536]{2,1,0:T(1,128)S(1)}, s32[1,1,65536]{2,1,0:T(1,128)}, u32[]{:S(2)}) copy-start(s32[1,1,65536]{2,1,0:T(1,128)} %param.13) | copy-start | bytes 786436
  46.1 63.0 %copy-start.7 = (f32[3,4,8192]{2,1,0:T(4,128)S(1)}, f32[3,4,8192]{2,1,0:T(4,128)}, u32[]{:S(2)}) copy-start(f32[3,4,8192]{2,1,0:T(4,128)} %grad.3) | copy-start | bytes 1179652
  46.2 63.0 %copy-start.10 = (s32[4,8192]{1,0:T(4,128)S(1)}, s32[4,8192]{1,0:T(4,128)}, u32[]{:S(2)}) copy-start(s32[4,8192]{1,0:T(4,128)} %nodes.1) | copy-start | bytes 393220
  46.2 10.0 %collective-permute-start.12 = (f32[8,1024]{1,0:T(8,128)S(1)}, f32[8,1024]{1,0:T(8,128)S(1)}, u32[]{:S(2)}, u32[]{:S(2)}) collective-permute-start(f32[8,1024]{1,0:T(8,128)S(1)} %get-tuple-element.43), channel_id=1, source_target_pairs={{0,96},{32,0},{64,32},{96,64},{1,97},{33,1},{65,33},{97,65},{2,98}... | collective-permute-start | bytes 98312 | tf_op jit(solution)/shard_map/ppermute | solution.py:153
  49.5 6.7 %collective-permute-start.13 = (f32[8,1024]{1,0:T(8,128)S(1)}, f32[8,1024]{1,0:T(8,128)S(1)}, u32[]{:S(2)}, u32[]{:S(2)}) collective-permute-start(f32[8,1024]{1,0:T(8,128)S(1)} %get-tuple-element.44), channel_id=1, source_target_pairs={{0,32},{32,64},{64,96},{96,0},{1,33},{33,65},{65,97},{97,1},{2,34}... | collective-permute-start | bytes 98312 | tf_op jit(solution)/shard_map/ppermute | solution.py:154
  49.5 1.7 %collective-permute-start.14 = (f32[32,128]{1,0:T(8,128)S(1)}, f32[32,128]{1,0:T(8,128)S(1)}, u32[]{:S(2)}, u32[]{:S(2)}) collective-permute-start(f32[32,128]{1,0:T(8,128)S(1)} %get-tuple-element.45), channel_id=1, source_target_pairs={{0,31},{1,0},{2,1},{3,2},{4,3},{5,4},{6,5},{7,6},{8,7},{9,8},{10,9... | collective-permute-start | bytes 49160 | tf_op jit(solution)/shard_map/ppermute | solution.py:155
  49.7 6.5 %collective-permute-start.15 = (f32[32,128]{1,0:T(8,128)S(1)}, f32[32,128]{1,0:T(8,128)S(1)}, u32[]{:S(2)}, u32[]{:S(2)}) collective-permute-start(f32[32,128]{1,0:T(8,128)S(1)} %get-tuple-element.46), channel_id=1, source_target_pairs={{0,1},{1,2},{2,3},{3,4},{4,5},{5,6},{6,7},{7,8},{8,9},{9,10},{10,1... | collective-permute-start | bytes 49160 | tf_op jit(solution)/shard_map/ppermute | solution.py:156
  100.8 5.2 %collective-permute-start.16 = (f32[64,128]{1,0:T(8,128)S(1)}, f32[64,128]{1,0:T(8,128)S(1)}, u32[]{:S(2)}, u32[]{:S(2)}) collective-permute-start(f32[64,128]{1,0:T(8,128)S(1)} %face_sums.1.part0), channel_id=1, source_target_pairs={{0,32},{32,64},{64,96},{96,0},{1,33},{33,65},{65,97},{97,1},{2,34}... | collective-permute-start | bytes 98312 | tf_op jit(solution)/shard_map/ppermute | solution.py:352
  100.9 6.6 %collective-permute-start.17 = (f32[64,128]{1,0:T(8,128)S(1)}, f32[64,128]{1,0:T(8,128)S(1)}, u32[]{:S(2)}, u32[]{:S(2)}) collective-permute-start(f32[64,128]{1,0:T(8,128)S(1)} %face_sums.1.part0), channel_id=1, source_target_pairs={{0,64},{32,96},{64,0},{96,32},{1,65},{33,97},{65,1},{97,33},{2,66}... | collective-permute-start | bytes 98312 | tf_op jit(solution)/shard_map/ppermute | solution.py:352
  105.2 3.9 %collective-permute-start.18 = (f32[64,128]{1,0:T(8,128)S(1)}, f32[64,128]{1,0:T(8,128)S(1)}, u32[]{:S(2)}, u32[]{:S(2)}) collective-permute-start(f32[64,128]{1,0:T(8,128)S(1)} %face_sums.1.part0), channel_id=1, source_target_pairs={{0,96},{32,0},{64,32},{96,64},{1,97},{33,1},{65,33},{97,65},{2,98}... | collective-permute-start | bytes 98312 | tf_op jit(solution)/shard_map/ppermute | solution.py:352
  115.7 6.8 %collective-permute-start.19 = (f32[3,32,128]{2,1,0:T(8,128)S(1)}, f32[3,32,128]{2,1,0:T(8,128)S(1)}, u32[]{:S(2)}, u32[]{:S(2)}) collective-permute-start(f32[3,32,128]{2,1,0:T(8,128)S(1)} %get-tuple-element.50), channel_id=1, source_target_pairs={{0,0},{1,1},{2,2},{3,3},{4,4},{5,5},{6,6},{7,7},{8,8},{9,9},{10,10... | collective-permute-start | bytes 147464 | tf_op jit(solution)/shard_map/ppermute | solution.py:356
  116.3 8.4 %collective-permute-start.20 = (f32[3,32,128]{2,1,0:T(8,128)S(1)}, f32[3,32,128]{2,1,0:T(8,128)S(1)}, u32[]{:S(2)}, u32[]{:S(2)}) collective-permute-start(f32[3,32,128]{2,1,0:T(8,128)S(1)} %get-tuple-element.50), channel_id=1, source_target_pairs={{0,32},{1,33},{2,34},{3,35},{4,36},{5,37},{6,38},{7,39},{8,40},{9,... | collective-permute-start | bytes 147464 | tf_op jit(solution)/shard_map/ppermute | solution.py:356
  117.4 7.6 %collective-permute-start.21 = (f32[3,32,128]{2,1,0:T(8,128)S(1)}, f32[3,32,128]{2,1,0:T(8,128)S(1)}, u32[]{:S(2)}, u32[]{:S(2)}) collective-permute-start(f32[3,32,128]{2,1,0:T(8,128)S(1)} %get-tuple-element.50), channel_id=1, source_target_pairs={{0,64},{1,65},{2,66},{3,67},{4,68},{5,69},{6,70},{7,71},{8,72},{9,... | collective-permute-start | bytes 147464 | tf_op jit(solution)/shard_map/ppermute | solution.py:356
  122.3 7.7 %collective-permute-start.22 = (f32[3,32,128]{2,1,0:T(8,128)S(1)}, f32[3,32,128]{2,1,0:T(8,128)S(1)}, u32[]{:S(2)}, u32[]{:S(2)}) collective-permute-start(f32[3,32,128]{2,1,0:T(8,128)S(1)} %get-tuple-element.50), channel_id=1, source_target_pairs={{0,96},{1,97},{2,98},{3,99},{4,100},{5,101},{6,102},{7,103},{8,104... | collective-permute-start | bytes 147464 | tf_op jit(solution)/shard_map/ppermute | solution.py:356

commit v2 on v1

--- a/solution.py
+++ b/solution.py
@@ -17,9 +17,12 @@
 N_DOM = 32
 LANES = 128
 TILES = CY // LANES
-SLOT_ROWS = CAP // LANES
-CHUNK_ROWS = 4
-CHUNK = CHUNK_ROWS * LANES
+SLOT_ROWS = N_DOM * CAP // LANES
+LIVE_ROWS = CELLS // LANES + N_DOM
+LIVE_PAD = 384
+GATHER_ROWS, GATHER_STEPS = 8, 18
+FACE_ROWS, FACE_STEPS = 16, 16
+NODE_ROWS, NODE_STEPS = 8, 4
 FACE_HI = FACE_DEV // LANES
 NODE_HI = NODE_DEV // LANES
 
@@ -225,36 +228,63 @@
     return lax.dot_general(left, right, (((1,), (1,)), ((), ())), preferred_element_type=F32)
 
 
+def live_rows_kernel(slots, out, line, done):
+    live = jnp.broadcast_to(slots[...].T[0:1] < CELLS, (8, SLOT_ROWS))
+    ones = jnp.where(live, 1.0, 0.0).astype(BF)
+    square = (SLOT_ROWS, SLOT_ROWS)
+    before = lax.broadcasted_iota(jnp.int32, square, 0) < lax.broadcasted_iota(jnp.int32, square, 1)
+    place = jnp.dot(ones, jnp.where(before, 1.0, 0.0).astype(BF), preferred_element_type=F32)
+    place = jnp.where(live, place, -1.0)[0:1].astype(jnp.int32)
+    at_place = lax.broadcasted_iota(jnp.int32, (LIVE_PAD, SLOT_ROWS), 0) == place
+    row = lax.broadcasted_iota(jnp.int32, (8, SLOT_ROWS), 1)
+    half = lax.broadcasted_iota(jnp.int32, (8, SLOT_ROWS), 0)
+    row = jnp.where(half == 0, row >> 4, row & 15).astype(F32).astype(BF)
+    found = outer_sum(row, jnp.where(at_place, 1.0, 0.0).astype(BF))
+    line[...] = jnp.broadcast_to(found[0:1] * 16.0 + found[1:2], line.shape).astype(jnp.int32)
+    copy = pltpu.make_async_copy(line, out, done)
+    copy.start()
+    copy.wait()
+
+
+def live_rows(slots):
+    return pl.pallas_call(
+        live_rows_kernel,
+        out_shape=jax.ShapeDtypeStruct((8, LIVE_PAD), jnp.int32),
+        in_specs=[VMEM],
+        out_specs=SMEM,
+        scratch_shapes=[pltpu.VMEM((8, LIVE_PAD), jnp.int32), pltpu.SemaphoreType.DMA],
+        compiler_params=PARAMS,
+        name="live_rows",
+    )(slots)
+
+
 def gather_kernel(live, sens, slots, out, table):
     cells = jnp.concatenate([sens[:, lane_tile(k)] for k in range(TILES)], axis=0).T
     for part, half in enumerate(two_parts(cells)):
         table[part * LANES : (part + 1) * LANES, :] = half.astype(BF)
-    place = lax.broadcasted_iota(jnp.int32, (LANES, CHUNK), 0)
+    place = lax.broadcasted_iota(jnp.int32, (LANES, GATHER_ROWS * LANES), 0)
     out[...] = jnp.zeros_like(out)
 
-    @pl.loop(0, N_DOM)
-    def owner(j):
-        @pl.loop(0, live[j])
-        def chunk(k):
-            first = j * SLOT_ROWS + k * CHUNK_ROWS
-            slot = rows_of(slots, first, CHUNK_ROWS)
+    @pl.loop(0, LIVE_ROWS // (GATHER_ROWS * GATHER_STEPS))
+    def part(j):
+        for step in range(GATHER_STEPS):
+            base = (j * GATHER_STEPS + step) * GATHER_ROWS
+            rows = [live[0, base + i] for i in range(GATHER_ROWS)]
+            slot = jnp.concatenate([slots[pl.ds(row, 1), :] for row in rows], axis=1)
             high = jnp.where(slot < CELLS, ((slot >> 7) & (TILES - 1)) * CX + (slot >> 10), 512)
             picked = jnp.dot(table[...], one_hot(high, 256), preferred_element_type=F32)
             picked = picked[:LANES] + picked[LANES:]
             value = jnp.sum(
                 jnp.where(place == (slot & (LANES - 1)), picked, 0.0), axis=0, keepdims=True
             )
-            for i in range(CHUNK_ROWS):
-                out[pl.ds(first + i, 1), :] = value[:, lane_tile(i)]
-
-
-def gather(sens, slots):
-    live = jnp.sum(
-        (slots.reshape(N_DOM, CAP // CHUNK, CHUNK)[:, :, 0] < CELLS).astype(jnp.int32), axis=1
-    )
+            for i, row in enumerate(rows):
+                out[pl.ds(row, 1), :] = value[:, lane_tile(i)]
+
+
+def gather(live, sens, slots):
     return pl.pallas_call(
         gather_kernel,
-        out_shape=f32(N_DOM * SLOT_ROWS, LANES),
+        out_shape=f32(SLOT_ROWS, LANES),
         in_specs=[SMEM, VMEM, VMEM],
         out_specs=VMEM,
         scratch_shapes=[pltpu.VMEM((2 * LANES, 2 * LANES), BF)],
@@ -266,13 +296,13 @@
 def face_kernel(values, faces, out, total):
     total[...] = jnp.zeros_like(total)
 
-    @pl.loop(0, N_DOM)
-    def sender(j):
+    @pl.loop(0, SLOT_ROWS // (FACE_ROWS * FACE_STEPS))
+    def chunk(j):
         part = None
-        for k in range(CAP // CHUNK):
-            first = j * SLOT_ROWS + k * CHUNK_ROWS
-            face = rows_of(faces, first, CHUNK_ROWS)
-            value = rows_of(values, first, CHUNK_ROWS)
+        for k in range(FACE_STEPS):
+            first = (j * FACE_STEPS + k) * FACE_ROWS
+            face = rows_of(faces, first, FACE_ROWS)
+            value = rows_of(values, first, FACE_ROWS)
             step = outer_sum(
                 weighted(face >> 7, FACE_HI, [value]), one_hot(face & (LANES - 1), LANES)
             )
@@ -301,18 +331,21 @@
     faces[...] = (part0[...] + part1[...]) + (part2[...] + part3[...])
     total[...] = jnp.zeros_like(total)
 
-    @pl.loop(0, FACE_DEV // CHUNK)
-    def chunk(g):
-        sens = rows_of(faces, g * CHUNK_ROWS, CHUNK_ROWS)
-        columns = pl.ds(pl.multiple_of(g * CHUNK, CHUNK), CHUNK)
+    @pl.loop(0, FACE_HI // (NODE_ROWS * NODE_STEPS))
+    def chunk(j):
         part = None
-        for k in range(4):
-            node = nodes[k : k + 1, columns] - base
-            values = [grad[c, k : k + 1, columns] * sens for c in range(3)]
-            step = outer_sum(
-                weighted(node >> 7, NODE_HI, values), one_hot(node & (LANES - 1), LANES)
-            )
-            part = step if part is None else part + step
+        for step in range(NODE_STEPS):
+            g = j * NODE_STEPS + step
+            sens = rows_of(faces, g * NODE_ROWS, NODE_ROWS)
+            size = NODE_ROWS * LANES
+            columns = pl.ds(pl.multiple_of(g * size, size), size)
+            for k in range(4):
+                node = nodes[k : k + 1, columns] - base
+                values = [grad[c, k : k + 1, columns] * sens for c in range(3)]
+                product = outer_sum(
+                    weighted(node >> 7, NODE_HI, values), one_hot(node & (LANES - 1), LANES)
+                )
+                part = product if part is None else part + product
         total[...] += part
 
     for c in range(3):
@@ -345,9 +378,10 @@
     adjoint_rhs, block_inverse, coupling, distance_grad, slot_cell, slot_face, area_grad, face_nodes
 ):
     adjoint, cell_sens = relax(adjoint_rhs, block_inverse, coupling, distance_grad)
-    slot_vals = gather(cell_sens, slot_cell.reshape(N_DOM * SLOT_ROWS, LANES))
+    slots = slot_cell.reshape(SLOT_ROWS, LANES)
+    slot_vals = gather(live_rows(slots), cell_sens, slots)
     received = lax.all_to_all(slot_vals, "dom", split_axis=0, concat_axis=0, tiled=True)
-    face_part = face_sums(received, slot_face.reshape(N_DOM * SLOT_ROWS, LANES))
+    face_part = face_sums(received, slot_face.reshape(SLOT_ROWS, LANES))
     parts = [face_part] + [
         lax.ppermute(face_part, "span", shifted("span", N_SPAN, turn)) for turn in range(1, N_SPAN)
     ]

time: 131 us -> 106 us (0.81)
  Pallas kernels: 43.4 us -> 23 us
  local copies, waits for them, and re-layouts: 8.14 us -> 5.2 us
  other arithmetic: 1.93 us -> 0.02 us
    pallas_call x1 -> x2, Pallas kernels: 20.2 us -> 8.26 us  [the longest x1 6.25 us: gather(): pl.pallas_call(gather_kernel, out_shape=f32(SLOT_ROWS, LANES), in_specs=[...]
    pallas_call x1, Pallas kernels: 10.5 us -> 4.76 us  [face_sums(): pl.pallas_call(face_kernel, out_shape=f32(FACE_HI, LANES), in_specs=[VMEM...]
    unnamed x24 -> x19, local copies, waits for them, and re-layouts: 8.05 us -> 5.2 us
    pallas_call x1, Pallas kernels: 6.52 us -> 3.69 us  [node_sums(): pl.pallas_call(node_kernel, out_shape=(f32(FACE_HI, LANES), f32(3, NODE_H...]
  transfers between devices with their start and end apart: 23 -> 23, of which waited for: 13 -> 13; matrix products, arithmetic and copies ran while one was open for 2% -> 0% of each run, Pallas kernels for 0% -> 2%
where the time goes in v2:
time: 106 us
  waiting for transfers between devices  33.7 us (32%)
  starting transfers between devices  31.2 us (29%)
  Pallas kernels  23 us (22%)
  blocking collectives  11.9 us (11%)
  local copies, waits for them, and re-layouts  5.2 us (5%)
    ppermute x4, waiting for transfers between devices, exchange(): before = lax.ppermute(right, 'dom', shifted('dom', N_DOM, 1))  19.1 us
    ppermute x4, starting transfers between devices, exchange(): above = lax.ppermute(low, 'span', shifted('span', N_SPAN, -1))  13.8 us
    all_to_all x1, blocking collectives, shards(): lax.all_to_all(slot_vals, 'dom', split_axis=0, concat_axis=0, tiled=True)  11.9 us
    ppermute x4, waiting for transfers between devices, shards(): lax.ppermute(part, ('span', 'dom'), to_node_owners(turn))  7.39 us
    ppermute x4, starting transfers between devices, shards(): lax.ppermute(part, ('span', 'dom'), to_node_owners(turn))  6.75 us
    pallas_call x1, Pallas kernels, gather(): pl.pallas_call(gather_kernel, out_shape=f32(SLOT_ROWS, LANES), in_specs=[...  6.25 us
    unnamed x19, local copies, waits for them, and re-layouts  5.2 us
    ppermute x3, starting transfers between devices, shards(): lax.ppermute(face_part, 'span', shifted('span', N_SPAN, turn))  4.77 us
  transfers between devices with their start and end apart: 23, of which 13 were waited for; matrix products, arithmetic and copies ran while one was open for 0% of the time, Pallas kernels for 2%

profile of v2, /device:TPU:0, one launch (start us, length us, event | category | flops | bytes accessed | tf_op | source)
XLA Modules:
  0.0 105.8 jit_solution(12022325116043349540)
XLA Ops:
  0.6 2.3 %copy-done = f32[6,6,32,1024]{3,2,1,0:T(8,128)S(1)} copy-done((f32[6,6,32,1024]{3,2,1,0:T(8,128)S(1)}, f32[6,6,32,1024]{3,2,1,0:T(8,128)}, u32[]{:S(2)}) %copy-start) | copy-done | bytes 4718616
  3.0 1.1 %copy-done.1 = f32[6,32,1024]{2,1,0:T(8,128)S(1)} copy-done((f32[6,32,1024]{2,1,0:T(8,128)S(1)}, f32[6,32,1024]{2,1,0:T(8,128)}, u32[]{:S(2)}) %copy-start.1) | copy-done | bytes 786456
  4.1 1.0 copy-done.3
  5.1 0.6 first_product.1
  5.7 4.2 %collective-permute-start = (f32[8,1024]{1,0:T(8,128)S(1)}, f32[8,1024]{1,0:T(8,128)S(1)}, u32[]{:S(2)}, u32[]{:S(2)}) collective-permute-start(f32[8,1024]{1,0:T(8,128)S(1)} %get-tuple-element.28), channel_id=1, source_target_pairs={{0,96},{32,0},{64,32},{96,64},{1,97},{33,1},{65,33},{97,65},{2,98}... | collective-permute-start | bytes 98312 | tf_op jit(solution)/shard_map/ppermute | solution.py:156
  9.9 4.4 %collective-permute-start.2 = (f32[32,128]{1,0:T(8,128)S(1)}, f32[32,128]{1,0:T(8,128)S(1)}, u32[]{:S(2)}, u32[]{:S(2)}) collective-permute-start(f32[32,128]{1,0:T(8,128)S(1)} %get-tuple-element.30), channel_id=1, source_target_pairs={{0,31},{1,0},{2,1},{3,2},{4,3},{5,4},{6,5},{7,6},{8,7},{9,8},{10,9... | collective-permute-start | bytes 49160 | tf_op jit(solution)/shard_map/ppermute | solution.py:158
  14.3 0.0 collective-permute-start.3
  14.3 1.4 %collective-permute-done.2.after = f32[32,128]{1,0:T(8,128)S(1)} collective-permute-done((f32[32,128]{1,0:T(8,128)S(1)}, f32[32,128]{1,0:T(8,128)S(1)}, u32[]{:S(2)}, u32[]{:S(2)}) %collective-permute-start.2) | collective-permute-done | bytes 16416 | tf_op jit(solution)/shard_map/ppermute | solution.py:158
  15.7 5.0 %collective-permute-done.3.before = f32[32,128]{1,0:T(8,128)S(1)} collective-permute-done((f32[32,128]{1,0:T(8,128)S(1)}, f32[32,128]{1,0:T(8,128)S(1)}, u32[]{:S(2)}, u32[]{:S(2)}) %collective-permute-start.3) | collective-permute-done | bytes 16416 | tf_op jit(solution)/shard_map/ppermute | solution.py:159
  20.8 0.0 collective-permute-done.above
  20.8 1.2 %sweep.3 = (f32[6,32,1024]{2,1,0:T(8,128)S(1)}, f32[8,1024]{1,0:T(8,128)S(1)}, f32[8,1024]{1,0:T(8,128)S(1)}, f32[32,128]{1,0:T(8,128)S(1)}, f32[32,128]{1,0:T(8,128)S(1)}) custom-call(f32[6,32,1024]{2,1,0:T(8,128)S(1)} %copy-done.1, f32[6,6,32,1024]{3,2,1,0:T(8,128)S(1)} %copy-done, f32[4,32,1024]{2,1,0:T(8,128)S(1)} %copy-done.3, ...), custom_call_target="tpu_custom_call" | custom-call | tf_op jit(solution)/shard_map/sweep/pallas_call | solution.py:174
  22.0 3.0 %collective-permute-start.4 = (f32[8,1024]{1,0:T(8,128)S(1)}, f32[8,1024]{1,0:T(8,128)S(1)}, u32[]{:S(2)}, u32[]{:S(2)}) collective-permute-start(f32[8,1024]{1,0:T(8,128)S(1)} %get-tuple-element.33), channel_id=1, source_target_pairs={{0,96},{32,0},{64,32},{96,64},{1,97},{33,1},{65,33},{97,65},{2,98}... | collective-permute-start | bytes 98312 | tf_op jit(solution)/shard_map/ppermute | solution.py:156
  25.0 0.0 collective-permute-start.5
  25.0 0.5 collective-permute-start.7
  25.5 0.9 collective-permute-done.6.after
  26.5 5.0 %collective-permute-done.7.before = f32[32,128]{1,0:T(8,128)S(1)} collective-permute-done((f32[32,128]{1,0:T(8,128)S(1)}, f32[32,128]{1,0:T(8,128)S(1)}, u32[]{:S(2)}, u32[]{:S(2)}) %collective-permute-start.7) | collective-permute-done | bytes 16416 | tf_op jit(solution)/shard_map/ppermute | solution.py:159
  31.5 1.2 %sweep.4 = (f32[6,32,1024]{2,1,0:T(8,128)S(1)}, f32[8,1024]{1,0:T(8,128)S(1)}, f32[8,1024]{1,0:T(8,128)S(1)}, f32[32,128]{1,0:T(8,128)S(1)}, f32[32,128]{1,0:T(8,128)S(1)}) custom-call(f32[6,32,1024]{2,1,0:T(8,128)S(1)} %copy-done.1, f32[6,6,32,1024]{3,2,1,0:T(8,128)S(1)} %copy-done, f32[4,32,1024]{2,1,0:T(8,128)S(1)} %copy-done.3, ...), custom_call_target="tpu_custom_call" | custom-call | tf_op jit(solution)/shard_map/sweep/pallas_call | solution.py:174
  32.8 0.0 copy-start.2
  32.8 0.0 copy-start.7
  32.8 3.3 %collective-permute-start.8 = (f32[8,1024]{1,0:T(8,128)S(1)}, f32[8,1024]{1,0:T(8,128)S(1)}, u32[]{:S(2)}, u32[]{:S(2)}) collective-permute-start(f32[8,1024]{1,0:T(8,128)S(1)} %get-tuple-element.38), channel_id=1, source_target_pairs={{0,96},{32,0},{64,32},{96,64},{1,97},{33,1},{65,33},{97,65},{2,98}... | collective-permute-start | bytes 98312 | tf_op jit(solution)/shard_map/ppermute | solution.py:156
  36.1 0.5 collective-permute-start.11
  36.6 0.9 collective-permute-done.10.after
  37.5 5.0 %collective-permute-done.11.before = f32[32,128]{1,0:T(8,128)S(1)} collective-permute-done((f32[32,128]{1,0:T(8,128)S(1)}, f32[32,128]{1,0:T(8,128)S(1)}, u32[]{:S(2)}, u32[]{:S(2)}) %collective-permute-start.11) | collective-permute-done | bytes 16416 | tf_op jit(solution)/shard_map/ppermute | solution.py:159
  42.6 1.2 %sweep.5 = (f32[6,32,1024]{2,1,0:T(8,128)S(1)}, f32[8,1024]{1,0:T(8,128)S(1)}, f32[8,1024]{1,0:T(8,128)S(1)}, f32[32,128]{1,0:T(8,128)S(1)}, f32[32,128]{1,0:T(8,128)S(1)}) custom-call(f32[6,32,1024]{2,1,0:T(8,128)S(1)} %copy-done.1, f32[6,6,32,1024]{3,2,1,0:T(8,128)S(1)} %copy-done, f32[4,32,1024]{2,1,0:T(8,128)S(1)} %copy-done.3, ...), custom_call_target="tpu_custom_call" | custom-call | tf_op jit(solution)/shard_map/sweep/pallas_call | solution.py:174
  43.8 0.0 copy-start.5
  43.8 0.0 copy-start.8
  43.8 3.3 %collective-permute-start.12 = (f32[8,1024]{1,0:T(8,128)S(1)}, f32[8,1024]{1,0:T(8,128)S(1)}, u32[]{:S(2)}, u32[]{:S(2)}) collective-permute-start(f32[8,1024]{1,0:T(8,128)S(1)} %get-tuple-element.43), channel_id=1, source_target_pairs={{0,96},{32,0},{64,32},{96,64},{1,97},{33,1},{65,33},{97,65},{2,98}... | collective-permute-start | bytes 98312 | tf_op jit(solution)/shard_map/ppermute | solution.py:156
  47.2 0.5 collective-permute-start.15
  47.7 2.0 %live_rows.1.live = s32[8,384]{1,0:T(8,128)S(1)} custom-call(s32[512,128]{1,0:T(8,128)S(1)} %bitcast.11), custom_call_target="tpu_custom_call" | custom-call | tf_op jit(solution)/shard_map/live_rows/pallas_call | solution.py:250
  49.7 3.9 %collective-permute-done.15.before = f32[32,128]{1,0:T(8,128)S(1)} collective-permute-done((f32[32,128]{1,0:T(8,128)S(1)}, f32[32,128]{1,0:T(8,128)S(1)}, u32[]{:S(2)}, u32[]{:S(2)}) %collective-permute-start.15) | collective-permute-done | bytes 16416 | tf_op jit(solution)/shard_map/ppermute | solution.py:159
  53.7 2.0 %last_sweep.1 = (f32[6,32,1024]{2,1,0:T(8,128)}, f32[32,1024]{1,0:T(8,128)S(1)}) custom-call(f32[6,32,1024]{2,1,0:T(8,128)S(1)} %copy-done.2, f32[6,6,32,1024]{3,2,1,0:T(8,128)S(1)} %copy-done, f32[4,32,1024]{2,1,0:T(8,128)S(1)} %copy-done.3, f32[6,32,1024]{2,1,0:T(8,128)S(1)} %get-tuple-element.42.field, f32[8,1024]{1,0:T(8,128)S(1)} %collective-permute-done.12.above, ...), custom_call_target="tpu_custom_call" | custom-call | tf_op jit(solution)/shard_map/last_sweep/pallas_call | solution.py:182
  55.6 6.2 %gather_slots.1 = f32[512,128]{1,0:T(8,128)S(1)} custom-call(s32[8,384]{1,0:T(8,128)S(1)} %live_rows.1.live, f32[32,1024]{1,0:T(8,128)S(1)} %get-tuple-element.48.sens, s32[512,128]{1,0:T(8,128)S(1)} %bitcast.12), custom_call_target="tpu_custom_call" | custom-call | tf_op jit(solution)/shard_map/gather_slots/pallas_call | solution.py:285
  61.9 11.9 %all_to_all.11 = f32[32,16,128]{2,1,0:T(8,128)S(1)} all-to-all(f32[32,16,128]{2,1,0:T(8,128)S(1)} %bitcast.13), channel_id=1, replica_groups=mesh['span'=4,'dom'=32] {'dom'}, dimensions={0} | all-to-all | bytes 524288 | tf_op jit(solution)/shard_map/all_to_all | solution.py:383
  73.8 4.8 %face_sums.1.part0 = f32[64,128]{1,0:T(8,128)S(1)} custom-call(f32[512,128]{1,0:T(8,128)S(1)} %bitcast.10, s32[512,128]{1,0:T(8,128)S(1)} %bitcast.14), custom_call_target="tpu_custom_call" | custom-call | tf_op jit(solution)/shard_map/face_sums/pallas_call | solution.py:316
  78.6 0.1 collective-permute-start.16
  78.6 4.7 %collective-permute-start.17 = (f32[64,128]{1,0:T(8,128)S(1)}, f32[64,128]{1,0:T(8,128)S(1)}, u32[]{:S(2)}, u32[]{:S(2)}) collective-permute-start(f32[64,128]{1,0:T(8,128)S(1)} %face_sums.1.part0), channel_id=1, source_target_pairs={{0,64},{32,96},{64,0},{96,32},{1,65},{33,97},{65,1},{97,33},{2,66}... | collective-permute-start | bytes 98312 | tf_op jit(solution)/shard_map/ppermute | solution.py:386
  83.3 0.4 collective-permute-done.16.part1
  83.8 1.8 %collective-permute-done.17.part2 = f32[64,128]{1,0:T(8,128)S(1)} collective-permute-done((f32[64,128]{1,0:T(8,128)S(1)}, f32[64,128]{1,0:T(8,128)S(1)}, u32[]{:S(2)}, u32[]{:S(2)}) %collective-permute-start.17) | collective-permute-done | bytes 32800 | tf_op jit(solution)/shard_map/ppermute | solution.py:386
  85.6 1.7 %collective-permute-done.18.part3 = f32[64,128]{1,0:T(8,128)S(1)} collective-permute-done((f32[64,128]{1,0:T(8,128)S(1)}, f32[64,128]{1,0:T(8,128)S(1)}, u32[]{:S(2)}, u32[]{:S(2)}) %collective-permute-start.18) | collective-permute-done | bytes 32800 | tf_op jit(solution)/shard_map/ppermute | solution.py:386
  87.3 3.7 %node_sums.1 = (f32[64,128]{1,0:T(8,128)}, f32[3,32,128]{2,1,0:T(8,128)S(1)}) custom-call(f32[64,128]{1,0:T(8,128)S(1)} %face_sums.1.part0, f32[64,128]{1,0:T(8,128)S(1)} %collective-permute-done.16.part1, f32[64,128]{1,0:T(8,128)S(1)} %collective-permute-done.17.part2, f32[64,128]{1,0:T(8,128)S(1)} %collective-permute-done.18.part3, ...), custom_call_target="tpu_custom_call" | custom-call | tf_op jit(solution)/shard_map/node_sums/pallas_call | solution.py:357
  90.9 0.7 collective-permute-start.19
  91.6 1.0 collective-permute-start.20
  92.7 4.7 %collective-permute-start.21 = (f32[3,32,128]{2,1,0:T(8,128)S(1)}, f32[3,32,128]{2,1,0:T(8,128)S(1)}, u32[]{:S(2)}, u32[]{:S(2)}) collective-permute-start(f32[3,32,128]{2,1,0:T(8,128)S(1)} %get-tuple-element.50), channel_id=1, source_target_pairs={{0,64},{1,65},{2,66},{3,67},{4,68},{5,69},{6,70},{7,71},{8,72},{9,... | collective-permute-start | bytes 147464 | tf_op jit(solution)/shard_map/ppermute | solution.py:390
  97.4 0.3 collective-permute-start.22
  97.7 2.4 %collective-permute-done.20 = f32[3,32,128]{2,1,0:T(8,128)S(1)} collective-permute-done((f32[3,32,128]{2,1,0:T(8,128)S(1)}, f32[3,32,128]{2,1,0:T(8,128)S(1)}, u32[]{:S(2)}, u32[]{:S(2)}) %collective-permute-start.20) | collective-permute-done | bytes 49184 | tf_op jit(solution)/shard_map/ppermute | solution.py:390
  100.1 0.1 collective-permute-done.21
  100.3 4.8 %collective-permute-done.22 = f32[3,32,128]{2,1,0:T(8,128)S(1)} collective-permute-done((f32[3,32,128]{2,1,0:T(8,128)S(1)}, f32[3,32,128]{2,1,0:T(8,128)S(1)}, u32[]{:S(2)}, u32[]{:S(2)}) %collective-permute-start.22) | collective-permute-done | bytes 49184 | tf_op jit(solution)/shard_map/ppermute | solution.py:390
  105.1 0.7 copy.13
  (28 shorter events, 0.1 us)
Async XLA Ops:
  0.6 2.3 %copy-start = (f32[6,6,32,1024]{3,2,1,0:T(8,128)S(1)}, f32[6,6,32,1024]{3,2,1,0:T(8,128)}, u32[]{:S(2)}) copy-start(f32[6,6,32,1024]{3,2,1,0:T(8,128)} %inverse.9) | copy-start | bytes 14155780
  3.0 1.1 %copy-start.1 = (f32[6,32,1024]{2,1,0:T(8,128)S(1)}, f32[6,32,1024]{2,1,0:T(8,128)}, u32[]{:S(2)}) copy-start(f32[6,32,1024]{2,1,0:T(8,128)} %rhs.9) | copy-start | bytes 2359300
  4.1 1.0 copy-start.3
  5.7 15.0 %collective-permute-start = (f32[8,1024]{1,0:T(8,128)S(1)}, f32[8,1024]{1,0:T(8,128)S(1)}, u32[]{:S(2)}, u32[]{:S(2)}) collective-permute-start(f32[8,1024]{1,0:T(8,128)S(1)} %get-tuple-element.28), channel_id=1, source_target_pairs={{0,96},{32,0},{64,32},{96,64},{1,97},{33,1},{65,33},{97,65},{2,98}... | collective-permute-start | bytes 98312 | tf_op jit(solution)/shard_map/ppermute | solution.py:156
  9.9 10.9 %collective-permute-start.1 = (f32[8,1024]{1,0:T(8,128)S(1)}, f32[8,1024]{1,0:T(8,128)S(1)}, u32[]{:S(2)}, u32[]{:S(2)}) collective-permute-start(f32[8,1024]{1,0:T(8,128)S(1)} %get-tuple-element.29), channel_id=1, source_target_pairs={{0,32},{32,64},{64,96},{96,0},{1,33},{33,65},{65,97},{97,1},{2,34}... | collective-permute-start | bytes 98312 | tf_op jit(solution)/shard_map/ppermute | solution.py:157
  9.9 5.8 %collective-permute-start.2 = (f32[32,128]{1,0:T(8,128)S(1)}, f32[32,128]{1,0:T(8,128)S(1)}, u32[]{:S(2)}, u32[]{:S(2)}) collective-permute-start(f32[32,128]{1,0:T(8,128)S(1)} %get-tuple-element.30), channel_id=1, source_target_pairs={{0,31},{1,0},{2,1},{3,2},{4,3},{5,4},{6,5},{7,6},{8,7},{9,8},{10,9... | collective-permute-start | bytes 49160 | tf_op jit(solution)/shard_map/ppermute | solution.py:158
  14.3 6.5 %collective-permute-start.3 = (f32[32,128]{1,0:T(8,128)S(1)}, f32[32,128]{1,0:T(8,128)S(1)}, u32[]{:S(2)}, u32[]{:S(2)}) collective-permute-start(f32[32,128]{1,0:T(8,128)S(1)} %get-tuple-element.31), channel_id=1, source_target_pairs={{0,1},{1,2},{2,3},{3,4},{4,5},{5,6},{6,7},{7,8},{8,9},{9,10},{10,1... | collective-permute-start | bytes 49160 | tf_op jit(solution)/shard_map/ppermute | solution.py:159
  22.0 9.5 %collective-permute-start.4 = (f32[8,1024]{1,0:T(8,128)S(1)}, f32[8,1024]{1,0:T(8,128)S(1)}, u32[]{:S(2)}, u32[]{:S(2)}) collective-permute-start(f32[8,1024]{1,0:T(8,128)S(1)} %get-tuple-element.33), channel_id=1, source_target_pairs={{0,96},{32,0},{64,32},{96,64},{1,97},{33,1},{65,33},{97,65},{2,98}... | collective-permute-start | bytes 98312 | tf_op jit(solution)/shard_map/ppermute | solution.py:156
  25.0 6.5 %collective-permute-start.5 = (f32[8,1024]{1,0:T(8,128)S(1)}, f32[8,1024]{1,0:T(8,128)S(1)}, u32[]{:S(2)}, u32[]{:S(2)}) collective-permute-start(f32[8,1024]{1,0:T(8,128)S(1)} %get-tuple-element.34), channel_id=1, source_target_pairs={{0,32},{32,64},{64,96},{96,0},{1,33},{33,65},{65,97},{97,1},{2,34}... | collective-permute-start | bytes 98312 | tf_op jit(solution)/shard_map/ppermute | solution.py:157
  25.0 1.4 %collective-permute-start.6 = (f32[32,128]{1,0:T(8,128)S(1)}, f32[32,128]{1,0:T(8,128)S(1)}, u32[]{:S(2)}, u32[]{:S(2)}) collective-permute-start(f32[32,128]{1,0:T(8,128)S(1)} %get-tuple-element.35), channel_id=1, source_target_pairs={{0,31},{1,0},{2,1},{3,2},{4,3},{5,4},{6,5},{7,6},{8,7},{9,8},{10,9... | collective-permute-start | bytes 49160 | tf_op jit(solution)/shard_map/ppermute | solution.py:158
  25.0 6.5 %collective-permute-start.7 = (f32[32,128]{1,0:T(8,128)S(1)}, f32[32,128]{1,0:T(8,128)S(1)}, u32[]{:S(2)}, u32[]{:S(2)}) collective-permute-start(f32[32,128]{1,0:T(8,128)S(1)} %get-tuple-element.36), channel_id=1, source_target_pairs={{0,1},{1,2},{2,3},{3,4},{4,5},{5,6},{6,7},{7,8},{8,9},{9,10},{10,1... | collective-permute-start | bytes 49160 | tf_op jit(solution)/shard_map/ppermute | solution.py:159
  32.8 14.9 %copy-start.4 = (s32[1,1,65536]{2,1,0:T(1,128)S(1)}, s32[1,1,65536]{2,1,0:T(1,128)}, u32[]{:S(2)}) copy-start(s32[1,1,65536]{2,1,0:T(1,128)} %param.12) | copy-start | bytes 786436
  32.8 20.9 %copy-start.2 = (f32[6,32,1024]{2,1,0:T(8,128)S(1)}, f32[6,32,1024]{2,1,0:T(8,128)}, u32[]{:S(2)}) copy-start(f32[6,32,1024]{2,1,0:T(8,128)} %rhs.9) | copy-start | bytes 2359300
  32.8 20.9 %copy-start.7 = (f32[1,32,1024]{2,1,0:T(8,128)S(1)}, f32[1,32,1024]{2,1,0:T(8,128)}, u32[]{:S(2)}) copy-start(f32[1,32,1024]{2,1,0:T(8,128)} %grad.2) | copy-start | bytes 393220
  32.8 9.8 %collective-permute-start.8 = (f32[8,1024]{1,0:T(8,128)S(1)}, f32[8,1024]{1,0:T(8,128)S(1)}, u32[]{:S(2)}, u32[]{:S(2)}) collective-permute-start(f32[8,1024]{1,0:T(8,128)S(1)} %get-tuple-element.38), channel_id=1, source_target_pairs={{0,96},{32,0},{64,32},{96,64},{1,97},{33,1},{65,33},{97,65},{2,98}... | collective-permute-start | bytes 98312 | tf_op jit(solution)/shard_map/ppermute | solution.py:156
  36.1 6.5 %collective-permute-start.9 = (f32[8,1024]{1,0:T(8,128)S(1)}, f32[8,1024]{1,0:T(8,128)S(1)}, u32[]{:S(2)}, u32[]{:S(2)}) collective-permute-start(f32[8,1024]{1,0:T(8,128)S(1)} %get-tuple-element.39), channel_id=1, source_target_pairs={{0,32},{32,64},{64,96},{96,0},{1,33},{33,65},{65,97},{97,1},{2,34}... | collective-permute-start | bytes 98312 | tf_op jit(solution)/shard_map/ppermute | solution.py:157
  36.1 1.4 %collective-permute-start.10 = (f32[32,128]{1,0:T(8,128)S(1)}, f32[32,128]{1,0:T(8,128)S(1)}, u32[]{:S(2)}, u32[]{:S(2)}) collective-permute-start(f32[32,128]{1,0:T(8,128)S(1)} %get-tuple-element.40), channel_id=1, source_target_pairs={{0,31},{1,0},{2,1},{3,2},{4,3},{5,4},{6,5},{7,6},{8,7},{9,8},{10,9... | collective-permute-start | bytes 49160 | tf_op jit(solution)/shard_map/ppermute | solution.py:158
  36.1 6.5 %collective-permute-start.11 = (f32[32,128]{1,0:T(8,128)S(1)}, f32[32,128]{1,0:T(8,128)S(1)}, u32[]{:S(2)}, u32[]{:S(2)}) collective-permute-start(f32[32,128]{1,0:T(8,128)S(1)} %get-tuple-element.41), channel_id=1, source_target_pairs={{0,1},{1,2},{2,3},{3,4},{4,5},{5,6},{6,7},{7,8},{8,9},{9,10},{10,1... | collective-permute-start | bytes 49160 | tf_op jit(solution)/shard_map/ppermute | solution.py:159
  43.8 30.0 %copy-start.6 = (s32[1,1,65536]{2,1,0:T(1,128)S(1)}, s32[1,1,65536]{2,1,0:T(1,128)}, u32[]{:S(2)}) copy-start(s32[1,1,65536]{2,1,0:T(1,128)} %param.13) | copy-start | bytes 786436
  43.8 43.4 %copy-start.5 = (f32[3,4,8192]{2,1,0:T(4,128)S(1)}, f32[3,4,8192]{2,1,0:T(4,128)}, u32[]{:S(2)}) copy-start(f32[3,4,8192]{2,1,0:T(4,128)} %grad.3) | copy-start | bytes 1179652
  43.8 43.4 %copy-start.8 = (s32[4,8192]{1,0:T(4,128)S(1)}, s32[4,8192]{1,0:T(4,128)}, u32[]{:S(2)}) copy-start(s32[4,8192]{1,0:T(4,128)} %nodes.1) | copy-start | bytes 393220
  43.8 9.8 %collective-permute-start.12 = (f32[8,1024]{1,0:T(8,128)S(1)}, f32[8,1024]{1,0:T(8,128)S(1)}, u32[]{:S(2)}, u32[]{:S(2)}) collective-permute-start(f32[8,1024]{1,0:T(8,128)S(1)} %get-tuple-element.43), channel_id=1, source_target_pairs={{0,96},{32,0},{64,32},{96,64},{1,97},{33,1},{65,33},{97,65},{2,98}... | collective-permute-start | bytes 98312 | tf_op jit(solution)/shard_map/ppermute | solution.py:156
  47.1 6.5 %collective-permute-start.13 = (f32[8,1024]{1,0:T(8,128)S(1)}, f32[8,1024]{1,0:T(8,128)S(1)}, u32[]{:S(2)}, u32[]{:S(2)}) collective-permute-start(f32[8,1024]{1,0:T(8,128)S(1)} %get-tuple-element.44), channel_id=1, source_target_pairs={{0,32},{32,64},{64,96},{96,0},{1,33},{33,65},{65,97},{97,1},{2,34}... | collective-permute-start | bytes 98312 | tf_op jit(solution)/shard_map/ppermute | solution.py:157
  47.1 2.5 %collective-permute-start.14 = (f32[32,128]{1,0:T(8,128)S(1)}, f32[32,128]{1,0:T(8,128)S(1)}, u32[]{:S(2)}, u32[]{:S(2)}) collective-permute-start(f32[32,128]{1,0:T(8,128)S(1)} %get-tuple-element.45), channel_id=1, source_target_pairs={{0,31},{1,0},{2,1},{3,2},{4,3},{5,4},{6,5},{7,6},{8,7},{9,8},{10,9... | collective-permute-start | bytes 49160 | tf_op jit(solution)/shard_map/ppermute | solution.py:158
  47.2 6.5 %collective-permute-start.15 = (f32[32,128]{1,0:T(8,128)S(1)}, f32[32,128]{1,0:T(8,128)S(1)}, u32[]{:S(2)}, u32[]{:S(2)}) collective-permute-start(f32[32,128]{1,0:T(8,128)S(1)} %get-tuple-element.46), channel_id=1, source_target_pairs={{0,1},{1,2},{2,3},{3,4},{4,5},{5,6},{6,7},{7,8},{8,9},{9,10},{10,1... | collective-permute-start | bytes 49160 | tf_op jit(solution)/shard_map/ppermute | solution.py:159
  78.6 5.2 %collective-permute-start.16 = (f32[64,128]{1,0:T(8,128)S(1)}, f32[64,128]{1,0:T(8,128)S(1)}, u32[]{:S(2)}, u32[]{:S(2)}) collective-permute-start(f32[64,128]{1,0:T(8,128)S(1)} %face_sums.1.part0), channel_id=1, source_target_pairs={{0,32},{32,64},{64,96},{96,0},{1,33},{33,65},{65,97},{97,1},{2,34}... | collective-permute-start | bytes 98312 | tf_op jit(solution)/shard_map/ppermute | solution.py:386
  78.6 6.9 %collective-permute-start.17 = (f32[64,128]{1,0:T(8,128)S(1)}, f32[64,128]{1,0:T(8,128)S(1)}, u32[]{:S(2)}, u32[]{:S(2)}) collective-permute-start(f32[64,128]{1,0:T(8,128)S(1)} %face_sums.1.part0), channel_id=1, source_target_pairs={{0,64},{32,96},{64,0},{96,32},{1,65},{33,97},{65,1},{97,33},{2,66}... | collective-permute-start | bytes 98312 | tf_op jit(solution)/shard_map/ppermute | solution.py:386
  83.3 3.9 %collective-permute-start.18 = (f32[64,128]{1,0:T(8,128)S(1)}, f32[64,128]{1,0:T(8,128)S(1)}, u32[]{:S(2)}, u32[]{:S(2)}) collective-permute-start(f32[64,128]{1,0:T(8,128)S(1)} %face_sums.1.part0), channel_id=1, source_target_pairs={{0,96},{32,0},{64,32},{96,64},{1,97},{33,1},{65,33},{97,65},{2,98}... | collective-permute-start | bytes 98312 | tf_op jit(solution)/shard_map/ppermute | solution.py:386
  90.9 6.8 %collective-permute-start.19 = (f32[3,32,128]{2,1,0:T(8,128)S(1)}, f32[3,32,128]{2,1,0:T(8,128)S(1)}, u32[]{:S(2)}, u32[]{:S(2)}) collective-permute-start(f32[3,32,128]{2,1,0:T(8,128)S(1)} %get-tuple-element.50), channel_id=1, source_target_pairs={{0,0},{1,1},{2,2},{3,3},{4,4},{5,5},{6,6},{7,7},{8,8},{9,9},{10,10... | collective-permute-start | bytes 147464 | tf_op jit(solution)/shard_map/ppermute | solution.py:390
  91.6 8.5 %collective-permute-start.20 = (f32[3,32,128]{2,1,0:T(8,128)S(1)}, f32[3,32,128]{2,1,0:T(8,128)S(1)}, u32[]{:S(2)}, u32[]{:S(2)}) collective-permute-start(f32[3,32,128]{2,1,0:T(8,128)S(1)} %get-tuple-element.50), channel_id=1, source_target_pairs={{0,32},{1,33},{2,34},{3,35},{4,36},{5,37},{6,38},{7,39},{8,40},{9,... | collective-permute-start | bytes 147464 | tf_op jit(solution)/shard_map/ppermute | solution.py:390
  92.7 7.6 %collective-permute-start.21 = (f32[3,32,128]{2,1,0:T(8,128)S(1)}, f32[3,32,128]{2,1,0:T(8,128)S(1)}, u32[]{:S(2)}, u32[]{:S(2)}) collective-permute-start(f32[3,32,128]{2,1,0:T(8,128)S(1)} %get-tuple-element.50), channel_id=1, source_target_pairs={{0,64},{1,65},{2,66},{3,67},{4,68},{5,69},{6,70},{7,71},{8,72},{9,... | collective-permute-start | bytes 147464 | tf_op jit(solution)/shard_map/ppermute | solution.py:390
  97.4 7.7 %collective-permute-start.22 = (f32[3,32,128]{2,1,0:T(8,128)S(1)}, f32[3,32,128]{2,1,0:T(8,128)S(1)}, u32[]{:S(2)}, u32[]{:S(2)}) collective-permute-start(f32[3,32,128]{2,1,0:T(8,128)S(1)} %get-tuple-element.50), channel_id=1, source_target_pairs={{0,96},{1,97},{2,98},{3,99},{4,100},{5,101},{6,102},{7,103},{8,104... | collective-permute-start | bytes 147464 | tf_op jit(solution)/shard_map/ppermute | solution.py:390

commit v3 on v2

--- a/solution.py
+++ b/solution.py
@@ -1,5 +1,6 @@
 import jax
 import jax.numpy as jnp
+import numpy as np
 from jax import lax
 from jax.experimental import pallas as pl
 from jax.experimental.pallas import tpu as pltpu
@@ -17,6 +18,14 @@
 N_DOM = 32
 LANES = 128
 TILES = CY // LANES
+EXT = CY + LANES
+WIDE = SWEEPS
+PER_TILE = LANES // WIDE
+GIVEN = NVAR * NVAR + NVAR + 4
+PACKED = 2
+AT_RHS = NVAR * NVAR
+AT_COUPLING = AT_RHS + NVAR
+AT_FIELD = AT_COUPLING + 8
 SLOT_ROWS = N_DOM * CAP // LANES
 LIVE_ROWS = CELLS // LANES + N_DOM
 LIVE_PAD = 384
@@ -41,152 +50,261 @@
     return slice(k * LANES, (k + 1) * LANES)
 
 
-def product(inverse, terms, k):
+def product(inverse, terms):
     out = []
     for a in range(NVAR):
-        total = inverse[0, a, :, lane_tile(k)] * terms[0]
+        total = inverse(0, a) * terms[0]
         for b in range(1, NVAR):
-            total = total + inverse[b, a, :, lane_tile(k)] * terms[b]
+            total = total + inverse(b, a) * terms[b]
         out.append(total)
     return out
 
 
-def store_edges(values, coupling, k, low, high, left, right):
-    for a in range(NVAR):
-        low[a : a + 1, lane_tile(k)] = coupling[1, 0:1, lane_tile(k)] * values[a][0:1]
-        high[a : a + 1, lane_tile(k)] = coupling[0, CX - 1 : CX, lane_tile(k)] * values[a][CX - 1 :]
+def pack_kernel(
+    inverse0, rhs0, coupling0, inverse7, rhs7, coupling7, first, last
+):
+    group = lax.broadcasted_iota(jnp.int32, (CX, LANES), 1) // WIDE
+    for inverse, rhs, coupling, start, out in (
+        (inverse0, rhs0, coupling0, 0, first),
+        (inverse7, rhs7, coupling7, LANES - WIDE, last),
+    ):
+        given = [inverse[b, a] for b in range(NVAR) for a in range(NVAR)]
+        given += [rhs[b] for b in range(NVAR)] + [coupling[i] for i in range(4)]
+        for t in range(PACKED):
+            total = jnp.zeros((CX, LANES), F32)
+            for q, value in enumerate(given[t * PER_TILE : (t + 1) * PER_TILE]):
+                moved = pltpu.roll(value, (q * WIDE - start) % LANES, 1)
+                total = jnp.where(group == q, moved, total)
+            out[t] = total
+
+
+def pack_columns(inverse, rhs, coupling):
+    def specs(k):
+        return [
+            pl.BlockSpec((NVAR, NVAR, CX, LANES), lambda i: (0, 0, 0, k)),
+            pl.BlockSpec((NVAR, CX, LANES), lambda i: (0, 0, k)),
+            pl.BlockSpec((4, CX, LANES), lambda i: (0, 0, k)),
+        ]
+
+    return pl.pallas_call(
+        pack_kernel,
+        grid=(1,),
+        out_shape=(f32(PACKED, CX, LANES),) * 2,
+        in_specs=specs(0) + specs(TILES - 1),
+        out_specs=[pl.BlockSpec((PACKED, CX, LANES), lambda i: (0, 0, 0))] * 2,
+        compiler_params=PARAMS,
+        name="pack_columns",
+    )(inverse, rhs, coupling, inverse, rhs, coupling)
+
+
+def first_kernel(
+    rhs, inverse, coupling, after, before, rhs_rim, inverse_rim, coupling_rim, out, low, high
+):
     lane = lax.broadcasted_iota(jnp.int32, (CX, LANES), 1)
-    if k == 0:
-        total = jnp.zeros((CX, LANES), F32)
+    for v in range(GIVEN):
+        t, q = divmod(v, PER_TILE)
+        follow = pltpu.roll(after[t], -q * WIDE % LANES, 1)
+        precede = pltpu.roll(before[t], LANES - WIDE - q * WIDE, 1)
+        value = jnp.where(lane < LANES // 2, follow, precede)
+        if v < NVAR * NVAR:
+            inverse_rim[v // NVAR, v % NVAR] = value
+        elif v < NVAR * (NVAR + 1):
+            rhs_rim[v - NVAR * NVAR] = value
+        else:
+            coupling_rim[v - NVAR * (NVAR + 1)] = value
+
+    for k in range(TILES + 1):
+        at = lane_tile(k)
+        if k < TILES:
+            terms = [rhs[b, :, at] for b in range(NVAR)]
+            values = product(lambda b, a: inverse[b, a, :, at], terms)
+        else:
+            terms = [rhs_rim[b] for b in range(NVAR)]
+            values = product(lambda b, a: inverse_rim[b, a], terms)
         for a in range(NVAR):
-            edge = coupling[3, :, lane_tile(k)] * values[a]
-            total = jnp.where(lane == a, pltpu.roll(edge, a, 1) if a else edge, total)
-        left[...] = total
-    if k == TILES - 1:
-        total = jnp.zeros((CX, LANES), F32)
+            out[a, :, at] = values[a]
+
+    for message, near, second in ((low, 0, 1), (high, CX - 1, CX - 2)):
+        message[...] = jnp.zeros_like(message)
+        for part, rim, at, rows in (
+            (inverse, inverse_rim, 0, (near,)),
+            (rhs, rhs_rim, AT_RHS, (near,)),
+            (coupling, coupling_rim, AT_COUPLING, (near, second)),
+        ):
+            shape = rim.shape[:-2]
+            for row in rows:
+                for index in np.ndindex(*shape):
+                    message[at : at + 1, :CY] = part[(*index, slice(row, row + 1), slice(None))]
+                    message[at : at + 1, CY:] = rim[(*index, slice(row, row + 1), slice(None))]
+                    at += 1
+        field_rows(message, AT_FIELD, out, near, second)
+
+
+def field_rows(message, at, field, near, second):
+    for row in (near, second):
+        for b in range(NVAR):
+            message[at : at + 1, :] = field[b, row : row + 1, :]
+            at += 1
+
+
+def halo_tile(above, below, at, second_at, k):
+    span = lax.axis_index("span")
+    row = lax.broadcasted_iota(jnp.int32, (8, LANES), 0)
+    tile = jnp.zeros((8, LANES), F32)
+    for source, end, places in ((above, N_SPAN - 1, (0, 1)), (below, 0, (7, 6))):
+        part = jnp.zeros((8, LANES), F32)
+        for place, index in zip(places, (at, second_at)):
+            if index is not None:
+                part = jnp.where(row == place, source[index : index + 1, lane_tile(k)], part)
+        tile = tile + jnp.where(span == end, 0.0, part)
+    return tile
+
+
+def with_halo(main, rim, halo, index, k):
+    core = rim[index] if k == TILES else main[(*index, slice(None), lane_tile(k))]
+    return jnp.concatenate([core, halo(index, k)], axis=0)
+
+
+def sweep(rows, tiles, rhs, inverse, coupling, field, store):
+    last = TILES + 1
+    lane = lax.broadcasted_iota(jnp.int32, (rows, LANES), 1)
+    rolled = {}
+
+    def shifted_lanes(k, b, side):
+        k = k % last
+        if (k, b, side) not in rolled:
+            part = coupling((3 - side,), k)[:rows] * field((b,), k)[:rows]
+            rolled[k, b, side] = pltpu.roll(part, 1 if side else LANES - 1, 1)
+        return rolled[k, b, side]
+
+    for k in range(tiles):
+        terms = []
+        for b in range(NVAR):
+            value = field((b,), k)
+            size = value.shape[0]
+            total = pltpu.roll(coupling((1,), k) * value, size - 1, 0)[:rows]
+            total = total + pltpu.roll(coupling((0,), k) * value, 1, 0)[:rows]
+            edge = lane == LANES - 1
+            total = total + jnp.where(edge, shifted_lanes(k + 1, b, 0), shifted_lanes(k, b, 0))
+            total = total + jnp.where(lane == 0, shifted_lanes(k - 1, b, 1), shifted_lanes(k, b, 1))
+            terms.append(rhs((b,), k)[:rows] - total)
+        store(k, product(lambda b, a: inverse((b, a), k)[:rows], terms))
+
+
+def two_sweeps(given, rims, halos, field, field_halo, middle, tiles, store):
+    def full(name):
+        return lambda index, k: with_halo(
+            given[name], rims[name], lambda i, t: halos[name][(*i, slice(None), lane_tile(t))], index, k
+        )
+
+    rhs, inverse, coupling = full("rhs"), full("inverse"), full("coupling")
+
+    def before(index, k):
+        (b,) = index
+        return jnp.concatenate([field[b, :, lane_tile(k)], field_halo[b, :, lane_tile(k)]], axis=0)
+
+    def keep(k, values):
         for a in range(NVAR):
-            edge = coupling[2, :, lane_tile(k)] * values[a]
-            total = jnp.where(lane == a, pltpu.roll(edge, a + 1, 1), total)
-        right[...] = total
-
-
-def first_kernel(rhs, inverse, coupling, out, low, high, left, right):
-    for edge in (low, high):
-        edge[...] = jnp.zeros_like(edge)
-    for k in range(TILES):
-        values = product(inverse, [rhs[b, :, lane_tile(k)] for b in range(NVAR)], k)
+            middle[a, :, lane_tile(k)] = values[a]
+
+    sweep(CX + 8, TILES + 1, rhs, inverse, coupling, before, keep)
+    sweep(CX, tiles, rhs, inverse, coupling, lambda i, k: middle[i[0], :, lane_tile(k)], store)
+
+
+def middle_kernel(
+    rhs, inverse, coupling, rhs_rim, inverse_rim, coupling_rim, field, above, below,
+    rhs_halo, inverse_halo, coupling_halo, out, low, high, field_halo, middle,
+):
+    for k in range(TILES + 1):
+        at = lane_tile(k)
+        for b in range(NVAR):
+            for a in range(NVAR):
+                inverse_halo[b, a, :, at] = halo_tile(above, below, b * NVAR + a, None, k)
+            rhs_halo[b, :, at] = halo_tile(above, below, AT_RHS + b, None, k)
+            field_halo[b, :, at] = halo_tile(above, below, AT_FIELD + b, AT_FIELD + NVAR + b, k)
+        for i in range(4):
+            coupling_halo[i, :, at] = halo_tile(above, below, AT_COUPLING + i, AT_COUPLING + 4 + i, k)
+
+    def store(k, values):
         for a in range(NVAR):
             out[a, :, lane_tile(k)] = values[a]
-        store_edges(values, coupling, k, low, high, left, right)
-
-
-def neighbour_terms(rhs, coupling, field, above, below, after, before):
-    at = lax.axis_index("span")
-    row = lax.broadcasted_iota(jnp.int32, (CX, LANES), 0)
-    lane = lax.broadcasted_iota(jnp.int32, (CX, LANES), 1)
-    after_rolled = {}
-    before_rolled = {}
-
-    def roll_back(k, b):
-        if (k, b) not in after_rolled:
-            if k == TILES:
-                after_rolled[k, b] = pltpu.roll(after[...], LANES - 1 - b, 1)
-            else:
-                part = coupling[3, :, lane_tile(k)] * field[b, :, lane_tile(k)]
-                after_rolled[k, b] = pltpu.roll(part, LANES - 1, 1)
-        return after_rolled[k, b]
-
-    def roll_on(k, b):
-        if (k, b) not in before_rolled:
-            if k < 0:
-                before_rolled[k, b] = pltpu.roll(before[...], LANES - b, 1) if b else before[...]
-            else:
-                part = coupling[2, :, lane_tile(k)] * field[b, :, lane_tile(k)]
-                before_rolled[k, b] = pltpu.roll(part, 1, 1)
-        return before_rolled[k, b]
-
-    def tile(k):
-        terms = []
+
+    two_sweeps(
+        dict(rhs=rhs, inverse=inverse, coupling=coupling),
+        dict(rhs=rhs_rim, inverse=inverse_rim, coupling=coupling_rim),
+        dict(rhs=rhs_halo, inverse=inverse_halo, coupling=coupling_halo),
+        field, field_halo, middle, TILES + 1, store,
+    )
+    for message, near, second in ((low, 0, 1), (high, CX - 1, CX - 2)):
+        message[...] = jnp.zeros_like(message)
+        field_rows(message, 0, out, near, second)
+
+
+def last_kernel(
+    rhs, inverse, coupling, rhs_rim, inverse_rim, coupling_rim, rhs_halo, inverse_halo,
+    coupling_halo, field, above, below, grad, out, sens, field_halo, middle,
+):
+    for k in range(TILES + 1):
         for b in range(NVAR):
-            value = field[b, :, lane_tile(k)]
-            up = pltpu.roll(coupling[1, :, lane_tile(k)] * value, CX - 1, 0)
-            edge = jnp.where(at == N_SPAN - 1, 0.0, above[b : b + 1, lane_tile(k)])
-            total = jnp.where(row == CX - 1, edge, up)
-            down = pltpu.roll(coupling[0, :, lane_tile(k)] * value, 1, 0)
-            edge = jnp.where(at == 0, 0.0, below[b : b + 1, lane_tile(k)])
-            total = total + jnp.where(row == 0, edge, down)
-            total = total + jnp.where(lane == LANES - 1, roll_back(k + 1, b), roll_back(k, b))
-            total = total + jnp.where(lane == 0, roll_on(k - 1, b), roll_on(k, b))
-            terms.append(rhs[b, :, lane_tile(k)] - total)
-        return terms
-
-    return tile
-
-
-def sweep_kernel(
-    rhs, inverse, coupling, field, above, below, after, before, out, low, high, left, right
-):
-    for edge in (low, high):
-        edge[...] = jnp.zeros_like(edge)
-    terms = neighbour_terms(rhs, coupling, field, above, below, after, before)
-    for k in range(TILES):
-        values = product(inverse, terms(k), k)
-        for a in range(NVAR):
-            out[a, :, lane_tile(k)] = values[a]
-        store_edges(values, coupling, k, low, high, left, right)
-
-
-def last_kernel(rhs, inverse, coupling, field, above, below, after, before, grad, out, sens):
-    terms = neighbour_terms(rhs, coupling, field, above, below, after, before)
-    for k in range(TILES):
-        values = product(inverse, terms(k), k)
+            field_halo[b, :, lane_tile(k)] = halo_tile(above, below, b, NVAR + b, k)
+
+    def store(k, values):
         for a in range(NVAR):
             out[a, :, lane_tile(k)] = values[a]
         sens[:, lane_tile(k)] = grad[0, :, lane_tile(k)] * values[NVAR - 1]
 
-
-EDGES = (f32(8, CY), f32(8, CY), f32(CX, LANES), f32(CX, LANES))
+    two_sweeps(
+        dict(rhs=rhs, inverse=inverse, coupling=coupling),
+        dict(rhs=rhs_rim, inverse=inverse_rim, coupling=coupling_rim),
+        dict(rhs=rhs_halo, inverse=inverse_halo, coupling=coupling_halo),
+        field, field_halo, middle, TILES, store,
+    )
 
 
 def shifted(axis, size, step):
     return [(i, (i + step) % size) for i in range(size)]
 
 
-def exchange(low, high, left, right):
+def to_span_neighbours(low, high):
     above = lax.ppermute(low, "span", shifted("span", N_SPAN, -1))
     below = lax.ppermute(high, "span", shifted("span", N_SPAN, 1))
-    after = lax.ppermute(left, "dom", shifted("dom", N_DOM, -1))
-    before = lax.ppermute(right, "dom", shifted("dom", N_DOM, 1))
-    return above, below, after, before
+    return above, below
 
 
 def relax(rhs, inverse, coupling, grad):
-    whole = f32(NVAR, CX, CY)
-    field, *edges = pl.pallas_call(
-        first_kernel,
-        out_shape=(whole, *EDGES),
-        in_specs=[VMEM] * 3,
-        out_specs=[VMEM] * 5,
-        compiler_params=PARAMS,
-        name="first_product",
-    )(rhs, inverse, coupling)
-    for sweep in range(SWEEPS - 1):
-        field, *edges = pl.pallas_call(
-            sweep_kernel,
-            out_shape=(whole, *EDGES),
-            in_specs=[VMEM] * 8,
-            out_specs=[VMEM] * 5,
+    def call(kernel, name, shapes, scratch, *arrays):
+        return pl.pallas_call(
+            kernel,
+            out_shape=shapes,
+            in_specs=[VMEM] * len(arrays),
+            out_specs=[VMEM] * len(shapes),
+            scratch_shapes=scratch,
             compiler_params=PARAMS,
-            name="sweep",
-        )(rhs, inverse, coupling, field, *exchange(*edges))
-    return pl.pallas_call(
-        last_kernel,
-        out_shape=(whole, f32(CX, CY)),
-        in_specs=[VMEM] * 9,
-        out_specs=[VMEM] * 2,
-        compiler_params=PARAMS,
-        name="last_sweep",
-    )(rhs, inverse, coupling, field, *exchange(*edges), grad)
+            name=name,
+        )(*arrays)
+
+    rims = (f32(NVAR, CX, LANES), f32(NVAR, NVAR, CX, LANES), f32(4, CX, LANES))
+    halos = (f32(NVAR, 8, EXT), f32(NVAR, NVAR, 8, EXT), f32(4, 8, EXT))
+    scratch = [pltpu.VMEM((NVAR, 8, EXT), F32), pltpu.VMEM((NVAR, CX + 8, EXT), F32)]
+    first, last = pack_columns(inverse, rhs, coupling)
+    after = lax.ppermute(first, "dom", shifted("dom", N_DOM, -1))
+    before = lax.ppermute(last, "dom", shifted("dom", N_DOM, 1))
+    given = (rhs, inverse, coupling)
+    whole = f32(NVAR, CX, EXT)
+    *rim, field, low, high = call(
+        first_kernel, "first_product", (*rims, whole, f32(64, EXT), f32(64, EXT)), [],
+        *given, after, before,
+    )
+    above, below = to_span_neighbours(low, high)
+    *halo, field, low, high = call(
+        middle_kernel, "sweeps_1_2", (*halos, whole, f32(16, EXT), f32(16, EXT)), scratch,
+        *given, *rim, field, above, below,
+    )
+    above, below = to_span_neighbours(low, high)
+    return call(
+        last_kernel, "sweeps_3_4", (f32(NVAR, CX, CY), f32(CX, CY)), scratch,
+        *given, *rim, *halo, field, above, below, grad,
+    )
 
 
 def two_parts(value):

time: 106 us -> 88.8 us (0.84)
  starting transfers between devices: 31.2 us -> 20.1 us
  waiting for transfers between devices: 33.7 us -> 25.3 us
  Pallas kernels: 23 us -> 24.7 us
    ppermute x16 -> x6, starting transfers between devices: 19.7 us -> 11 us  [the longest x1 4.8 us: relax(): after = lax.ppermute(first, 'dom', shifted('dom', N_DOM, -1))]
    ppermute x16 -> x6, waiting for transfers between devices: 22.4 us -> 16.4 us  [the longest x2 5.17 us: to_span_neighbours(): below = lax.ppermute(high, 'span', shifted('span', N_SPAN, 1))]
    pallas_call x5 -> x4, Pallas kernels: 6.25 us -> 8.01 us  [the longest x3 7.57 us: call(): pl.pallas_call(kernel, out_shape=shapes, in_specs=[VMEM] * len(arrays), o...]
    ppermute x4, waiting for transfers between devices: 7.39 us -> 5.9 us  [shards(): lax.ppermute(part, ('span', 'dom'), to_node_owners(turn))]
    ppermute x3, starting transfers between devices: 4.77 us -> 3.39 us  [shards(): lax.ppermute(face_part, 'span', shifted('span', N_SPAN, turn))]
    unnamed x19 -> x21, local copies, waits for them, and re-layouts: 5.2 us -> 5.21 us
  transfers between devices with their start and end apart: 23 -> 13, of which waited for: 13 -> 11; matrix products, arithmetic and copies ran while one was open for 0% -> 0% of each run, Pallas kernels for 2% -> 2%
where the time goes in v3:
time: 88.8 us; the launch traced here: 88 us
  waiting for transfers between devices  25.3 us (28%)
  Pallas kernels  24.7 us (28%)
  starting transfers between devices  20.1 us (23%)
  blocking collectives  11.9 us (13%)
  local copies, waits for them, and re-layouts  5.21 us (6%)
    all_to_all x1, blocking collectives, shards(): lax.all_to_all(slot_vals, 'dom', split_axis=0, concat_axis=0, tiled=True)  11.9 us
    pallas_call x3, Pallas kernels, call(): pl.pallas_call(kernel, out_shape=shapes, in_specs=[VMEM] * len(arrays), o...  7.57 us
    pallas_call x1, Pallas kernels, gather(): pl.pallas_call(gather_kernel, out_shape=f32(SLOT_ROWS, LANES), in_specs=[...  6.25 us
    ppermute x4, waiting for transfers between devices, shards(): lax.ppermute(part, ('span', 'dom'), to_node_owners(turn))  5.9 us
    ppermute x4, starting transfers between devices, shards(): lax.ppermute(part, ('span', 'dom'), to_node_owners(turn))  5.69 us
    unnamed x21, local copies, waits for them, and re-layouts  5.21 us
    ppermute x2, waiting for transfers between devices, to_span_neighbours(): below = lax.ppermute(high, 'span', shifted('span', N_SPAN, 1))  5.17 us
    ppermute x1, waiting for transfers between devices, relax(): before = lax.ppermute(last, 'dom', shifted('dom', N_DOM, 1))  5.06 us
  transfers between devices with their start and end apart: 13, of which 11 were waited for; matrix products, arithmetic and copies ran while one was open for 0% of the time, Pallas kernels for 2%

profile of v3, /device:TPU:0, one launch (start us, length us, event | category | flops | bytes accessed | tf_op | source)
XLA Modules:
  0.0 88.0 jit_solution(9721430460105054157)
XLA Ops:
  0.6 0.0 copy-start
  0.6 2.3 %copy-done = f32[6,6,32,1024]{3,2,1,0:T(8,128)S(1)} copy-done((f32[6,6,32,1024]{3,2,1,0:T(8,128)S(1)}, f32[6,6,32,1024]{3,2,1,0:T(8,128)}, u32[]{:S(2)}) %copy-start) | copy-done | bytes 4718616
  3.0 1.1 %copy-done.1 = f32[6,32,1024]{2,1,0:T(8,128)S(1)} copy-done((f32[6,32,1024]{2,1,0:T(8,128)S(1)}, f32[6,32,1024]{2,1,0:T(8,128)}, u32[]{:S(2)}) %copy-start.1) | copy-done | bytes 786456
  4.1 1.0 %copy-done.2 = f32[4,32,1024]{2,1,0:T(8,128)S(1)} copy-done((f32[4,32,1024]{2,1,0:T(8,128)S(1)}, f32[4,32,1024]{2,1,0:T(8,128)}, u32[]{:S(2)}) %copy-start.2) | copy-done | bytes 524312
  5.1 0.4 pack_columns.1
  5.6 4.8 %collective-permute-start = (f32[2,32,128]{2,1,0:T(8,128)S(1)}, f32[2,32,128]{2,1,0:T(8,128)S(1)}, u32[]{:S(2)}, u32[]{:S(2)}) collective-permute-start(f32[2,32,128]{2,1,0:T(8,128)S(1)} %get-tuple-element.21), channel_id=1, source_target_pairs={{0,31},{1,0},{2,1},{3,2},{4,3},{5,4},{6,5},{7,6},{8,7},{9,8},{10,9... | collective-permute-start | bytes 98312 | tf_op jit(solution)/shard_map/ppermute | solution.py:290
  10.4 0.0 collective-permute-start.1
  10.4 1.6 %collective-permute-done.after = f32[2,32,128]{2,1,0:T(8,128)S(1)} collective-permute-done((f32[2,32,128]{2,1,0:T(8,128)S(1)}, f32[2,32,128]{2,1,0:T(8,128)S(1)}, u32[]{:S(2)}, u32[]{:S(2)}) %collective-permute-start) | collective-permute-done | bytes 32800 | tf_op jit(solution)/shard_map/ppermute | solution.py:290
  12.0 5.1 %collective-permute-done.1.before = f32[2,32,128]{2,1,0:T(8,128)S(1)} collective-permute-done((f32[2,32,128]{2,1,0:T(8,128)S(1)}, f32[2,32,128]{2,1,0:T(8,128)S(1)}, u32[]{:S(2)}, u32[]{:S(2)}) %collective-permute-start.1) | collective-permute-done | bytes 32800 | tf_op jit(solution)/shard_map/ppermute | solution.py:291
  17.0 1.2 %first_product.1 = (f32[6,32,128]{2,1,0:T(8,128)S(1)}, f32[6,6,32,128]{3,2,1,0:T(8,128)S(1)}, f32[4,32,128]{2,1,0:T(8,128)S(1)}, f32[6,32,1152]{2,1,0:T(8,128)S(...) custom-call(f32[6,32,1024]{2,1,0:T(8,128)S(1)} %copy-done.1, f32[6,6,32,1024]{3,2,1,0:T(8,128)S(1)} %copy-done, ...), custom_call_target="tpu_custom_call" | custom-call | tf_op jit(solution)/shard_map/first_product/pallas_call | solution.py:276
  18.3 0.0 copy-start.3
  18.3 0.0 slice-start
  18.3 0.0 copy-start.6
  18.3 4.1 %collective-permute-start.2 = (f32[64,1152]{1,0:T(8,128)S(1)}, f32[64,1152]{1,0:T(8,128)S(1)}, u32[]{:S(2)}, u32[]{:S(2)}) collective-permute-start(f32[64,1152]{1,0:T(8,128)S(1)} %get-tuple-element.27), channel_id=1, source_target_pairs={{0,96},{32,0},{64,32},{96,64},{1,97},{33,1},{65,33},{97,65},{2,98}... | collective-permute-start | bytes 884744 | tf_op jit(solution)/shard_map/ppermute | solution.py:269
  22.4 0.0 collective-permute-start.3
  22.4 4.2 %collective-permute-done.2.above = f32[64,1152]{1,0:T(8,128)S(1)} collective-permute-done((f32[64,1152]{1,0:T(8,128)S(1)}, f32[64,1152]{1,0:T(8,128)S(1)}, u32[]{:S(2)}, u32[]{:S(2)}) %collective-permute-start.2) | collective-permute-done | bytes 294944 | tf_op jit(solution)/shard_map/ppermute | solution.py:269
  26.7 3.7 %collective-permute-done.3.below = f32[64,1152]{1,0:T(8,128)S(1)} collective-permute-done((f32[64,1152]{1,0:T(8,128)S(1)}, f32[64,1152]{1,0:T(8,128)S(1)}, u32[]{:S(2)}, u32[]{:S(2)}) %collective-permute-start.3) | collective-permute-done | bytes 294944 | tf_op jit(solution)/shard_map/ppermute | solution.py:270
  30.4 2.8 %sweeps_1_2.1 = (f32[6,8,1152]{2,1,0:T(8,128)S(1)}, f32[6,6,8,1152]{3,2,1,0:T(8,128)S(1)}, f32[4,8,1152]{2,1,0:T(8,128)S(1)}, f32[6,32,1152]{2,1,0:T(8,128)S(1)}...) custom-call(f32[6,32,1024]{2,1,0:T(8,128)S(1)} %copy-done.1, f32[6,6,32,1024]{3,2,1,0:T(8,128)S(1)} %copy-done, ...), custom_call_target="tpu_custom_call" | custom-call | tf_op jit(solution)/shard_map/sweeps_1_2/pallas_call | solution.py:276
  33.2 0.1 collective-permute-start.4
  33.3 2.0 %collective-permute-start.5 = (f32[16,1152]{1,0:T(8,128)S(1)}, f32[16,1152]{1,0:T(8,128)S(1)}, u32[]{:S(2)}, u32[]{:S(2)}) collective-permute-start(f32[16,1152]{1,0:T(8,128)S(1)} %get-tuple-element.34), channel_id=1, source_target_pairs={{0,32},{32,64},{64,96},{96,0},{1,33},{33,65},{65,97},{97,1},{2,34}... | collective-permute-start | bytes 221192 | tf_op jit(solution)/shard_map/ppermute | solution.py:270
  35.3 0.0 copy-done.3
  35.3 2.0 %live_rows.1.live = s32[8,384]{1,0:T(8,128)S(1)} custom-call(s32[512,128]{1,0:T(8,128)S(1)} %bitcast.13), custom_call_target="tpu_custom_call" | custom-call | tf_op jit(solution)/shard_map/live_rows/pallas_call | solution.py:368
  37.3 0.3 collective-permute-done.4.above
  37.6 1.5 %collective-permute-done.5.below = f32[16,1152]{1,0:T(8,128)S(1)} collective-permute-done((f32[16,1152]{1,0:T(8,128)S(1)}, f32[16,1152]{1,0:T(8,128)S(1)}, u32[]{:S(2)}, u32[]{:S(2)}) %collective-permute-start.5) | collective-permute-done | bytes 73760 | tf_op jit(solution)/shard_map/ppermute | solution.py:270
  39.1 0.0 slice-done.1
  39.1 0.0 copy-start.5
  39.1 0.0 copy-start.4
  39.1 0.0 copy-start.7
  39.1 3.5 %sweeps_3_4.1 = (f32[6,32,1024]{2,1,0:T(8,128)}, f32[32,1024]{1,0:T(8,128)S(1)}) custom-call(f32[6,32,1024]{2,1,0:T(8,128)S(1)} %copy-done.1, f32[6,6,32,1024]{3,2,1,0:T(8,128)S(1)} %bitcast.11, f32[4,32,1024]{2,1,0:T(8,128)S(1)} %copy-done.2, f32[6,32,128]{2,1,0:T(8,128)S(1)} %get-tuple-element.23.rhs_rim, ...), custom_call_target="tpu_custom_call" | custom-call | tf_op jit(solution)/shard_map/sweeps_3_4/pallas_call | solution.py:276
  42.7 6.2 %gather_slots.1 = f32[512,128]{1,0:T(8,128)S(1)} custom-call(s32[8,384]{1,0:T(8,128)S(1)} %live_rows.1.live, f32[32,1024]{1,0:T(8,128)S(1)} %get-tuple-element.36.sens, s32[512,128]{1,0:T(8,128)S(1)} %bitcast.14), custom_call_target="tpu_custom_call" | custom-call | tf_op jit(solution)/shard_map/gather_slots/pallas_call | solution.py:403
  48.9 11.9 %all_to_all.11 = f32[32,16,128]{2,1,0:T(8,128)S(1)} all-to-all(f32[32,16,128]{2,1,0:T(8,128)S(1)} %bitcast.15), channel_id=1, replica_groups=mesh['span'=4,'dom'=32] {'dom'}, dimensions={0} | all-to-all | bytes 524288 | tf_op jit(solution)/shard_map/all_to_all | solution.py:501
  60.8 4.8 %face_sums.1.part0 = f32[64,128]{1,0:T(8,128)S(1)} custom-call(f32[512,128]{1,0:T(8,128)S(1)} %bitcast.12, s32[512,128]{1,0:T(8,128)S(1)} %bitcast.16), custom_call_target="tpu_custom_call" | custom-call | tf_op jit(solution)/shard_map/face_sums/pallas_call | solution.py:434
  65.6 0.6 collective-permute-start.6
  66.2 0.7 collective-permute-start.7
  66.9 2.1 %collective-permute-start.8 = (f32[64,128]{1,0:T(8,128)S(1)}, f32[64,128]{1,0:T(8,128)S(1)}, u32[]{:S(2)}, u32[]{:S(2)}) collective-permute-start(f32[64,128]{1,0:T(8,128)S(1)} %face_sums.1.part0), channel_id=1, source_target_pairs={{0,96},{32,0},{64,32},{96,64},{1,97},{33,1},{65,33},{97,65},{2,98}... | collective-permute-start | bytes 98312 | tf_op jit(solution)/shard_map/ppermute | solution.py:504
  69.0 2.0 %collective-permute-done.6.part1 = f32[64,128]{1,0:T(8,128)S(1)} collective-permute-done((f32[64,128]{1,0:T(8,128)S(1)}, f32[64,128]{1,0:T(8,128)S(1)}, u32[]{:S(2)}, u32[]{:S(2)}) %collective-permute-start.6) | collective-permute-done | bytes 32800 | tf_op jit(solution)/shard_map/ppermute | solution.py:504
  71.0 0.6 collective-permute-done.7.part2
  71.6 0.4 collective-permute-done.8.part3
  72.0 3.7 %node_sums.1 = (f32[64,128]{1,0:T(8,128)}, f32[3,32,128]{2,1,0:T(8,128)S(1)}) custom-call(f32[64,128]{1,0:T(8,128)S(1)} %face_sums.1.part0, f32[64,128]{1,0:T(8,128)S(1)} %collective-permute-done.6.part1, f32[64,128]{1,0:T(8,128)S(1)} %collective-permute-done.7.part2, f32[64,128]{1,0:T(8,128)S(1)} %collective-permute-done.8.part3, ...), custom_call_target="tpu_custom_call" | custom-call | tf_op jit(solution)/shard_map/node_sums/pallas_call | solution.py:475
  75.7 1.8 %collective-permute-start.10 = (f32[3,32,128]{2,1,0:T(8,128)S(1)}, f32[3,32,128]{2,1,0:T(8,128)S(1)}, u32[]{:S(2)}, u32[]{:S(2)}) collective-permute-start(f32[3,32,128]{2,1,0:T(8,128)S(1)} %get-tuple-element.38), channel_id=1, source_target_pairs={{0,32},{1,33},{2,34},{3,35},{4,36},{5,37},{6,38},{7,39},{8,40},{9,... | collective-permute-start | bytes 147464 | tf_op jit(solution)/shard_map/ppermute | solution.py:508
  77.4 2.1 %collective-permute-start.11 = (f32[3,32,128]{2,1,0:T(8,128)S(1)}, f32[3,32,128]{2,1,0:T(8,128)S(1)}, u32[]{:S(2)}, u32[]{:S(2)}) collective-permute-start(f32[3,32,128]{2,1,0:T(8,128)S(1)} %get-tuple-element.38), channel_id=1, source_target_pairs={{0,64},{1,65},{2,66},{3,67},{4,68},{5,69},{6,70},{7,71},{8,72},{9,... | collective-permute-start | bytes 147464 | tf_op jit(solution)/shard_map/ppermute | solution.py:508
  79.5 1.2 %collective-permute-start.12 = (f32[3,32,128]{2,1,0:T(8,128)S(1)}, f32[3,32,128]{2,1,0:T(8,128)S(1)}, u32[]{:S(2)}, u32[]{:S(2)}) collective-permute-start(f32[3,32,128]{2,1,0:T(8,128)S(1)} %get-tuple-element.38), channel_id=1, source_target_pairs={{0,96},{1,97},{2,98},{3,99},{4,100},{5,101},{6,102},{7,103},{8,104... | collective-permute-start | bytes 147464 | tf_op jit(solution)/shard_map/ppermute | solution.py:508
  80.7 0.7 collective-permute-start.9
  81.4 2.4 %collective-permute-done.10 = f32[3,32,128]{2,1,0:T(8,128)S(1)} collective-permute-done((f32[3,32,128]{2,1,0:T(8,128)S(1)}, f32[3,32,128]{2,1,0:T(8,128)S(1)}, u32[]{:S(2)}, u32[]{:S(2)}) %collective-permute-start.10) | collective-permute-done | bytes 49184 | tf_op jit(solution)/shard_map/ppermute | solution.py:508
  83.8 0.0 collective-permute-done.11
  83.8 3.5 %collective-permute-done.12 = f32[3,32,128]{2,1,0:T(8,128)S(1)} collective-permute-done((f32[3,32,128]{2,1,0:T(8,128)S(1)}, f32[3,32,128]{2,1,0:T(8,128)S(1)}, u32[]{:S(2)}, u32[]{:S(2)}) %collective-permute-start.12) | collective-permute-done | bytes 49184 | tf_op jit(solution)/shard_map/ppermute | solution.py:508
  87.3 0.0 collective-permute-done.9
  87.3 0.7 copy.13
  (10 shorter events, 0.0 us)
Async XLA Ops:
  0.6 2.3 %copy-start = (f32[6,6,32,1024]{3,2,1,0:T(8,128)S(1)}, f32[6,6,32,1024]{3,2,1,0:T(8,128)}, u32[]{:S(2)}) copy-start(f32[6,6,32,1024]{3,2,1,0:T(8,128)} %inverse.5) | copy-start | bytes 14155780
  3.0 1.1 %copy-start.1 = (f32[6,32,1024]{2,1,0:T(8,128)S(1)}, f32[6,32,1024]{2,1,0:T(8,128)}, u32[]{:S(2)}) copy-start(f32[6,32,1024]{2,1,0:T(8,128)} %rhs.5) | copy-start | bytes 2359300
  4.1 1.0 %copy-start.2 = (f32[4,32,1024]{2,1,0:T(8,128)S(1)}, f32[4,32,1024]{2,1,0:T(8,128)}, u32[]{:S(2)}) copy-start(f32[4,32,1024]{2,1,0:T(8,128)} %coupling.5) | copy-start | bytes 1572868
  5.6 6.4 %collective-permute-start = (f32[2,32,128]{2,1,0:T(8,128)S(1)}, f32[2,32,128]{2,1,0:T(8,128)S(1)}, u32[]{:S(2)}, u32[]{:S(2)}) collective-permute-start(f32[2,32,128]{2,1,0:T(8,128)S(1)} %get-tuple-element.21), channel_id=1, source_target_pairs={{0,31},{1,0},{2,1},{3,2},{4,3},{5,4},{6,5},{7,6},{8,7},{9,8},{10,9... | collective-permute-start | bytes 98312 | tf_op jit(solution)/shard_map/ppermute | solution.py:290
  10.4 6.7 %collective-permute-start.1 = (f32[2,32,128]{2,1,0:T(8,128)S(1)}, f32[2,32,128]{2,1,0:T(8,128)S(1)}, u32[]{:S(2)}, u32[]{:S(2)}) collective-permute-start(f32[2,32,128]{2,1,0:T(8,128)S(1)} %get-tuple-element.22), channel_id=1, source_target_pairs={{0,1},{1,2},{2,3},{3,4},{4,5},{5,6},{6,7},{7,8},{8,9},{9,10},{10,1... | collective-permute-start | bytes 98312 | tf_op jit(solution)/shard_map/ppermute | solution.py:291
  18.3 17.0 %copy-start.3 = (s32[1,1,65536]{2,1,0:T(1,128)S(1)}, s32[1,1,65536]{2,1,0:T(1,128)}, u32[]{:S(2)}) copy-start(s32[1,1,65536]{2,1,0:T(1,128)} %param.12) | copy-start | bytes 786436
  18.3 20.8 %slice-start = ((s8[4718592]{0:T(1024)(128)(4,1)}), s8[4194304]{0:T(1024)(128)(4,1)S(1)}, s32[]{:S(2)}) async-start(s8[4718592]{0:T(1024)(128)(4,1)} %bitcast.10), calls=%async_computation.1 | async-start | bytes 8388608
  18.3 20.8 %copy-start.6 = (f32[1,32,1024]{2,1,0:T(8,128)S(1)}, f32[1,32,1024]{2,1,0:T(8,128)}, u32[]{:S(2)}) copy-start(f32[1,32,1024]{2,1,0:T(8,128)} %grad.2) | copy-start | bytes 393220
  18.3 8.3 %collective-permute-start.2 = (f32[64,1152]{1,0:T(8,128)S(1)}, f32[64,1152]{1,0:T(8,128)S(1)}, u32[]{:S(2)}, u32[]{:S(2)}) collective-permute-start(f32[64,1152]{1,0:T(8,128)S(1)} %get-tuple-element.27), channel_id=1, source_target_pairs={{0,96},{32,0},{64,32},{96,64},{1,97},{33,1},{65,33},{97,65},{2,98}... | collective-permute-start | bytes 884744 | tf_op jit(solution)/shard_map/ppermute | solution.py:269
  22.4 7.9 %collective-permute-start.3 = (f32[64,1152]{1,0:T(8,128)S(1)}, f32[64,1152]{1,0:T(8,128)S(1)}, u32[]{:S(2)}, u32[]{:S(2)}) collective-permute-start(f32[64,1152]{1,0:T(8,128)S(1)} %get-tuple-element.28), channel_id=1, source_target_pairs={{0,32},{32,64},{64,96},{96,0},{1,33},{33,65},{65,97},{97,1},{2,34}... | collective-permute-start | bytes 884744 | tf_op jit(solution)/shard_map/ppermute | solution.py:270
  30.4 8.7 %slice-start.1 = ((s8[4718592]{0:T(1024)(128)(4,1)}), s8[524288]{0:T(1024)(128)(4,1)S(1)}, s32[]{:S(2)}) async-start(s8[4718592]{0:T(1024)(128)(4,1)} %bitcast.10), calls=%async_computation.2 | async-start | bytes 1048576
  33.2 4.4 %collective-permute-start.4 = (f32[16,1152]{1,0:T(8,128)S(1)}, f32[16,1152]{1,0:T(8,128)S(1)}, u32[]{:S(2)}, u32[]{:S(2)}) collective-permute-start(f32[16,1152]{1,0:T(8,128)S(1)} %get-tuple-element.33), channel_id=1, source_target_pairs={{0,96},{32,0},{64,32},{96,64},{1,97},{33,1},{65,33},{97,65},{2,98}... | collective-permute-start | bytes 221192 | tf_op jit(solution)/shard_map/ppermute | solution.py:269
  33.3 5.8 %collective-permute-start.5 = (f32[16,1152]{1,0:T(8,128)S(1)}, f32[16,1152]{1,0:T(8,128)S(1)}, u32[]{:S(2)}, u32[]{:S(2)}) collective-permute-start(f32[16,1152]{1,0:T(8,128)S(1)} %get-tuple-element.34), channel_id=1, source_target_pairs={{0,32},{32,64},{64,96},{96,0},{1,33},{33,65},{65,97},{97,1},{2,34}... | collective-permute-start | bytes 221192 | tf_op jit(solution)/shard_map/ppermute | solution.py:270
  39.1 21.7 %copy-start.5 = (s32[1,1,65536]{2,1,0:T(1,128)S(1)}, s32[1,1,65536]{2,1,0:T(1,128)}, u32[]{:S(2)}) copy-start(s32[1,1,65536]{2,1,0:T(1,128)} %param.13) | copy-start | bytes 786436
  39.1 32.9 %copy-start.4 = (f32[3,4,8192]{2,1,0:T(4,128)S(1)}, f32[3,4,8192]{2,1,0:T(4,128)}, u32[]{:S(2)}) copy-start(f32[3,4,8192]{2,1,0:T(4,128)} %grad.3) | copy-start | bytes 1179652
  39.1 32.9 %copy-start.7 = (s32[4,8192]{1,0:T(4,128)S(1)}, s32[4,8192]{1,0:T(4,128)}, u32[]{:S(2)}) copy-start(s32[4,8192]{1,0:T(4,128)} %nodes.1) | copy-start | bytes 393220
  65.6 5.4 %collective-permute-start.6 = (f32[64,128]{1,0:T(8,128)S(1)}, f32[64,128]{1,0:T(8,128)S(1)}, u32[]{:S(2)}, u32[]{:S(2)}) collective-permute-start(f32[64,128]{1,0:T(8,128)S(1)} %face_sums.1.part0), channel_id=1, source_target_pairs={{0,32},{32,64},{64,96},{96,0},{1,33},{33,65},{65,97},{97,1},{2,34}... | collective-permute-start | bytes 98312 | tf_op jit(solution)/shard_map/ppermute | solution.py:504
  66.2 5.4 %collective-permute-start.7 = (f32[64,128]{1,0:T(8,128)S(1)}, f32[64,128]{1,0:T(8,128)S(1)}, u32[]{:S(2)}, u32[]{:S(2)}) collective-permute-start(f32[64,128]{1,0:T(8,128)S(1)} %face_sums.1.part0), channel_id=1, source_target_pairs={{0,64},{32,96},{64,0},{96,32},{1,65},{33,97},{65,1},{97,33},{2,66}... | collective-permute-start | bytes 98312 | tf_op jit(solution)/shard_map/ppermute | solution.py:504
  66.9 5.1 %collective-permute-start.8 = (f32[64,128]{1,0:T(8,128)S(1)}, f32[64,128]{1,0:T(8,128)S(1)}, u32[]{:S(2)}, u32[]{:S(2)}) collective-permute-start(f32[64,128]{1,0:T(8,128)S(1)} %face_sums.1.part0), channel_id=1, source_target_pairs={{0,96},{32,0},{64,32},{96,64},{1,97},{33,1},{65,33},{97,65},{2,98}... | collective-permute-start | bytes 98312 | tf_op jit(solution)/shard_map/ppermute | solution.py:504
  75.7 8.1 %collective-permute-start.10 = (f32[3,32,128]{2,1,0:T(8,128)S(1)}, f32[3,32,128]{2,1,0:T(8,128)S(1)}, u32[]{:S(2)}, u32[]{:S(2)}) collective-permute-start(f32[3,32,128]{2,1,0:T(8,128)S(1)} %get-tuple-element.38), channel_id=1, source_target_pairs={{0,32},{1,33},{2,34},{3,35},{4,36},{5,37},{6,38},{7,39},{8,40},{9,... | collective-permute-start | bytes 147464 | tf_op jit(solution)/shard_map/ppermute | solution.py:508
  77.4 6.3 %collective-permute-start.11 = (f32[3,32,128]{2,1,0:T(8,128)S(1)}, f32[3,32,128]{2,1,0:T(8,128)S(1)}, u32[]{:S(2)}, u32[]{:S(2)}) collective-permute-start(f32[3,32,128]{2,1,0:T(8,128)S(1)} %get-tuple-element.38), channel_id=1, source_target_pairs={{0,64},{1,65},{2,66},{3,67},{4,68},{5,69},{6,70},{7,71},{8,72},{9,... | collective-permute-start | bytes 147464 | tf_op jit(solution)/shard_map/ppermute | solution.py:508
  79.5 7.7 %collective-permute-start.12 = (f32[3,32,128]{2,1,0:T(8,128)S(1)}, f32[3,32,128]{2,1,0:T(8,128)S(1)}, u32[]{:S(2)}, u32[]{:S(2)}) collective-permute-start(f32[3,32,128]{2,1,0:T(8,128)S(1)} %get-tuple-element.38), channel_id=1, source_target_pairs={{0,96},{1,97},{2,98},{3,99},{4,100},{5,101},{6,102},{7,103},{8,104... | collective-permute-start | bytes 147464 | tf_op jit(solution)/shard_map/ppermute | solution.py:508
  80.7 6.6 %collective-permute-start.9 = (f32[3,32,128]{2,1,0:T(8,128)S(1)}, f32[3,32,128]{2,1,0:T(8,128)S(1)}, u32[]{:S(2)}, u32[]{:S(2)}) collective-permute-start(f32[3,32,128]{2,1,0:T(8,128)S(1)} %get-tuple-element.38), channel_id=1, source_target_pairs={{0,0},{1,1},{2,2},{3,3},{4,4},{5,5},{6,6},{7,7},{8,8},{9,9},{10,10... | collective-permute-start | bytes 147464 | tf_op jit(solution)/shard_map/ppermute | solution.py:508

commit v4 on v3

--- a/solution.py
+++ b/solution.py
@@ -25,7 +25,11 @@
 PACKED = 2
 AT_RHS = NVAR * NVAR
 AT_COUPLING = AT_RHS + NVAR
-AT_FIELD = AT_COUPLING + 8
+GIVEN_ROWS = AT_COUPLING + 8
+RAW_ROWS = 56
+AT_RIM = 2 * NVAR * (TILES + 1)
+FIELD_ROWS = 112
+FIRST_ROWS = 160
 SLOT_ROWS = N_DOM * CAP // LANES
 LIVE_ROWS = CELLS // LANES + N_DOM
 LIVE_PAD = 384
@@ -37,6 +41,7 @@
 
 VMEM = pl.BlockSpec(memory_space=pltpu.VMEM)
 SMEM = pl.BlockSpec(memory_space=pltpu.SMEM)
+ANY = pl.BlockSpec(memory_space=pl.ANY)
 PARAMS = pltpu.CompilerParams(vmem_limit_bytes=40 << 20)
 BF = jnp.bfloat16
 F32 = jnp.float32
@@ -50,9 +55,9 @@
     return slice(k * LANES, (k + 1) * LANES)
 
 
-def product(inverse, terms):
+def product(inverse, terms, variables=range(NVAR)):
     out = []
-    for a in range(NVAR):
+    for a in variables:
         total = inverse(0, a) * terms[0]
         for b in range(1, NVAR):
             total = total + inverse(b, a) * terms[b]
@@ -60,14 +65,23 @@
     return out
 
 
-def pack_kernel(
-    inverse0, rhs0, coupling0, inverse7, rhs7, coupling7, first, last
-):
+def pack_kernel(rhs, inverse, coupling, first, last, low, high, *scratch):
+    blocks, done = scratch[:-1], scratch[-1]
+    ends = [(slice(None), lane_tile(k)) for k in (0, TILES - 1)]
+    ends += [(slice(row, row + 8), slice(None)) for row in (0, CX - 8)]
+    copies = []
+    for end, place in enumerate(ends):
+        for i, source in enumerate((inverse, rhs, coupling)):
+            at = (slice(None),) * (len(source.shape) - 2) + place
+            n = end * 3 + i
+            copies.append(pltpu.make_async_copy(source.at[at], blocks[n], done.at[n]))
+    for copy in copies:
+        copy.start()
     group = lax.broadcasted_iota(jnp.int32, (CX, LANES), 1) // WIDE
-    for inverse, rhs, coupling, start, out in (
-        (inverse0, rhs0, coupling0, 0, first),
-        (inverse7, rhs7, coupling7, LANES - WIDE, last),
-    ):
+    for end, (out, start) in enumerate(((first, 0), (last, LANES - WIDE))):
+        for copy in copies[end * 3 : end * 3 + 3]:
+            copy.wait()
+        inverse, rhs, coupling = blocks[end * 3 : end * 3 + 3]
         given = [inverse[b, a] for b in range(NVAR) for a in range(NVAR)]
         given += [rhs[b] for b in range(NVAR)] + [coupling[i] for i in range(4)]
         for t in range(PACKED):
@@ -76,30 +90,45 @@
                 moved = pltpu.roll(value, (q * WIDE - start) % LANES, 1)
                 total = jnp.where(group == q, moved, total)
             out[t] = total
-
-
-def pack_columns(inverse, rhs, coupling):
-    def specs(k):
-        return [
-            pl.BlockSpec((NVAR, NVAR, CX, LANES), lambda i: (0, 0, 0, k)),
-            pl.BlockSpec((NVAR, CX, LANES), lambda i: (0, 0, k)),
-            pl.BlockSpec((4, CX, LANES), lambda i: (0, 0, k)),
-        ]
-
-    return pl.pallas_call(
-        pack_kernel,
-        grid=(1,),
-        out_shape=(f32(PACKED, CX, LANES),) * 2,
-        in_specs=specs(0) + specs(TILES - 1),
-        out_specs=[pl.BlockSpec((PACKED, CX, LANES), lambda i: (0, 0, 0))] * 2,
-        compiler_params=PARAMS,
-        name="pack_columns",
-    )(inverse, rhs, coupling, inverse, rhs, coupling)
-
-
-def first_kernel(
-    rhs, inverse, coupling, after, before, rhs_rim, inverse_rim, coupling_rim, out, low, high
-):
+    for end, (out, near, second) in enumerate(((low, 0, 1), (high, 7, 6))):
+        for copy in copies[6 + end * 3 : 9 + end * 3]:
+            copy.wait()
+        parts = blocks[6 + end * 3 : 9 + end * 3]
+        out[GIVEN_ROWS:] = jnp.zeros((RAW_ROWS - GIVEN_ROWS, CY), F32)
+        for at, (i, index, row) in enumerate(given_rows(near, second)):
+            out[at : at + 1, :] = parts[i][(*index, slice(row, row + 1), slice(None))]
+
+
+def load_kernel(rhs, inverse, coupling, packed, rhs_own, inverse_own, coupling_own, field, done):
+    arrays = ((inverse, inverse_own), (rhs, rhs_own), (coupling, coupling_own))
+    groups = [slice(row, row + 8) for row in range(0, CX, 8)]
+    copies = []
+    for g, rows in enumerate(groups):
+        for i, (source, own) in enumerate(arrays):
+            at = (slice(None),) * (len(source.shape) - 2) + (rows, slice(None))
+            copies.append(pltpu.make_async_copy(source.at[at], own.at[at], done.at[g * 3 + i]))
+    for copy in copies:
+        copy.start()
+    for g, rows in enumerate(groups):
+        for copy in copies[g * 3 : g * 3 + 3]:
+            copy.wait()
+        for k in range(TILES):
+            at = lane_tile(k)
+            values = product(
+                lambda b, a: inverse_own[b, a, rows, at],
+                [rhs_own[b, rows, at] for b in range(NVAR)],
+            )
+            for a in range(NVAR):
+                field[a, rows, at] = values[a]
+
+
+def given_rows(near, second):
+    rows = [(0, (b, a), near) for b in range(NVAR) for a in range(NVAR)]
+    rows += [(1, (b,), near) for b in range(NVAR)]
+    return rows + [(2, (i,), row) for row in (near, second) for i in range(4)]
+
+
+def rim_kernel(field, after, before, rhs_rim, inverse_rim, coupling_rim, field_rim, low, high):
     lane = lax.broadcasted_iota(jnp.int32, (CX, LANES), 1)
     for v in range(GIVEN):
         t, q = divmod(v, PER_TILE)
@@ -112,60 +141,58 @@
             rhs_rim[v - NVAR * NVAR] = value
         else:
             coupling_rim[v - NVAR * (NVAR + 1)] = value
-
-    for k in range(TILES + 1):
-        at = lane_tile(k)
-        if k < TILES:
-            terms = [rhs[b, :, at] for b in range(NVAR)]
-            values = product(lambda b, a: inverse[b, a, :, at], terms)
-        else:
-            terms = [rhs_rim[b] for b in range(NVAR)]
-            values = product(lambda b, a: inverse_rim[b, a], terms)
-        for a in range(NVAR):
-            out[a, :, at] = values[a]
+    values = product(lambda b, a: inverse_rim[b, a], [rhs_rim[b] for b in range(NVAR)])
+    for a in range(NVAR):
+        field_rim[a] = values[a]
+
+    def pick(b, row, k):
+        return field_rim[b, row, :] if k == TILES else field[b, row, lane_tile(k)]
 
     for message, near, second in ((low, 0, 1), (high, CX - 1, CX - 2)):
-        message[...] = jnp.zeros_like(message)
-        for part, rim, at, rows in (
-            (inverse, inverse_rim, 0, (near,)),
-            (rhs, rhs_rim, AT_RHS, (near,)),
-            (coupling, coupling_rim, AT_COUPLING, (near, second)),
-        ):
-            shape = rim.shape[:-2]
-            for row in rows:
-                for index in np.ndindex(*shape):
-                    message[at : at + 1, :CY] = part[(*index, slice(row, row + 1), slice(None))]
-                    message[at : at + 1, CY:] = rim[(*index, slice(row, row + 1), slice(None))]
-                    at += 1
-        field_rows(message, AT_FIELD, out, near, second)
-
-
-def field_rows(message, at, field, near, second):
-    for row in (near, second):
+        field_rows(message, pick, near, second)
+        parts = (inverse_rim, rhs_rim, coupling_rim)
+        at = AT_RIM
+        for i, index, row in given_rows(near, second):
+            message[at : at + 1, :] = parts[i][(*index, slice(row, row + 1), slice(None))]
+            at += 1
+        message[at:] = jnp.zeros((FIRST_ROWS - at, LANES), F32)
+
+
+def field_rows(message, pick, near, second):
+    for i, row in enumerate((near, second)):
         for b in range(NVAR):
-            message[at : at + 1, :] = field[b, row : row + 1, :]
-            at += 1
-
-
-def halo_tile(above, below, at, second_at, k):
+            for k in range(TILES + 1):
+                at = field_row(i, b, k)
+                message[at : at + 1, :] = pick(b, slice(row, row + 1), k)
+
+
+def field_row(i, b, k):
+    return (i * NVAR + b) * (TILES + 1) + k
+
+
+def halo_tile(sides, near, second=None):
     span = lax.axis_index("span")
     row = lax.broadcasted_iota(jnp.int32, (8, LANES), 0)
     tile = jnp.zeros((8, LANES), F32)
-    for source, end, places in ((above, N_SPAN - 1, (0, 1)), (below, 0, (7, 6))):
+    for side, end, places in zip(sides, (N_SPAN - 1, 0), ((0, 1), (7, 6))):
         part = jnp.zeros((8, LANES), F32)
-        for place, index in zip(places, (at, second_at)):
-            if index is not None:
-                part = jnp.where(row == place, source[index : index + 1, lane_tile(k)], part)
+        for place, pick in zip(places, (near, second)):
+            if pick is not None:
+                part = jnp.where(row == place, pick(side), part)
         tile = tile + jnp.where(span == end, 0.0, part)
     return tile
 
 
-def with_halo(main, rim, halo, index, k):
-    core = rim[index] if k == TILES else main[(*index, slice(None), lane_tile(k))]
-    return jnp.concatenate([core, halo(index, k)], axis=0)
-
-
-def sweep(rows, tiles, rhs, inverse, coupling, field, store):
+def field_halo_tiles(field_halo, above, below):
+    for k in range(TILES + 1):
+        for b in range(NVAR):
+            picks = [
+                lambda side, at=field_row(i, b, k): side[at : at + 1, :] for i in range(2)
+            ]
+            field_halo[b, :, lane_tile(k)] = halo_tile((above, below), *picks)
+
+
+def sweep(rows, tiles, rhs, inverse, coupling, field, store, variables=range(NVAR)):
     last = TILES + 1
     lane = lax.broadcasted_iota(jnp.int32, (rows, LANES), 1)
     rolled = {}
@@ -188,77 +215,112 @@
             total = total + jnp.where(edge, shifted_lanes(k + 1, b, 0), shifted_lanes(k, b, 0))
             total = total + jnp.where(lane == 0, shifted_lanes(k - 1, b, 1), shifted_lanes(k, b, 1))
             terms.append(rhs((b,), k)[:rows] - total)
-        store(k, product(lambda b, a: inverse((b, a), k)[:rows], terms))
-
-
-def two_sweeps(given, rims, halos, field, field_halo, middle, tiles, store):
-    def full(name):
-        return lambda index, k: with_halo(
-            given[name], rims[name], lambda i, t: halos[name][(*i, slice(None), lane_tile(t))], index, k
-        )
-
-    rhs, inverse, coupling = full("rhs"), full("inverse"), full("coupling")
-
+        store(k, product(lambda b, a: inverse((b, a), k)[:rows], terms, variables))
+
+
+def with_halos(given, rims, halos):
+    def full(main, rim, halo):
+        def tiles(index, k):
+            edge = halo[(*index, slice(None), lane_tile(k))]
+            core = rim[index] if k == TILES else main[(*index, slice(None), lane_tile(k))]
+            return jnp.concatenate([core, edge], axis=0)
+
+        return tiles
+
+    return [full(*three) for three in zip(given, rims, halos)]
+
+
+def odd_sweep(arrays, field, field_halo, middle):
     def before(index, k):
         (b,) = index
-        return jnp.concatenate([field[b, :, lane_tile(k)], field_halo[b, :, lane_tile(k)]], axis=0)
+        return jnp.concatenate([field(b, k), field_halo[b, :, lane_tile(k)]], axis=0)
 
     def keep(k, values):
         for a in range(NVAR):
             middle[a, :, lane_tile(k)] = values[a]
 
-    sweep(CX + 8, TILES + 1, rhs, inverse, coupling, before, keep)
-    sweep(CX, tiles, rhs, inverse, coupling, lambda i, k: middle[i[0], :, lane_tile(k)], store)
+    sweep(CX + 8, TILES + 1, *arrays, before, keep)
+
+
+def even_sweep(tiles, arrays, middle, store, variables=range(NVAR)):
+    field = lambda index, k: middle[index[0], :, lane_tile(k)]
+    sweep(CX, tiles, *arrays, field, store, variables)
 
 
 def middle_kernel(
-    rhs, inverse, coupling, rhs_rim, inverse_rim, coupling_rim, field, above, below,
-    rhs_halo, inverse_halo, coupling_halo, out, low, high, field_halo, middle,
+    rhs, inverse, coupling, rhs_rim, inverse_rim, coupling_rim, field_rim, field, raw_above,
+    raw_below, above, below, rhs_halo, inverse_halo, coupling_halo, out, low, high, field_halo, middle,
 ):
+    field_halo_tiles(field_halo, above, below)
     for k in range(TILES + 1):
         at = lane_tile(k)
+
+        def given(row):
+            if k == TILES:
+                return lambda side: side[1][AT_RIM + row : AT_RIM + row + 1, :]
+            return lambda side: side[0][row : row + 1, at]
+
+        sides = ((raw_above, above), (raw_below, below))
         for b in range(NVAR):
             for a in range(NVAR):
-                inverse_halo[b, a, :, at] = halo_tile(above, below, b * NVAR + a, None, k)
-            rhs_halo[b, :, at] = halo_tile(above, below, AT_RHS + b, None, k)
-            field_halo[b, :, at] = halo_tile(above, below, AT_FIELD + b, AT_FIELD + NVAR + b, k)
+                inverse_halo[b, a, :, at] = halo_tile(sides, given(b * NVAR + a))
+            rhs_halo[b, :, at] = halo_tile(sides, given(AT_RHS + b))
         for i in range(4):
-            coupling_halo[i, :, at] = halo_tile(above, below, AT_COUPLING + i, AT_COUPLING + 4 + i, k)
+            coupling_halo[i, :, at] = halo_tile(
+                sides, given(AT_COUPLING + i), given(AT_COUPLING + 4 + i)
+            )
 
     def store(k, values):
         for a in range(NVAR):
             out[a, :, lane_tile(k)] = values[a]
 
-    two_sweeps(
-        dict(rhs=rhs, inverse=inverse, coupling=coupling),
-        dict(rhs=rhs_rim, inverse=inverse_rim, coupling=coupling_rim),
-        dict(rhs=rhs_halo, inverse=inverse_halo, coupling=coupling_halo),
-        field, field_halo, middle, TILES + 1, store,
-    )
+    arrays = with_halos(
+        (rhs, inverse, coupling),
+        (rhs_rim, inverse_rim, coupling_rim),
+        (rhs_halo, inverse_halo, coupling_halo),
+    )
+    first = lambda b, k: field_rim[b] if k == TILES else field[b, :, lane_tile(k)]
+    odd_sweep(arrays, first, field_halo, middle)
+    even_sweep(TILES + 1, arrays, middle, store)
     for message, near, second in ((low, 0, 1), (high, CX - 1, CX - 2)):
-        message[...] = jnp.zeros_like(message)
-        field_rows(message, 0, out, near, second)
-
-
-def last_kernel(
+        field_rows(message, lambda b, row, k: out[b, row, lane_tile(k)], near, second)
+        message[AT_RIM:] = jnp.zeros((FIELD_ROWS - AT_RIM, LANES), F32)
+
+
+def sens_kernel(
     rhs, inverse, coupling, rhs_rim, inverse_rim, coupling_rim, rhs_halo, inverse_halo,
-    coupling_halo, field, above, below, grad, out, sens, field_halo, middle,
+    coupling_halo, field, above, below, grad, live, slots, values, middle, field_halo, sens, table,
 ):
-    for k in range(TILES + 1):
-        for b in range(NVAR):
-            field_halo[b, :, lane_tile(k)] = halo_tile(above, below, b, NVAR + b, k)
+    field_halo_tiles(field_halo, above, below)
+    arrays = with_halos(
+        (rhs, inverse, coupling),
+        (rhs_rim, inverse_rim, coupling_rim),
+        (rhs_halo, inverse_halo, coupling_halo),
+    )
+
+    def store(k, values):
+        sens[:, lane_tile(k)] = grad[0, :, lane_tile(k)] * values[0]
+
+    odd_sweep(arrays, lambda b, k: field[b, :, lane_tile(k)], field_halo, middle)
+    even_sweep(TILES, arrays, middle, store, (NVAR - 1,))
+    gather_slots(live, sens, slots, values, table)
+
+
+def adjoint_kernel(
+    rhs, inverse, coupling, rhs_rim, inverse_rim, coupling_rim, rhs_halo, inverse_halo,
+    coupling_halo, middle, out,
+):
+    arrays = with_halos(
+        (rhs, inverse, coupling),
+        (rhs_rim, inverse_rim, coupling_rim),
+        (rhs_halo, inverse_halo, coupling_halo),
+    )
 
     def store(k, values):
         for a in range(NVAR):
             out[a, :, lane_tile(k)] = values[a]
-        sens[:, lane_tile(k)] = grad[0, :, lane_tile(k)] * values[NVAR - 1]
-
-    two_sweeps(
-        dict(rhs=rhs, inverse=inverse, coupling=coupling),
-        dict(rhs=rhs_rim, inverse=inverse_rim, coupling=coupling_rim),
-        dict(rhs=rhs_halo, inverse=inverse_halo, coupling=coupling_halo),
-        field, field_halo, middle, TILES, store,
-    )
+
+    even_sweep(TILES, arrays, middle, store)
 
 
 def shifted(axis, size, step):
@@ -271,40 +333,68 @@
     return above, below
 
 
-def relax(rhs, inverse, coupling, grad):
-    def call(kernel, name, shapes, scratch, *arrays):
+def relax_and_gather(rhs, inverse, coupling, grad, slots):
+    hbm = pl.BlockSpec(memory_space=pltpu.HBM)
+
+    def call(kernel, name, shapes, scratch, *arrays, in_specs=None, out_specs=None, cost=None):
         return pl.pallas_call(
             kernel,
             out_shape=shapes,
-            in_specs=[VMEM] * len(arrays),
-            out_specs=[VMEM] * len(shapes),
+            in_specs=in_specs or [VMEM] * len(arrays),
+            out_specs=out_specs or [VMEM] * len(shapes),
             scratch_shapes=scratch,
             compiler_params=PARAMS,
+            cost_estimate=cost,
             name=name,
         )(*arrays)
 
     rims = (f32(NVAR, CX, LANES), f32(NVAR, NVAR, CX, LANES), f32(4, CX, LANES))
     halos = (f32(NVAR, 8, EXT), f32(NVAR, NVAR, 8, EXT), f32(4, 8, EXT))
-    scratch = [pltpu.VMEM((NVAR, 8, EXT), F32), pltpu.VMEM((NVAR, CX + 8, EXT), F32)]
-    first, last = pack_columns(inverse, rhs, coupling)
+    in_hbm = [pltpu.with_memory_space_constraint(a, pltpu.HBM) for a in (rhs, inverse, coupling)]
+    blocks = [
+        pltpu.VMEM((*lead, *size), F32)
+        for size in ((CX, LANES),) * 2 + ((8, CY),) * 2
+        for lead in ((NVAR, NVAR), (NVAR,), (4,))
+    ]
+    first, last, low, high = call(
+        pack_kernel, "pack_given", (f32(PACKED, CX, LANES),) * 2 + (f32(RAW_ROWS, CY),) * 2,
+        [*blocks, pltpu.SemaphoreType.DMA((len(blocks),))], *in_hbm, in_specs=[hbm] * 3,
+    )
     after = lax.ppermute(first, "dom", shifted("dom", N_DOM, -1))
     before = lax.ppermute(last, "dom", shifted("dom", N_DOM, 1))
-    given = (rhs, inverse, coupling)
-    whole = f32(NVAR, CX, EXT)
-    *rim, field, low, high = call(
-        first_kernel, "first_product", (*rims, whole, f32(64, EXT), f32(64, EXT)), [],
-        *given, after, before,
-    )
-    above, below = to_span_neighbours(low, high)
+    *given, field = call(
+        load_kernel, "load_and_product",
+        (*(f32(*array.shape) for array in (rhs, inverse, coupling)), f32(NVAR, CX, CY)),
+        [pltpu.SemaphoreType.DMA((3 * CX // 8,))], *in_hbm, first, in_specs=[hbm] * 3 + [ANY],
+        cost=pl.CostEstimate(flops=2 * 36 * CX * CY, bytes_accessed=13 << 20, transcendentals=0),
+    )
+    raw = to_span_neighbours(low, high)
+    live = live_rows(slots)
+    *rim, low, high = call(
+        rim_kernel, "rim_product",
+        (*rims, f32(NVAR, CX, LANES), f32(FIRST_ROWS, LANES), f32(FIRST_ROWS, LANES)), [],
+        field, after, before,
+    )
+    scratch = [pltpu.VMEM((NVAR, 8, EXT), F32), pltpu.VMEM((NVAR, CX + 8, EXT), F32)]
     *halo, field, low, high = call(
-        middle_kernel, "sweeps_1_2", (*halos, whole, f32(16, EXT), f32(16, EXT)), scratch,
-        *given, *rim, field, above, below,
-    )
-    above, below = to_span_neighbours(low, high)
-    return call(
-        last_kernel, "sweeps_3_4", (f32(NVAR, CX, CY), f32(CX, CY)), scratch,
-        *given, *rim, *halo, field, above, below, grad,
-    )
+        middle_kernel, "sweeps_1_2",
+        (*halos, f32(NVAR, CX, EXT), f32(FIELD_ROWS, LANES), f32(FIELD_ROWS, LANES)), scratch,
+        *given, *rim, field, *raw, *to_span_neighbours(low, high),
+    )
+    arrays = (*given, *rim[:3], *halo)
+    values, middle = call(
+        sens_kernel, "sweep_3_and_gather",
+        (f32(SLOT_ROWS, LANES), f32(NVAR, CX + 8, EXT)),
+        [
+            pltpu.VMEM((NVAR, 8, EXT), F32),
+            pltpu.VMEM((CX, CY), F32),
+            pltpu.VMEM((2 * LANES, 2 * LANES), BF),
+        ],
+        *arrays, field, *to_span_neighbours(low, high), grad, live, slots,
+        in_specs=[VMEM] * 13 + [SMEM, VMEM],
+    )
+    (adjoint,) = call(adjoint_kernel, "sweep_4", (f32(NVAR, CX, CY),), [], *arrays, middle)
+    return adjoint, values
 
 
 def two_parts(value):
@@ -376,7 +466,7 @@
     )(slots)
 
 
-def gather_kernel(live, sens, slots, out, table):
+def gather_slots(live, sens, slots, out, table):
     cells = jnp.concatenate([sens[:, lane_tile(k)] for k in range(TILES)], axis=0).T
     for part, half in enumerate(two_parts(cells)):
         table[part * LANES : (part + 1) * LANES, :] = half.astype(BF)
@@ -397,18 +487,6 @@
             )
             for i, row in enumerate(rows):
                 out[pl.ds(row, 1), :] = value[:, lane_tile(i)]
-
-
-def gather(live, sens, slots):
-    return pl.pallas_call(
-        gather_kernel,
-        out_shape=f32(SLOT_ROWS, LANES),
-        in_specs=[SMEM, VMEM, VMEM],
-        out_specs=VMEM,
-        scratch_shapes=[pltpu.VMEM((2 * LANES, 2 * LANES), BF)],
-        compiler_params=PARAMS,
-        name="gather_slots",
-    )(live, sens, slots)
 
 
 def face_kernel(values, faces, out, total):
@@ -483,6 +561,24 @@
     )(*parts, grad, nodes)
 
 
+def add_kernel(part0, part1, part2, part3, out):
+    for c in range(3):
+        total = (part0[c] + part1[c]) + (part2[c] + part3[c])
+        for row in range(NODE_HI):
+            out[c : c + 1, lane_tile(row)] = total[row : row + 1]
+
+
+def add_parts(parts):
+    return pl.pallas_call(
+        add_kernel,
+        out_shape=f32(3, NODE_DEV),
+        in_specs=[VMEM] * 4,
+        out_specs=VMEM,
+        compiler_params=PARAMS,
+        name="add_parts",
+    )(*parts)
+
+
 def to_node_owners(turn):
     offsets = (0, 1, N_DOM - 1, N_DOM // 2)
     return [
@@ -495,19 +591,20 @@
 def shards(
     adjoint_rhs, block_inverse, coupling, distance_grad, slot_cell, slot_face, area_grad, face_nodes
 ):
-    adjoint, cell_sens = relax(adjoint_rhs, block_inverse, coupling, distance_grad)
     slots = slot_cell.reshape(SLOT_ROWS, LANES)
-    slot_vals = gather(live_rows(slots), cell_sens, slots)
+    adjoint, slot_vals = relax_and_gather(
+        adjoint_rhs, block_inverse, coupling, distance_grad, slots
+    )
     received = lax.all_to_all(slot_vals, "dom", split_axis=0, concat_axis=0, tiled=True)
     face_part = face_sums(received, slot_face.reshape(SLOT_ROWS, LANES))
     parts = [face_part] + [
         lax.ppermute(face_part, "span", shifted("span", N_SPAN, turn)) for turn in range(1, N_SPAN)
     ]
     face_sens, part = node_sums(parts, area_grad, face_nodes)
-    node_sens = sum(
-        lax.ppermute(part, ("span", "dom"), to_node_owners(turn)) for turn in range(N_SPAN)
-    )
-    return (adjoint, face_sens.reshape(FACE_DEV), node_sens.reshape(3, NODE_DEV))
+    parts = [
+        lax.ppermute(part, ("span", "dom"), to_node_owners(turn)) for turn in (1, 2, 3, 0)
+    ]
+    return (adjoint, face_sens.reshape(FACE_DEV), add_parts(parts))
 
 
 def solution(mesh):

time: 88.8 us -> 84.9 us (0.956)
  Pallas kernels: 24.7 us -> 30.6 us
  waiting for transfers between devices: 25.3 us -> 20.1 us
  local copies, waits for them, and re-layouts: 5.21 us -> 0.02 us
    pallas_call x5 -> x7, Pallas kernels: 14.3 us -> 20.1 us  [the longest x6 19.4 us: call(): pl.pallas_call(kernel, out_shape=shapes, in_specs=in_specs or [VMEM] * le...]
    unnamed x21 -> x10, local copies, waits for them, and re-layouts: 5.21 us -> 0.02 us
    ppermute x2 -> x3, starting transfers between devices: 4.18 us -> 7.29 us  [to_span_neighbours(): above = lax.ppermute(low, 'span', shifted('span', N_SPAN, -1))]
    ppermute x2, waiting for transfers between devices: 6.66 us -> 3.74 us  [the longest x1 3.74 us: relax_and_gather(): before = lax.ppermute(last, 'dom', shifted('dom', N_DOM, 1))]
    ppermute x2 -> x3, waiting for transfers between devices: 4.55 us -> 2.19 us  [to_span_neighbours(): above = lax.ppermute(low, 'span', shifted('span', N_SPAN, -1))]
    ppermute x3, waiting for transfers between devices: 3.01 us -> 4.81 us  [shards(): lax.ppermute(face_part, 'span', shifted('span', N_SPAN, turn))]
    ppermute x4, waiting for transfers between devices: 5.9 us -> 4.28 us  [shards(): lax.ppermute(part, ('span', 'dom'), to_node_owners(turn))]
    ppermute x4, starting transfers between devices: 5.69 us -> 4.58 us  [shards(): lax.ppermute(part, ('span', 'dom'), to_node_owners(turn))]
  transfers between devices with their start and end apart: 13 -> 15, of which waited for: 11 -> 10; matrix products, arithmetic and copies ran while one was open for 0% -> 0% of each run, Pallas kernels for 2% -> 9%
where the time goes in v4:
time: 84.9 us; the launch traced here: 84.2 us
  Pallas kernels  30.6 us (36%)
  starting transfers between devices  20.9 us (25%)
  waiting for transfers between devices  20.1 us (24%)
  blocking collectives  11.9 us (14%)
    pallas_call x6, Pallas kernels, call(): pl.pallas_call(kernel, out_shape=shapes, in_specs=in_specs or [VMEM] * le...  19.4 us
    all_to_all x1, blocking collectives, shards(): lax.all_to_all(slot_vals, 'dom', split_axis=0, concat_axis=0, tiled=True)  11.9 us
    ppermute x3, starting transfers between devices, to_span_neighbours(): above = lax.ppermute(low, 'span', shifted('span', N_SPAN, -1))  7.29 us
    ppermute x3, waiting for transfers between devices, to_span_neighbours(): below = lax.ppermute(high, 'span', shifted('span', N_SPAN, 1))  5.07 us
    ppermute x3, waiting for transfers between devices, shards(): lax.ppermute(face_part, 'span', shifted('span', N_SPAN, turn))  4.81 us
    pallas_call x1, Pallas kernels, face_sums(): pl.pallas_call(face_kernel, out_shape=f32(FACE_HI, LANES), in_specs=[VMEM...  4.76 us
    ppermute x4, starting transfers between devices, shards(): lax.ppermute(part, ('span', 'dom'), to_node_owners(turn))  4.58 us
    ppermute x1, starting transfers between devices, relax_and_gather(): after = lax.ppermute(first, 'dom', shifted('dom', N_DOM, -1))  4.37 us
  transfers between devices with their start and end apart: 15, of which 10 were waited for; matrix products, arithmetic and copies ran while one was open for 0% of the time, Pallas kernels for 9%

profile of v4, /device:TPU:0, one launch (start us, length us, event | category | flops | bytes accessed | tf_op | source)
XLA Modules:
  0.0 84.2 jit_solution(8477958109127711058)
XLA Ops:
  0.6 2.4 %pack_given.1 = (f32[2,32,128]{2,1,0:T(8,128)S(1)}, f32[2,32,128]{2,1,0:T(8,128)S(1)}, f32[56,1024]{1,0:T(8,128)S(1)}, f32[56,1024]{1,0:T(8,128)S(1)}) custom-call(f32[6,32,1024]{2,1,0:T(8,128)} %rhs.3, f32[6,6,32,1024]{3,2,1,0:T(8,128)} %inverse.3, f32[4,32,1024]{2,1,0:T(8,128)} %coupling.3), custom_call_target="tpu_custom_call" | custom-call | tf_op jit(solution)/shard_map/pack_given/pallas_call | solution.py:340
  3.1 4.2 %collective-permute-start.2 = (f32[56,1024]{1,0:T(8,128)S(1)}, f32[56,1024]{1,0:T(8,128)S(1)}, u32[]{:S(2)}, u32[]{:S(2)}) collective-permute-start(f32[56,1024]{1,0:T(8,128)S(1)} %get-tuple-element.37), channel_id=1, source_target_pairs={{0,96},{32,0},{64,32},{96,64},{1,97},{33,1},{65,33},{97,65},{2,98}... | collective-permute-start | bytes 688136 | tf_op jit(solution)/shard_map/ppermute | solution.py:331
  7.2 0.0 collective-permute-start.3
  7.3 4.4 %collective-permute-start = (f32[2,32,128]{2,1,0:T(8,128)S(1)}, f32[2,32,128]{2,1,0:T(8,128)S(1)}, u32[]{:S(2)}, u32[]{:S(2)}) collective-permute-start(f32[2,32,128]{2,1,0:T(8,128)S(1)} %get-tuple-element.27.packed), channel_id=1, source_target_pairs={{0,31},{1,0},{2,1},{3,2},{4,3},{5,4},{6,5},{7,6},{8,7},{9,8},{10,9... | collective-permute-start | bytes 98312 | tf_op jit(solution)/shard_map/ppermute | solution.py:363
  11.6 0.0 collective-permute-start.1
  11.6 2.9 %load_and_product.1 = (f32[6,32,1024]{2,1,0:T(8,128)S(1)}, f32[6,6,32,1024]{3,2,1,0:T(8,128)S(1)}, f32[4,32,1024]{2,1,0:T(8,128)S(1)}, f32[6,32,1024]{2,1,0:T(8,128)S(1)}) custom-call(f32[6,32,1024]{2,1,0:T(8,128)} %rhs.3, f32[6,6,32,1024]{3,2,1,0:T(8,128)} %inverse.3, f32[4,32,1024]{2,1,0:T(8,128)} %coupling.3, f32[2,32,128]{2,1,0:T(8,128)S(1)} %get-tuple-element.27.packed), custom_call_target="tpu_custom_call" | custom-call | flops 2359296 | bytes 13631488 | tf_op jit(solution)/shard_map/load_and_product/pallas_call | solution.py:340
  14.5 0.0 copy-start
  14.5 0.0 collective-permute-done.after
  14.5 3.7 %collective-permute-done.1.before = f32[2,32,128]{2,1,0:T(8,128)S(1)} collective-permute-done((f32[2,32,128]{2,1,0:T(8,128)S(1)}, f32[2,32,128]{2,1,0:T(8,128)S(1)}, u32[]{:S(2)}, u32[]{:S(2)}) %collective-permute-start.1) | collective-permute-done | bytes 32800 | tf_op jit(solution)/shard_map/ppermute | solution.py:364
  18.3 0.0 copy-start.3
  18.3 0.5 rim_product.1
  18.8 3.0 %collective-permute-start.4 = (f32[160,128]{1,0:T(8,128)S(1)}, f32[160,128]{1,0:T(8,128)S(1)}, u32[]{:S(2)}, u32[]{:S(2)}) collective-permute-start(f32[160,128]{1,0:T(8,128)S(1)} %get-tuple-element.39), channel_id=1, source_target_pairs={{0,96},{32,0},{64,32},{96,64},{1,97},{33,1},{65,33},{97,65},{2,98}... | collective-permute-start | bytes 245768 | tf_op jit(solution)/shard_map/ppermute | solution.py:331
  21.9 0.0 collective-permute-start.5
  21.9 2.1 %collective-permute-done.4.above = f32[160,128]{1,0:T(8,128)S(1)} collective-permute-done((f32[160,128]{1,0:T(8,128)S(1)}, f32[160,128]{1,0:T(8,128)S(1)}, u32[]{:S(2)}, u32[]{:S(2)}) %collective-permute-start.4) | collective-permute-done | bytes 81952 | tf_op jit(solution)/shard_map/ppermute | solution.py:331
  23.9 3.6 %collective-permute-done.5.below = f32[160,128]{1,0:T(8,128)S(1)} collective-permute-done((f32[160,128]{1,0:T(8,128)S(1)}, f32[160,128]{1,0:T(8,128)S(1)}, u32[]{:S(2)}, u32[]{:S(2)}) %collective-permute-start.5) | collective-permute-done | bytes 81952 | tf_op jit(solution)/shard_map/ppermute | solution.py:332
  27.5 0.0 collective-permute-done.2.raw_above
  27.5 0.0 collective-permute-done.3.raw_below
  27.5 3.1 %sweeps_1_2.1 = (f32[6,8,1152]{2,1,0:T(8,128)S(1)}, f32[6,6,8,1152]{3,2,1,0:T(8,128)S(1)}, f32[4,8,1152]{2,1,0:T(8,128)S(1)}, f32[6,32,1152]{2,1,0:T(8,128)S(1)}...) custom-call(f32[6,32,1024]{2,1,0:T(8,128)S(1)} %get-tuple-element.28.rhs, ...), custom_call_target="tpu_custom_call" | custom-call | tf_op jit(solution)/shard_map/sweeps_1_2/pallas_call | solution.py:340
  30.6 0.1 collective-permute-start.6
  30.7 2.0 %collective-permute-start.7 = (f32[112,128]{1,0:T(8,128)S(1)}, f32[112,128]{1,0:T(8,128)S(1)}, u32[]{:S(2)}, u32[]{:S(2)}) collective-permute-start(f32[112,128]{1,0:T(8,128)S(1)} %get-tuple-element.46), channel_id=1, source_target_pairs={{0,32},{32,64},{64,96},{96,0},{1,33},{33,65},{65,97},{97,1},{2,34}... | collective-permute-start | bytes 172040 | tf_op jit(solution)/shard_map/ppermute | solution.py:332
  32.7 0.0 copy-done
  32.7 2.0 %live_rows.1.live = s32[8,384]{1,0:T(8,128)S(1)} custom-call(s32[512,128]{1,0:T(8,128)S(1)} %bitcast.5), custom_call_target="tpu_custom_call" | custom-call | tf_op jit(solution)/shard_map/live_rows/pallas_call | solution.py:458
  34.7 0.1 collective-permute-done.6.above
  34.8 1.5 %collective-permute-done.7.below = f32[112,128]{1,0:T(8,128)S(1)} collective-permute-done((f32[112,128]{1,0:T(8,128)S(1)}, f32[112,128]{1,0:T(8,128)S(1)}, u32[]{:S(2)}, u32[]{:S(2)}) %collective-permute-start.7) | collective-permute-done | bytes 57376 | tf_op jit(solution)/shard_map/ppermute | solution.py:332
  36.3 0.0 copy-done.3
  36.3 8.5 %sweep_3_and_gather.1 = (f32[512,128]{1,0:T(8,128)S(1)}, f32[6,40,1152]{2,1,0:T(8,128)S(1)}) custom-call(f32[6,32,1024]{2,1,0:T(8,128)S(1)} %get-tuple-element.28.rhs, f32[6,6,32,1024]{3,2,1,0:T(8,128)S(1)} %get-tuple-element.29.inverse, f32[4,32,1024]{2,1,0:T(8,128)S(1)} %get-tuple-element.30.coupling, f32[6,32,128]{2,1,0:T(8,128)S(1)} %get-tuple-element.33.rhs_rim, ...), custom_call_target="tpu_custom_call" | custom-call | tf_op jit(solution)/shard_map/sweep_3_and_gather/pallas_call | solution.py:340
  44.8 11.9 %all_to_all.11 = f32[32,16,128]{2,1,0:T(8,128)S(1)} all-to-all(f32[32,16,128]{2,1,0:T(8,128)S(1)} %bitcast.9), channel_id=1, replica_groups=mesh['span'=4,'dom'=32] {'dom'}, dimensions={0} | all-to-all | bytes 524288 | tf_op jit(solution)/shard_map/all_to_all | solution.py:598
  56.7 0.0 copy-done.2
  56.7 4.8 %face_sums.1.part0 = f32[64,128]{1,0:T(8,128)S(1)} custom-call(f32[512,128]{1,0:T(8,128)S(1)} %bitcast.7, s32[512,128]{1,0:T(8,128)S(1)} %bitcast.8), custom_call_target="tpu_custom_call" | custom-call | tf_op jit(solution)/shard_map/face_sums/pallas_call | solution.py:512
  61.4 0.1 collective-permute-start.10
  61.5 2.0 %collective-permute-start.8 = (f32[64,128]{1,0:T(8,128)S(1)}, f32[64,128]{1,0:T(8,128)S(1)}, u32[]{:S(2)}, u32[]{:S(2)}) collective-permute-start(f32[64,128]{1,0:T(8,128)S(1)} %face_sums.1.part0), channel_id=1, source_target_pairs={{0,32},{32,64},{64,96},{96,0},{1,33},{33,65},{65,97},{97,1},{2,34}... | collective-permute-start | bytes 98312 | tf_op jit(solution)/shard_map/ppermute | solution.py:601
  63.5 0.6 collective-permute-start.9
  64.1 1.3 %collective-permute-done.10.part3 = f32[64,128]{1,0:T(8,128)S(1)} collective-permute-done((f32[64,128]{1,0:T(8,128)S(1)}, f32[64,128]{1,0:T(8,128)S(1)}, u32[]{:S(2)}, u32[]{:S(2)}) %collective-permute-start.10) | collective-permute-done | bytes 32800 | tf_op jit(solution)/shard_map/ppermute | solution.py:601
  65.4 1.3 %collective-permute-done.8.part1 = f32[64,128]{1,0:T(8,128)S(1)} collective-permute-done((f32[64,128]{1,0:T(8,128)S(1)}, f32[64,128]{1,0:T(8,128)S(1)}, u32[]{:S(2)}, u32[]{:S(2)}) %collective-permute-start.8) | collective-permute-done | bytes 32800 | tf_op jit(solution)/shard_map/ppermute | solution.py:601
  66.7 2.2 %collective-permute-done.9.part2 = f32[64,128]{1,0:T(8,128)S(1)} collective-permute-done((f32[64,128]{1,0:T(8,128)S(1)}, f32[64,128]{1,0:T(8,128)S(1)}, u32[]{:S(2)}, u32[]{:S(2)}) %collective-permute-start.9) | collective-permute-done | bytes 32800 | tf_op jit(solution)/shard_map/ppermute | solution.py:601
  69.0 0.0 copy-done.1
  69.0 0.0 copy-done.4
  69.0 3.7 %node_sums.1 = (f32[64,128]{1,0:T(8,128)}, f32[3,32,128]{2,1,0:T(8,128)S(1)}) custom-call(f32[64,128]{1,0:T(8,128)S(1)} %face_sums.1.part0, f32[64,128]{1,0:T(8,128)S(1)} %collective-permute-done.8.part1, f32[64,128]{1,0:T(8,128)S(1)} %collective-permute-done.9.part2, f32[64,128]{1,0:T(8,128)S(1)} %collective-permute-done.10.part3, ...), custom_call_target="tpu_custom_call" | custom-call | tf_op jit(solution)/shard_map/node_sums/pallas_call | solution.py:553
  72.7 0.6 collective-permute-start.11
  73.3 2.1 %collective-permute-start.12 = (f32[3,32,128]{2,1,0:T(8,128)S(1)}, f32[3,32,128]{2,1,0:T(8,128)S(1)}, u32[]{:S(2)}, u32[]{:S(2)}) collective-permute-start(f32[3,32,128]{2,1,0:T(8,128)S(1)} %get-tuple-element.50), channel_id=1, source_target_pairs={{0,64},{1,65},{2,66},{3,67},{4,68},{5,69},{6,70},{7,71},{8,72},{9,... | collective-permute-start | bytes 147464 | tf_op jit(solution)/shard_map/ppermute | solution.py:605
  75.4 1.2 %collective-permute-start.13 = (f32[3,32,128]{2,1,0:T(8,128)S(1)}, f32[3,32,128]{2,1,0:T(8,128)S(1)}, u32[]{:S(2)}, u32[]{:S(2)}) collective-permute-start(f32[3,32,128]{2,1,0:T(8,128)S(1)} %get-tuple-element.50), channel_id=1, source_target_pairs={{0,96},{1,97},{2,98},{3,99},{4,100},{5,101},{6,102},{7,103},{8,104... | collective-permute-start | bytes 147464 | tf_op jit(solution)/shard_map/ppermute | solution.py:605
  76.6 0.7 collective-permute-start.14
  77.2 2.1 %sweep_4.1 = f32[6,32,1024]{2,1,0:T(8,128)} custom-call(f32[6,32,1024]{2,1,0:T(8,128)S(1)} %get-tuple-element.28.rhs, f32[6,6,32,1024]{3,2,1,0:T(8,128)S(1)} %get-tuple-element.29.inverse, f32[4,32,1024]{2,1,0:T(8,128)S(1)} %get-tuple-element.30.coupling, f32[6,32,128]{2,1,0:T(8,128)S(1)} %get-tuple-element.33.rhs_rim, ...), custom_call_target="tpu_custom_call" | custom-call | tf_op jit(solution)/shard_map/sweep_4/pallas_call | solution.py:340
  79.3 1.1 %collective-permute-done.11.part0 = f32[3,32,128]{2,1,0:T(8,128)S(1)} collective-permute-done((f32[3,32,128]{2,1,0:T(8,128)S(1)}, f32[3,32,128]{2,1,0:T(8,128)S(1)}, u32[]{:S(2)}, u32[]{:S(2)}) %collective-permute-start.11) | collective-permute-done | bytes 49184 | tf_op jit(solution)/shard_map/ppermute | solution.py:605
  80.4 0.0 collective-permute-done.12.part1
  80.4 3.1 %collective-permute-done.13.part2 = f32[3,32,128]{2,1,0:T(8,128)S(1)} collective-permute-done((f32[3,32,128]{2,1,0:T(8,128)S(1)}, f32[3,32,128]{2,1,0:T(8,128)S(1)}, u32[]{:S(2)}, u32[]{:S(2)}) %collective-permute-start.13) | collective-permute-done | bytes 49184 | tf_op jit(solution)/shard_map/ppermute | solution.py:605
  83.6 0.0 collective-permute-done.14.part3
  83.6 0.7 add_parts.1
  (3 shorter events, 0.0 us)
Async XLA Ops:
  3.1 24.5 %collective-permute-start.2 = (f32[56,1024]{1,0:T(8,128)S(1)}, f32[56,1024]{1,0:T(8,128)S(1)}, u32[]{:S(2)}, u32[]{:S(2)}) collective-permute-start(f32[56,1024]{1,0:T(8,128)S(1)} %get-tuple-element.37), channel_id=1, source_target_pairs={{0,96},{32,0},{64,32},{96,64},{1,97},{33,1},{65,33},{97,65},{2,98}... | collective-permute-start | bytes 688136 | tf_op jit(solution)/shard_map/ppermute | solution.py:331
  7.2 20.3 %collective-permute-start.3 = (f32[56,1024]{1,0:T(8,128)S(1)}, f32[56,1024]{1,0:T(8,128)S(1)}, u32[]{:S(2)}, u32[]{:S(2)}) collective-permute-start(f32[56,1024]{1,0:T(8,128)S(1)} %get-tuple-element.38), channel_id=1, source_target_pairs={{0,32},{32,64},{64,96},{96,0},{1,33},{33,65},{65,97},{97,1},{2,34}... | collective-permute-start | bytes 688136 | tf_op jit(solution)/shard_map/ppermute | solution.py:332
  7.3 7.3 %collective-permute-start = (f32[2,32,128]{2,1,0:T(8,128)S(1)}, f32[2,32,128]{2,1,0:T(8,128)S(1)}, u32[]{:S(2)}, u32[]{:S(2)}) collective-permute-start(f32[2,32,128]{2,1,0:T(8,128)S(1)} %get-tuple-element.27.packed), channel_id=1, source_target_pairs={{0,31},{1,0},{2,1},{3,2},{4,3},{5,4},{6,5},{7,6},{8,7},{9,8},{10,9... | collective-permute-start | bytes 98312 | tf_op jit(solution)/shard_map/ppermute | solution.py:363
  11.6 6.7 %collective-permute-start.1 = (f32[2,32,128]{2,1,0:T(8,128)S(1)}, f32[2,32,128]{2,1,0:T(8,128)S(1)}, u32[]{:S(2)}, u32[]{:S(2)}) collective-permute-start(f32[2,32,128]{2,1,0:T(8,128)S(1)} %get-tuple-element.32), channel_id=1, source_target_pairs={{0,1},{1,2},{2,3},{3,4},{4,5},{5,6},{6,7},{7,8},{8,9},{9,10},{10,1... | collective-permute-start | bytes 98312 | tf_op jit(solution)/shard_map/ppermute | solution.py:364
  14.5 18.2 %copy-start = (s32[1,1,65536]{2,1,0:T(1,128)S(1)}, s32[1,1,65536]{2,1,0:T(1,128)}, u32[]{:S(2)}) copy-start(s32[1,1,65536]{2,1,0:T(1,128)} %param.12) | copy-start | bytes 786436
  18.3 18.0 %copy-start.3 = (f32[1,32,1024]{2,1,0:T(8,128)S(1)}, f32[1,32,1024]{2,1,0:T(8,128)}, u32[]{:S(2)}) copy-start(f32[1,32,1024]{2,1,0:T(8,128)} %grad.2) | copy-start | bytes 393220
  18.8 5.1 %collective-permute-start.4 = (f32[160,128]{1,0:T(8,128)S(1)}, f32[160,128]{1,0:T(8,128)S(1)}, u32[]{:S(2)}, u32[]{:S(2)}) collective-permute-start(f32[160,128]{1,0:T(8,128)S(1)} %get-tuple-element.39), channel_id=1, source_target_pairs={{0,96},{32,0},{64,32},{96,64},{1,97},{33,1},{65,33},{97,65},{2,98}... | collective-permute-start | bytes 245768 | tf_op jit(solution)/shard_map/ppermute | solution.py:331
  21.9 5.7 %collective-permute-start.5 = (f32[160,128]{1,0:T(8,128)S(1)}, f32[160,128]{1,0:T(8,128)S(1)}, u32[]{:S(2)}, u32[]{:S(2)}) collective-permute-start(f32[160,128]{1,0:T(8,128)S(1)} %get-tuple-element.40), channel_id=1, source_target_pairs={{0,32},{32,64},{64,96},{96,0},{1,33},{33,65},{65,97},{97,1},{2,34}... | collective-permute-start | bytes 245768 | tf_op jit(solution)/shard_map/ppermute | solution.py:332
  30.6 4.2 %collective-permute-start.6 = (f32[112,128]{1,0:T(8,128)S(1)}, f32[112,128]{1,0:T(8,128)S(1)}, u32[]{:S(2)}, u32[]{:S(2)}) collective-permute-start(f32[112,128]{1,0:T(8,128)S(1)} %get-tuple-element.45), channel_id=1, source_target_pairs={{0,96},{32,0},{64,32},{96,64},{1,97},{33,1},{65,33},{97,65},{2,98}... | collective-permute-start | bytes 172040 | tf_op jit(solution)/shard_map/ppermute | solution.py:331
  30.7 5.6 %collective-permute-start.7 = (f32[112,128]{1,0:T(8,128)S(1)}, f32[112,128]{1,0:T(8,128)S(1)}, u32[]{:S(2)}, u32[]{:S(2)}) collective-permute-start(f32[112,128]{1,0:T(8,128)S(1)} %get-tuple-element.46), channel_id=1, source_target_pairs={{0,32},{32,64},{64,96},{96,0},{1,33},{33,65},{65,97},{97,1},{2,34}... | collective-permute-start | bytes 172040 | tf_op jit(solution)/shard_map/ppermute | solution.py:332
  36.3 20.4 %copy-start.2 = (s32[1,1,65536]{2,1,0:T(1,128)S(1)}, s32[1,1,65536]{2,1,0:T(1,128)}, u32[]{:S(2)}) copy-start(s32[1,1,65536]{2,1,0:T(1,128)} %param.13) | copy-start | bytes 786436
  36.3 32.7 %copy-start.1 = (f32[3,4,8192]{2,1,0:T(4,128)S(1)}, f32[3,4,8192]{2,1,0:T(4,128)}, u32[]{:S(2)}) copy-start(f32[3,4,8192]{2,1,0:T(4,128)} %grad.3) | copy-start | bytes 1179652
  36.3 32.7 %copy-start.4 = (s32[4,8192]{1,0:T(4,128)S(1)}, s32[4,8192]{1,0:T(4,128)}, u32[]{:S(2)}) copy-start(s32[4,8192]{1,0:T(4,128)} %nodes.1) | copy-start | bytes 393220
  61.4 4.0 %collective-permute-start.10 = (f32[64,128]{1,0:T(8,128)S(1)}, f32[64,128]{1,0:T(8,128)S(1)}, u32[]{:S(2)}, u32[]{:S(2)}) collective-permute-start(f32[64,128]{1,0:T(8,128)S(1)} %face_sums.1.part0), channel_id=1, source_target_pairs={{0,96},{32,0},{64,32},{96,64},{1,97},{33,1},{65,33},{97,65},{2,98}... | collective-permute-start | bytes 98312 | tf_op jit(solution)/shard_map/ppermute | solution.py:601
  61.5 5.2 %collective-permute-start.8 = (f32[64,128]{1,0:T(8,128)S(1)}, f32[64,128]{1,0:T(8,128)S(1)}, u32[]{:S(2)}, u32[]{:S(2)}) collective-permute-start(f32[64,128]{1,0:T(8,128)S(1)} %face_sums.1.part0), channel_id=1, source_target_pairs={{0,32},{32,64},{64,96},{96,0},{1,33},{33,65},{65,97},{97,1},{2,34}... | collective-permute-start | bytes 98312 | tf_op jit(solution)/shard_map/ppermute | solution.py:601
  63.5 5.4 %collective-permute-start.9 = (f32[64,128]{1,0:T(8,128)S(1)}, f32[64,128]{1,0:T(8,128)S(1)}, u32[]{:S(2)}, u32[]{:S(2)}) collective-permute-start(f32[64,128]{1,0:T(8,128)S(1)} %face_sums.1.part0), channel_id=1, source_target_pairs={{0,64},{32,96},{64,0},{96,32},{1,65},{33,97},{65,1},{97,33},{2,66}... | collective-permute-start | bytes 98312 | tf_op jit(solution)/shard_map/ppermute | solution.py:601
  72.7 7.8 %collective-permute-start.11 = (f32[3,32,128]{2,1,0:T(8,128)S(1)}, f32[3,32,128]{2,1,0:T(8,128)S(1)}, u32[]{:S(2)}, u32[]{:S(2)}) collective-permute-start(f32[3,32,128]{2,1,0:T(8,128)S(1)} %get-tuple-element.50), channel_id=1, source_target_pairs={{0,32},{1,33},{2,34},{3,35},{4,36},{5,37},{6,38},{7,39},{8,40},{9,... | collective-permute-start | bytes 147464 | tf_op jit(solution)/shard_map/ppermute | solution.py:605
  73.3 7.1 %collective-permute-start.12 = (f32[3,32,128]{2,1,0:T(8,128)S(1)}, f32[3,32,128]{2,1,0:T(8,128)S(1)}, u32[]{:S(2)}, u32[]{:S(2)}) collective-permute-start(f32[3,32,128]{2,1,0:T(8,128)S(1)} %get-tuple-element.50), channel_id=1, source_target_pairs={{0,64},{1,65},{2,66},{3,67},{4,68},{5,69},{6,70},{7,71},{8,72},{9,... | collective-permute-start | bytes 147464 | tf_op jit(solution)/shard_map/ppermute | solution.py:605
  75.4 8.2 %collective-permute-start.13 = (f32[3,32,128]{2,1,0:T(8,128)S(1)}, f32[3,32,128]{2,1,0:T(8,128)S(1)}, u32[]{:S(2)}, u32[]{:S(2)}) collective-permute-start(f32[3,32,128]{2,1,0:T(8,128)S(1)} %get-tuple-element.50), channel_id=1, source_target_pairs={{0,96},{1,97},{2,98},{3,99},{4,100},{5,101},{6,102},{7,103},{8,104... | collective-permute-start | bytes 147464 | tf_op jit(solution)/shard_map/ppermute | solution.py:605
  76.6 7.0 %collective-permute-start.14 = (f32[3,32,128]{2,1,0:T(8,128)S(1)}, f32[3,32,128]{2,1,0:T(8,128)S(1)}, u32[]{:S(2)}, u32[]{:S(2)}) collective-permute-start(f32[3,32,128]{2,1,0:T(8,128)S(1)} %get-tuple-element.50), channel_id=1, source_target_pairs={{0,0},{1,1},{2,2},{3,3},{4,4},{5,5},{6,6},{7,7},{8,8},{9,9},{10,10... | collective-permute-start | bytes 147464 | tf_op jit(solution)/shard_map/ppermute | solution.py:605

commit v5 on v4

--- a/solution.py
+++ b/solution.py
@@ -43,6 +43,7 @@
 SMEM = pl.BlockSpec(memory_space=pltpu.SMEM)
 ANY = pl.BlockSpec(memory_space=pl.ANY)
 PARAMS = pltpu.CompilerParams(vmem_limit_bytes=40 << 20)
+INNER = pl.CostEstimate(flops=2 * 90 * CX * CY, bytes_accessed=8 << 20, transcendentals=0)
 BF = jnp.bfloat16
 F32 = jnp.float32
 
@@ -192,15 +193,14 @@
             field_halo[b, :, lane_tile(k)] = halo_tile((above, below), *picks)
 
 
-def sweep(rows, tiles, rhs, inverse, coupling, field, store, variables=range(NVAR)):
+def sweep(cut, tiles, rhs, inverse, coupling, field, store, variables=range(NVAR)):
     last = TILES + 1
-    lane = lax.broadcasted_iota(jnp.int32, (rows, LANES), 1)
     rolled = {}
 
     def shifted_lanes(k, b, side):
         k = k % last
         if (k, b, side) not in rolled:
-            part = coupling((3 - side,), k)[:rows] * field((b,), k)[:rows]
+            part = cut(coupling((3 - side,), k)) * cut(field((b,), k))
             rolled[k, b, side] = pltpu.roll(part, 1 if side else LANES - 1, 1)
         return rolled[k, b, side]
 
@@ -208,48 +208,73 @@
         terms = []
         for b in range(NVAR):
             value = field((b,), k)
-            size = value.shape[0]
-            total = pltpu.roll(coupling((1,), k) * value, size - 1, 0)[:rows]
-            total = total + pltpu.roll(coupling((0,), k) * value, 1, 0)[:rows]
+            total = cut(pltpu.roll(coupling((1,), k) * value, value.shape[0] - 1, 0))
+            total = total + cut(pltpu.roll(coupling((0,), k) * value, 1, 0))
+            lane = lax.broadcasted_iota(jnp.int32, total.shape, 1)
             edge = lane == LANES - 1
             total = total + jnp.where(edge, shifted_lanes(k + 1, b, 0), shifted_lanes(k, b, 0))
             total = total + jnp.where(lane == 0, shifted_lanes(k - 1, b, 1), shifted_lanes(k, b, 1))
-            terms.append(rhs((b,), k)[:rows] - total)
-        store(k, product(lambda b, a: inverse((b, a), k)[:rows], terms, variables))
-
-
-def with_halos(given, rims, halos):
-    def full(main, rim, halo):
-        def tiles(index, k):
-            edge = halo[(*index, slice(None), lane_tile(k))]
-            core = rim[index] if k == TILES else main[(*index, slice(None), lane_tile(k))]
-            return jnp.concatenate([core, edge], axis=0)
-
-        return tiles
-
-    return [full(*three) for three in zip(given, rims, halos)]
-
-
-def odd_sweep(arrays, field, field_halo, middle):
-    def before(index, k):
-        (b,) = index
-        return jnp.concatenate([field(b, k), field_halo[b, :, lane_tile(k)]], axis=0)
-
-    def keep(k, values):
+            terms.append(cut(rhs((b,), k)) - total)
+        store(k, product(lambda b, a: cut(inverse((b, a), k)), terms, variables))
+
+
+def all_rows(part):
+    return part
+
+
+def own_rows(part):
+    return part[:CX]
+
+
+def end_rows(part):
+    return jnp.concatenate([part[:8], part[16:]], axis=0)
+
+
+def own_tiles(main, rim):
+    return lambda index, k: rim[index] if k == TILES else main[(*index, slice(None), lane_tile(k))]
+
+
+def strip_tiles(own, halo):
+    def tiles(index, k):
+        part = own(index, k)
+        edge = halo[(*index, slice(None), lane_tile(k))]
+        return jnp.concatenate([part[CX - 8 :], edge, part[:8]], axis=0)
+
+    return tiles
+
+
+def with_ends(part, ends):
+    row = lax.broadcasted_iota(jnp.int32, (8, LANES), 0)
+    first = jnp.where(row < 4, ends[8:], part[:8])
+    last = jnp.where(row < 4, part[CX - 8 :], ends[:8])
+    return jnp.concatenate([first, part[8 : CX - 8], last], axis=0)
+
+
+def keep_in(ref):
+    def store(k, values):
         for a in range(NVAR):
-            middle[a, :, lane_tile(k)] = values[a]
-
-    sweep(CX + 8, TILES + 1, *arrays, before, keep)
-
-
-def even_sweep(tiles, arrays, middle, store, variables=range(NVAR)):
-    field = lambda index, k: middle[index[0], :, lane_tile(k)]
-    sweep(CX, tiles, *arrays, field, store, variables)
-
-
-def middle_kernel(
+            ref[a, :, lane_tile(k)] = values[a]
+
+    return store
+
+
+def tiles_of(ref):
+    return lambda index, k: ref[(*index, slice(None), lane_tile(k))]
+
+
+def inner_kernel(
+    rhs, inverse, coupling, rhs_rim, inverse_rim, coupling_rim, field_rim, field, odd, even
+):
+    arrays = [own_tiles(rhs, rhs_rim), own_tiles(inverse, inverse_rim)]
+    arrays.append(own_tiles(coupling, coupling_rim))
+    sweep(all_rows, TILES + 1, *arrays, own_tiles(field, field_rim), keep_in(odd))
+    sweep(all_rows, TILES + 1, *arrays, tiles_of(odd), keep_in(even))
+
+
+def edge_kernel(
     rhs, inverse, coupling, rhs_rim, inverse_rim, coupling_rim, field_rim, field, raw_above,
-    raw_below, above, below, rhs_halo, inverse_halo, coupling_halo, out, low, high, field_halo, middle,
+    raw_below, above, below, even, live, rhs_halo, inverse_halo, coupling_halo, out, low, high,
+    field_halo, strip,
 ):
     field_halo_tiles(field_halo, above, below)
     for k in range(TILES + 1):
@@ -269,58 +294,77 @@
             coupling_halo[i, :, at] = halo_tile(
                 sides, given(AT_COUPLING + i), given(AT_COUPLING + 4 + i)
             )
+    arrays = [
+        strip_tiles(own_tiles(rhs, rhs_rim), rhs_halo),
+        strip_tiles(own_tiles(inverse, inverse_rim), inverse_halo),
+        strip_tiles(own_tiles(coupling, coupling_rim), coupling_halo),
+    ]
 
     def store(k, values):
         for a in range(NVAR):
-            out[a, :, lane_tile(k)] = values[a]
-
-    arrays = with_halos(
-        (rhs, inverse, coupling),
-        (rhs_rim, inverse_rim, coupling_rim),
-        (rhs_halo, inverse_halo, coupling_halo),
-    )
-    first = lambda b, k: field_rim[b] if k == TILES else field[b, :, lane_tile(k)]
-    odd_sweep(arrays, first, field_halo, middle)
-    even_sweep(TILES + 1, arrays, middle, store)
+            out[a, :, lane_tile(k)] = with_ends(even[a, :, lane_tile(k)], values[a])
+
+    first = strip_tiles(own_tiles(field, field_rim), field_halo)
+    sweep(all_rows, TILES + 1, *arrays, first, keep_in(strip))
+    sweep(end_rows, TILES + 1, *arrays, tiles_of(strip), store)
     for message, near, second in ((low, 0, 1), (high, CX - 1, CX - 2)):
         field_rows(message, lambda b, row, k: out[b, row, lane_tile(k)], near, second)
         message[AT_RIM:] = jnp.zeros((FIELD_ROWS - AT_RIM, LANES), F32)
 
 
+def inner_sens_kernel(
+    rhs, inverse, coupling, rhs_rim, inverse_rim, coupling_rim, field, grad, odd, sens
+):
+    arrays = [own_tiles(rhs, rhs_rim), own_tiles(inverse, inverse_rim)]
+    arrays.append(own_tiles(coupling, coupling_rim))
+
+    def store(k, values):
+        sens[:, lane_tile(k)] = grad[0, :, lane_tile(k)] * values[0]
+
+    sweep(all_rows, TILES + 1, *arrays, tiles_of(field), keep_in(odd))
+    sweep(all_rows, TILES, *arrays, tiles_of(odd), store, (NVAR - 1,))
+
+
 def sens_kernel(
     rhs, inverse, coupling, rhs_rim, inverse_rim, coupling_rim, rhs_halo, inverse_halo,
-    coupling_halo, field, above, below, grad, live, slots, values, middle, field_halo, sens, table,
+    coupling_halo, field, above, below, grad, inner_sens, live_list, slots, values, strip,
+    field_halo, sens, table, live, done,
 ):
+    copy = pltpu.make_async_copy(live_list, live, done)
+    copy.start()
     field_halo_tiles(field_halo, above, below)
-    arrays = with_halos(
-        (rhs, inverse, coupling),
-        (rhs_rim, inverse_rim, coupling_rim),
-        (rhs_halo, inverse_halo, coupling_halo),
-    )
+    arrays = [
+        strip_tiles(own_tiles(rhs, rhs_rim), rhs_halo),
+        strip_tiles(own_tiles(inverse, inverse_rim), inverse_halo),
+        strip_tiles(own_tiles(coupling, coupling_rim), coupling_halo),
+    ]
 
     def store(k, values):
-        sens[:, lane_tile(k)] = grad[0, :, lane_tile(k)] * values[0]
-
-    odd_sweep(arrays, lambda b, k: field[b, :, lane_tile(k)], field_halo, middle)
-    even_sweep(TILES, arrays, middle, store, (NVAR - 1,))
+        scale = jnp.concatenate([grad[0, CX - 8 :, lane_tile(k)], grad[0, :8, lane_tile(k)]], axis=0)
+        ends = scale * values[0]
+        sens[:, lane_tile(k)] = with_ends(inner_sens[:, lane_tile(k)], ends)
+
+    sweep(all_rows, TILES + 1, *arrays, strip_tiles(tiles_of(field), field_halo), keep_in(strip))
+    sweep(end_rows, TILES, *arrays, tiles_of(strip), store, (NVAR - 1,))
+    copy.wait()
     gather_slots(live, sens, slots, values, table)
 
 
 def adjoint_kernel(
-    rhs, inverse, coupling, rhs_rim, inverse_rim, coupling_rim, rhs_halo, inverse_halo,
-    coupling_halo, middle, out,
+    rhs, inverse, coupling, rhs_rim, inverse_rim, coupling_rim, coupling_halo, odd, strip, out
 ):
-    arrays = with_halos(
-        (rhs, inverse, coupling),
-        (rhs_rim, inverse_rim, coupling_rim),
-        (rhs_halo, inverse_halo, coupling_halo),
-    )
-
-    def store(k, values):
-        for a in range(NVAR):
-            out[a, :, lane_tile(k)] = values[a]
-
-    even_sweep(TILES, arrays, middle, store)
+    inner = [own_tiles(rhs, rhs_rim), own_tiles(inverse, inverse_rim)]
+
+    def coupled(index, k):
+        own = own_tiles(coupling, coupling_rim)(index, k)
+        return jnp.concatenate([own, coupling_halo[(*index, slice(None), lane_tile(k))]], axis=0)
+
+    def field(index, k):
+        ends = strip[(*index, slice(None), lane_tile(k))]
+        own = with_ends(odd[(*index, slice(None), lane_tile(k))], end_rows(ends))
+        return jnp.concatenate([own, ends[8:16]], axis=0)
+
+    sweep(own_rows, TILES, *inner, coupled, field, keep_in(out))
 
 
 def shifted(axis, size, step):
@@ -375,25 +419,30 @@
         (*rims, f32(NVAR, CX, LANES), f32(FIRST_ROWS, LANES), f32(FIRST_ROWS, LANES)), [],
         field, after, before,
     )
-    scratch = [pltpu.VMEM((NVAR, 8, EXT), F32), pltpu.VMEM((NVAR, CX + 8, EXT), F32)]
+    whole, strip = f32(NVAR, CX, EXT), f32(NVAR, 24, EXT)
+    field_halo = pltpu.VMEM((NVAR, 8, EXT), F32)
+    arrays = (*given, *rim[:3])
+    odd, even = call(inner_kernel, "inner_1_2", (whole,) * 2, [], *given, *rim, field, cost=INNER)
     *halo, field, low, high = call(
-        middle_kernel, "sweeps_1_2",
-        (*halos, f32(NVAR, CX, EXT), f32(FIELD_ROWS, LANES), f32(FIELD_ROWS, LANES)), scratch,
-        *given, *rim, field, *raw, *to_span_neighbours(low, high),
-    )
-    arrays = (*given, *rim[:3], *halo)
-    values, middle = call(
-        sens_kernel, "sweep_3_and_gather",
-        (f32(SLOT_ROWS, LANES), f32(NVAR, CX + 8, EXT)),
+        edge_kernel, "edges_1_2",
+        (*halos, whole, f32(FIELD_ROWS, LANES), f32(FIELD_ROWS, LANES)),
+        [field_halo, pltpu.VMEM(strip.shape, F32)],
+        *given, *rim, field, *raw, *to_span_neighbours(low, high), even, live,
+    )
+    odd, inner_sens = call(
+        inner_sens_kernel, "inner_3", (whole, f32(CX, CY)), [], *arrays, field, grad, cost=INNER
+    )
+    values, strip = call(
+        sens_kernel, "edges_3_and_gather", (f32(SLOT_ROWS, LANES), strip),
         [
-            pltpu.VMEM((NVAR, 8, EXT), F32),
-            pltpu.VMEM((CX, CY), F32),
-            pltpu.VMEM((2 * LANES, 2 * LANES), BF),
+            field_halo, pltpu.VMEM((CX, CY), F32), pltpu.VMEM((2 * LANES, 2 * LANES), BF),
+            pltpu.SMEM((8, LIVE_PAD), jnp.int32), pltpu.SemaphoreType.DMA,
         ],
-        *arrays, field, *to_span_neighbours(low, high), grad, live, slots,
-        in_specs=[VMEM] * 13 + [SMEM, VMEM],
-    )
-    (adjoint,) = call(adjoint_kernel, "sweep_4", (f32(NVAR, CX, CY),), [], *arrays, middle)
+        *arrays, *halo, field, *to_span_neighbours(low, high), grad, inner_sens, live, slots,
+    )
+    (adjoint,) = call(
+        adjoint_kernel, "sweep_4", (f32(NVAR, CX, CY),), [], *arrays, halo[2], odd, strip
+    )
     return adjoint, values
 
 
@@ -436,22 +485,22 @@
     return lax.dot_general(left, right, (((1,), (1,)), ((), ())), preferred_element_type=F32)
 
 
-def live_rows_kernel(slots, out, line, done):
-    live = jnp.broadcast_to(slots[...].T[0:1] < CELLS, (8, SLOT_ROWS))
-    ones = jnp.where(live, 1.0, 0.0).astype(BF)
+def live_rows_kernel(slots, out):
+    live = jnp.where(slots[...] < CELLS, 1.0, 0.0).astype(BF)
+    first = jnp.where(lax.broadcasted_iota(jnp.int32, (16, LANES), 1) == 0, 1.0, 0.0).astype(BF)
+    live = outer_sum(first, live)
     square = (SLOT_ROWS, SLOT_ROWS)
     before = lax.broadcasted_iota(jnp.int32, square, 0) < lax.broadcasted_iota(jnp.int32, square, 1)
-    place = jnp.dot(ones, jnp.where(before, 1.0, 0.0).astype(BF), preferred_element_type=F32)
-    place = jnp.where(live, place, -1.0)[0:1].astype(jnp.int32)
+    place = jnp.dot(
+        live.astype(BF), jnp.where(before, 1.0, 0.0).astype(BF), preferred_element_type=F32
+    )
+    place = jnp.where(live > 0.5, place, -1.0)[0:1].astype(jnp.int32)
     at_place = lax.broadcasted_iota(jnp.int32, (LIVE_PAD, SLOT_ROWS), 0) == place
     row = lax.broadcasted_iota(jnp.int32, (8, SLOT_ROWS), 1)
     half = lax.broadcasted_iota(jnp.int32, (8, SLOT_ROWS), 0)
     row = jnp.where(half == 0, row >> 4, row & 15).astype(F32).astype(BF)
     found = outer_sum(row, jnp.where(at_place, 1.0, 0.0).astype(BF))
-    line[...] = jnp.broadcast_to(found[0:1] * 16.0 + found[1:2], line.shape).astype(jnp.int32)
-    copy = pltpu.make_async_copy(line, out, done)
-    copy.start()
-    copy.wait()
+    out[...] = jnp.broadcast_to(found[0:1] * 16.0 + found[1:2], out.shape).astype(jnp.int32)
 
 
 def live_rows(slots):
@@ -459,8 +508,7 @@
         live_rows_kernel,
         out_shape=jax.ShapeDtypeStruct((8, LIVE_PAD), jnp.int32),
         in_specs=[VMEM],
-        out_specs=SMEM,
-        scratch_shapes=[pltpu.VMEM((8, LIVE_PAD), jnp.int32), pltpu.SemaphoreType.DMA],
+        out_specs=VMEM,
         compiler_params=PARAMS,
         name="live_rows",
     )(slots)
@@ -602,7 +650,7 @@
     ]
     face_sens, part = node_sums(parts, area_grad, face_nodes)
     parts = [
-        lax.ppermute(part, ("span", "dom"), to_node_owners(turn)) for turn in (1, 2, 3, 0)
+        lax.ppermute(part, ("span", "dom"), to_node_owners(turn)) for turn in (0, 3, 2, 1)
     ]
     return (adjoint, face_sens.reshape(FACE_DEV), add_parts(parts))
 

time: 84.9 us -> 80.3 us (0.946)
  waiting for transfers between devices: 20.1 us -> 14.2 us
  blocking collectives: 11.9 us -> 12.8 us
    ppermute x1, waiting for transfers between devices: 3.74 us -> 0.01 us  [relax_and_gather(): before = lax.ppermute(last, 'dom', shifted('dom', N_DOM, 1))]
    ppermute x3, waiting for transfers between devices: 2.19 us -> 0.31 us  [to_span_neighbours(): above = lax.ppermute(low, 'span', shifted('span', N_SPAN, -1))]
    pallas_call x1, Pallas kernels: 2.01 us -> 0.53 us  [live_rows(): pl.pallas_call(live_rows_kernel, out_shape=jax.ShapeDtypeStruct((8, LIVE_...]
    pallas_call x6 -> x8, Pallas kernels: 19.4 us -> 20.7 us  [call(): pl.pallas_call(kernel, out_shape=shapes, in_specs=in_specs or [VMEM] * le...]
    all_to_all x1, blocking collectives: 11.9 us -> 12.8 us  [shards(): lax.all_to_all(slot_vals, 'dom', split_axis=0, concat_axis=0, tiled=True)]
  transfers between devices with their start and end apart: 15 -> 15, of which waited for: 10 -> 8; matrix products, arithmetic and copies ran while one was open for 0% -> 0% of each run, Pallas kernels for 9% -> 13%
where the time goes in v5:
time: 80.3 us; the launch traced here: 79.6 us
  Pallas kernels  30.4 us (38%)
  starting transfers between devices  21.4 us (27%)
  waiting for transfers between devices  14.2 us (18%)
  blocking collectives  12.8 us (16%)
    pallas_call x8, Pallas kernels, call(): pl.pallas_call(kernel, out_shape=shapes, in_specs=in_specs or [VMEM] * le...  20.7 us
    all_to_all x1, blocking collectives, shards(): lax.all_to_all(slot_vals, 'dom', split_axis=0, concat_axis=0, tiled=True)  12.8 us
    ppermute x3, starting transfers between devices, to_span_neighbours(): above = lax.ppermute(low, 'span', shifted('span', N_SPAN, -1))  8.13 us
    ppermute x3, waiting for transfers between devices, shards(): lax.ppermute(face_part, 'span', shifted('span', N_SPAN, turn))  5.12 us
    ppermute x1, starting transfers between devices, relax_and_gather(): after = lax.ppermute(first, 'dom', shifted('dom', N_DOM, -1))  5.06 us
    pallas_call x1, Pallas kernels, face_sums(): pl.pallas_call(face_kernel, out_shape=f32(FACE_HI, LANES), in_specs=[VMEM...  4.76 us
    ppermute x3, waiting for transfers between devices, to_span_neighbours(): below = lax.ppermute(high, 'span', shifted('span', N_SPAN, 1))  4.48 us
    ppermute x4, starting transfers between devices, shards(): lax.ppermute(part, ('span', 'dom'), to_node_owners(turn))  4.47 us
  transfers between devices with their start and end apart: 15, of which 8 were waited for; matrix products, arithmetic and copies ran while one was open for 0% of the time, Pallas kernels for 13%

profile of v5, /device:TPU:0, one launch (start us, length us, event | category | flops | bytes accessed | tf_op | source)
XLA Modules:
  0.0 79.6 jit_solution(8277159166695108075)
XLA Ops:
  0.6 2.4 %pack_given.1 = (f32[2,32,128]{2,1,0:T(8,128)S(1)}, f32[2,32,128]{2,1,0:T(8,128)S(1)}, f32[56,1024]{1,0:T(8,128)S(1)}, f32[56,1024]{1,0:T(8,128)S(1)}) custom-call(f32[6,32,1024]{2,1,0:T(8,128)} %rhs.3, f32[6,6,32,1024]{3,2,1,0:T(8,128)} %inverse.3, f32[4,32,1024]{2,1,0:T(8,128)} %coupling.3), custom_call_target="tpu_custom_call" | custom-call | tf_op jit(solution)/shard_map/pack_given/pallas_call | solution.py:384
  3.1 0.0 copy-start
  3.1 4.2 %collective-permute-start.2 = (f32[56,1024]{1,0:T(8,128)S(1)}, f32[56,1024]{1,0:T(8,128)S(1)}, u32[]{:S(2)}, u32[]{:S(2)}) collective-permute-start(f32[56,1024]{1,0:T(8,128)S(1)} %get-tuple-element.40), channel_id=1, source_target_pairs={{0,96},{32,0},{64,32},{96,64},{1,97},{33,1},{65,33},{97,65},{2,98}... | collective-permute-start | bytes 688136 | tf_op jit(solution)/shard_map/ppermute | solution.py:375
  7.3 0.0 collective-permute-start.3
  7.3 0.0 collective-permute-start.1
  7.3 5.1 %collective-permute-start = (f32[2,32,128]{2,1,0:T(8,128)S(1)}, f32[2,32,128]{2,1,0:T(8,128)S(1)}, u32[]{:S(2)}, u32[]{:S(2)}) collective-permute-start(f32[2,32,128]{2,1,0:T(8,128)S(1)} %get-tuple-element.30.packed), channel_id=1, source_target_pairs={{0,31},{1,0},{2,1},{3,2},{4,3},{5,4},{6,5},{7,6},{8,7},{9,8},{10,9... | collective-permute-start | bytes 98312 | tf_op jit(solution)/shard_map/ppermute | solution.py:407
  12.3 2.9 %load_and_product.1 = (f32[6,32,1024]{2,1,0:T(8,128)S(1)}, f32[6,6,32,1024]{3,2,1,0:T(8,128)S(1)}, f32[4,32,1024]{2,1,0:T(8,128)S(1)}, f32[6,32,1024]{2,1,0:T(8,128)S(1)}) custom-call(f32[6,32,1024]{2,1,0:T(8,128)} %rhs.3, f32[6,6,32,1024]{3,2,1,0:T(8,128)} %inverse.3, f32[4,32,1024]{2,1,0:T(8,128)} %coupling.3, f32[2,32,128]{2,1,0:T(8,128)S(1)} %get-tuple-element.30.packed), custom_call_target="tpu_custom_call" | custom-call | flops 2359296 | bytes 13631488 | tf_op jit(solution)/shard_map/load_and_product/pallas_call | solution.py:384
  15.2 0.0 collective-permute-done.1.before
  15.3 0.0 collective-permute-done.after
  15.3 0.5 rim_product.1
  15.8 3.3 %collective-permute-start.4 = (f32[160,128]{1,0:T(8,128)S(1)}, f32[160,128]{1,0:T(8,128)S(1)}, u32[]{:S(2)}, u32[]{:S(2)}) collective-permute-start(f32[160,128]{1,0:T(8,128)S(1)} %get-tuple-element.42), channel_id=1, source_target_pairs={{0,96},{32,0},{64,32},{96,64},{1,97},{33,1},{65,33},{97,65},{2,98}... | collective-permute-start | bytes 245768 | tf_op jit(solution)/shard_map/ppermute | solution.py:375
  19.1 0.0 collective-permute-start.5
  19.1 0.0 copy-done
  19.1 0.5 live_rows.1.live.live_list
  19.6 2.4 %inner_1_2.1 = (f32[6,32,1152]{2,1,0:T(8,128)}, f32[6,32,1152]{2,1,0:T(8,128)S(1)}) custom-call(f32[6,32,1024]{2,1,0:T(8,128)S(1)} %get-tuple-element.31.rhs, f32[6,6,32,1024]{3,2,1,0:T(8,128)S(1)} %get-tuple-element.32.inverse, f32[4,32,1024]{2,1,0:T(8,128)S(1)} %get-tuple-element.33.coupling, f32[6,32,128]{2,1,0:T(8,128)S(1)} %get-tuple-element.36.rhs_rim, ...), custom_call_target="tpu_custom_call" | custom-call | flops 5898240 | bytes 8388608 | tf_op jit(solution)/shard_map/inner_1_2/pallas_call | solution.py:384
  22.0 0.0 copy-start.1
  22.1 0.0 collective-permute-done.4.above
  22.1 2.7 %collective-permute-done.5.below = f32[160,128]{1,0:T(8,128)S(1)} collective-permute-done((f32[160,128]{1,0:T(8,128)S(1)}, f32[160,128]{1,0:T(8,128)S(1)}, u32[]{:S(2)}, u32[]{:S(2)}) %collective-permute-start.5) | collective-permute-done | bytes 81952 | tf_op jit(solution)/shard_map/ppermute | solution.py:376
  24.8 0.0 collective-permute-done.2.raw_above
  24.8 0.0 collective-permute-done.3.raw_below
  24.8 1.8 %edges_1_2.1 = (f32[6,8,1152]{2,1,0:T(8,128)S(1)}, f32[6,6,8,1152]{3,2,1,0:T(8,128)S(1)}, f32[4,8,1152]{2,1,0:T(8,128)S(1)}, f32[6,32,1152]{2,1,0:T(8,128)S(1)},...) custom-call(f32[6,32,1024]{2,1,0:T(8,128)S(1)} %get-tuple-element.31.rhs, ...), custom_call_target="tpu_custom_call" | custom-call | tf_op jit(solution)/shard_map/edges_1_2/pallas_call | solution.py:384
  26.5 0.6 collective-permute-start.6
  27.2 1.5 %collective-permute-start.7 = (f32[112,128]{1,0:T(8,128)S(1)}, f32[112,128]{1,0:T(8,128)S(1)}, u32[]{:S(2)}, u32[]{:S(2)}) collective-permute-start(f32[112,128]{1,0:T(8,128)S(1)} %get-tuple-element.51), channel_id=1, source_target_pairs={{0,32},{32,64},{64,96},{96,0},{1,33},{33,65},{65,97},{97,1},{2,34}... | collective-permute-start | bytes 172040 | tf_op jit(solution)/shard_map/ppermute | solution.py:376
  28.6 0.0 copy-done.1
  28.6 1.8 %inner_3.1 = (f32[6,32,1152]{2,1,0:T(8,128)S(1)}, f32[32,1024]{1,0:T(8,128)S(1)}) custom-call(f32[6,32,1024]{2,1,0:T(8,128)S(1)} %get-tuple-element.31.rhs, f32[6,6,32,1024]{3,2,1,0:T(8,128)S(1)} %get-tuple-element.32.inverse, f32[4,32,1024]{2,1,0:T(8,128)S(1)} %get-tuple-element.33.coupling, f32[6,32,128]{2,1,0:T(8,128)S(1)} %get-tuple-element.36.rhs_rim, ...), custom_call_target="tpu_custom_call" | custom-call | flops 5898240 | bytes 8388608 | tf_op jit(solution)/shard_map/inner_3/pallas_call | solution.py:384
  30.5 0.3 collective-permute-done.6.above
  30.8 1.8 %collective-permute-done.7.below = f32[112,128]{1,0:T(8,128)S(1)} collective-permute-done((f32[112,128]{1,0:T(8,128)S(1)}, f32[112,128]{1,0:T(8,128)S(1)}, u32[]{:S(2)}, u32[]{:S(2)}) %collective-permute-start.7) | collective-permute-done | bytes 57376 | tf_op jit(solution)/shard_map/ppermute | solution.py:376
  32.6 6.8 %edges_3_and_gather.1 = (f32[512,128]{1,0:T(8,128)S(1)}, f32[6,24,1152]{2,1,0:T(8,128)S(1)}) custom-call(f32[6,32,1024]{2,1,0:T(8,128)S(1)} %get-tuple-element.31.rhs, f32[6,6,32,1024]{3,2,1,0:T(8,128)S(1)} %get-tuple-element.32.inverse, f32[4,32,1024]{2,1,0:T(8,128)S(1)} %get-tuple-element.33.coupling, f32[6,32,128]{2,1,0:T(8,128)S(1)} %get-tuple-element.36.rhs_rim, ...), custom_call_target="tpu_custom_call" | custom-call | tf_op jit(solution)/shard_map/edges_3_and_gather/pallas_call | solution.py:384
  39.4 12.8 %all_to_all.11 = f32[32,16,128]{2,1,0:T(8,128)S(1)} all-to-all(f32[32,16,128]{2,1,0:T(8,128)S(1)} %bitcast.9), channel_id=1, replica_groups=mesh['span'=4,'dom'=32] {'dom'}, dimensions={0} | all-to-all | bytes 524288 | tf_op jit(solution)/shard_map/all_to_all | solution.py:646
  52.2 4.8 %face_sums.1.part0 = f32[64,128]{1,0:T(8,128)S(1)} custom-call(f32[512,128]{1,0:T(8,128)S(1)} %bitcast.7, s32[512,128]{1,0:T(8,128)S(1)} %bitcast.8), custom_call_target="tpu_custom_call" | custom-call | tf_op jit(solution)/shard_map/face_sums/pallas_call | solution.py:560
  56.9 0.1 collective-permute-start.10
  57.0 2.2 %collective-permute-start.9 = (f32[64,128]{1,0:T(8,128)S(1)}, f32[64,128]{1,0:T(8,128)S(1)}, u32[]{:S(2)}, u32[]{:S(2)}) collective-permute-start(f32[64,128]{1,0:T(8,128)S(1)} %face_sums.1.part0), channel_id=1, source_target_pairs={{0,64},{32,96},{64,0},{96,32},{1,65},{33,97},{65,1},{97,33},{2,66}... | collective-permute-start | bytes 98312 | tf_op jit(solution)/shard_map/ppermute | solution.py:649
  59.2 0.0 collective-permute-start.8
  59.2 1.7 %collective-permute-done.10.part3 = f32[64,128]{1,0:T(8,128)S(1)} collective-permute-done((f32[64,128]{1,0:T(8,128)S(1)}, f32[64,128]{1,0:T(8,128)S(1)}, u32[]{:S(2)}, u32[]{:S(2)}) %collective-permute-start.10) | collective-permute-done | bytes 32800 | tf_op jit(solution)/shard_map/ppermute | solution.py:649
  60.9 1.6 %collective-permute-done.9.part2 = f32[64,128]{1,0:T(8,128)S(1)} collective-permute-done((f32[64,128]{1,0:T(8,128)S(1)}, f32[64,128]{1,0:T(8,128)S(1)}, u32[]{:S(2)}, u32[]{:S(2)}) %collective-permute-start.9) | collective-permute-done | bytes 32800 | tf_op jit(solution)/shard_map/ppermute | solution.py:649
  62.5 1.8 %collective-permute-done.8.part1 = f32[64,128]{1,0:T(8,128)S(1)} collective-permute-done((f32[64,128]{1,0:T(8,128)S(1)}, f32[64,128]{1,0:T(8,128)S(1)}, u32[]{:S(2)}, u32[]{:S(2)}) %collective-permute-start.8) | collective-permute-done | bytes 32800 | tf_op jit(solution)/shard_map/ppermute | solution.py:649
  64.4 0.0 copy-done.4
  64.4 3.7 %node_sums.1 = (f32[64,128]{1,0:T(8,128)}, f32[3,32,128]{2,1,0:T(8,128)S(1)}) custom-call(f32[64,128]{1,0:T(8,128)S(1)} %face_sums.1.part0, f32[64,128]{1,0:T(8,128)S(1)} %collective-permute-done.8.part1, f32[64,128]{1,0:T(8,128)S(1)} %collective-permute-done.9.part2, f32[64,128]{1,0:T(8,128)S(1)} %collective-permute-done.10.part3, ...), custom_call_target="tpu_custom_call" | custom-call | tf_op jit(solution)/shard_map/node_sums/pallas_call | solution.py:601
  68.1 0.2 collective-permute-start.14
  68.2 2.3 %collective-permute-start.13 = (f32[3,32,128]{2,1,0:T(8,128)S(1)}, f32[3,32,128]{2,1,0:T(8,128)S(1)}, u32[]{:S(2)}, u32[]{:S(2)}) collective-permute-start(f32[3,32,128]{2,1,0:T(8,128)S(1)} %get-tuple-element.56), channel_id=1, source_target_pairs={{0,64},{1,65},{2,66},{3,67},{4,68},{5,69},{6,70},{7,71},{8,72},{9,... | collective-permute-start | bytes 147464 | tf_op jit(solution)/shard_map/ppermute | solution.py:653
  70.5 1.4 %collective-permute-start.12 = (f32[3,32,128]{2,1,0:T(8,128)S(1)}, f32[3,32,128]{2,1,0:T(8,128)S(1)}, u32[]{:S(2)}, u32[]{:S(2)}) collective-permute-start(f32[3,32,128]{2,1,0:T(8,128)S(1)} %get-tuple-element.56), channel_id=1, source_target_pairs={{0,96},{1,97},{2,98},{3,99},{4,100},{5,101},{6,102},{7,103},{8,104... | collective-permute-start | bytes 147464 | tf_op jit(solution)/shard_map/ppermute | solution.py:653
  71.9 0.7 collective-permute-start.11
  72.5 2.1 %sweep_4.1 = f32[6,32,1024]{2,1,0:T(8,128)} custom-call(f32[6,32,1024]{2,1,0:T(8,128)S(1)} %get-tuple-element.31.rhs, f32[6,6,32,1024]{3,2,1,0:T(8,128)S(1)} %get-tuple-element.32.inverse, f32[4,32,1024]{2,1,0:T(8,128)S(1)} %get-tuple-element.33.coupling, f32[6,32,128]{2,1,0:T(8,128)S(1)} %get-tuple-element.36.rhs_rim, ...), custom_call_target="tpu_custom_call" | custom-call | tf_op jit(solution)/shard_map/sweep_4/pallas_call | solution.py:384
  74.6 1.6 %collective-permute-done.14.part3 = f32[3,32,128]{2,1,0:T(8,128)S(1)} collective-permute-done((f32[3,32,128]{2,1,0:T(8,128)S(1)}, f32[3,32,128]{2,1,0:T(8,128)S(1)}, u32[]{:S(2)}, u32[]{:S(2)}) %collective-permute-start.14) | collective-permute-done | bytes 49184 | tf_op jit(solution)/shard_map/ppermute | solution.py:653
  76.2 0.0 collective-permute-done.13.part2
  76.2 2.7 %collective-permute-done.12.part1 = f32[3,32,128]{2,1,0:T(8,128)S(1)} collective-permute-done((f32[3,32,128]{2,1,0:T(8,128)S(1)}, f32[3,32,128]{2,1,0:T(8,128)S(1)}, u32[]{:S(2)}, u32[]{:S(2)}) %collective-permute-start.12) | collective-permute-done | bytes 49184 | tf_op jit(solution)/shard_map/ppermute | solution.py:653
  79.0 0.0 collective-permute-done.11.part0
  79.0 0.7 add_parts.1
  (5 shorter events, 0.0 us)
Async XLA Ops:
  3.1 16.1 %copy-start = (s32[1,1,65536]{2,1,0:T(1,128)S(1)}, s32[1,1,65536]{2,1,0:T(1,128)}, u32[]{:S(2)}) copy-start(s32[1,1,65536]{2,1,0:T(1,128)} %param.12) | copy-start | bytes 786436
  3.1 21.7 %collective-permute-start.2 = (f32[56,1024]{1,0:T(8,128)S(1)}, f32[56,1024]{1,0:T(8,128)S(1)}, u32[]{:S(2)}, u32[]{:S(2)}) collective-permute-start(f32[56,1024]{1,0:T(8,128)S(1)} %get-tuple-element.40), channel_id=1, source_target_pairs={{0,96},{32,0},{64,32},{96,64},{1,97},{33,1},{65,33},{97,65},{2,98}... | collective-permute-start | bytes 688136 | tf_op jit(solution)/shard_map/ppermute | solution.py:375
  7.3 17.5 %collective-permute-start.3 = (f32[56,1024]{1,0:T(8,128)S(1)}, f32[56,1024]{1,0:T(8,128)S(1)}, u32[]{:S(2)}, u32[]{:S(2)}) collective-permute-start(f32[56,1024]{1,0:T(8,128)S(1)} %get-tuple-element.41), channel_id=1, source_target_pairs={{0,32},{32,64},{64,96},{96,0},{1,33},{33,65},{65,97},{97,1},{2,34}... | collective-permute-start | bytes 688136 | tf_op jit(solution)/shard_map/ppermute | solution.py:376
  7.3 8.0 %collective-permute-start.1 = (f32[2,32,128]{2,1,0:T(8,128)S(1)}, f32[2,32,128]{2,1,0:T(8,128)S(1)}, u32[]{:S(2)}, u32[]{:S(2)}) collective-permute-start(f32[2,32,128]{2,1,0:T(8,128)S(1)} %get-tuple-element.35), channel_id=1, source_target_pairs={{0,1},{1,2},{2,3},{3,4},{4,5},{5,6},{6,7},{7,8},{8,9},{9,10},{10,1... | collective-permute-start | bytes 98312 | tf_op jit(solution)/shard_map/ppermute | solution.py:408
  7.3 8.0 %collective-permute-start = (f32[2,32,128]{2,1,0:T(8,128)S(1)}, f32[2,32,128]{2,1,0:T(8,128)S(1)}, u32[]{:S(2)}, u32[]{:S(2)}) collective-permute-start(f32[2,32,128]{2,1,0:T(8,128)S(1)} %get-tuple-element.30.packed), channel_id=1, source_target_pairs={{0,31},{1,0},{2,1},{3,2},{4,3},{5,4},{6,5},{7,6},{8,7},{9,8},{10,9... | collective-permute-start | bytes 98312 | tf_op jit(solution)/shard_map/ppermute | solution.py:407
  15.8 6.3 %collective-permute-start.4 = (f32[160,128]{1,0:T(8,128)S(1)}, f32[160,128]{1,0:T(8,128)S(1)}, u32[]{:S(2)}, u32[]{:S(2)}) collective-permute-start(f32[160,128]{1,0:T(8,128)S(1)} %get-tuple-element.42), channel_id=1, source_target_pairs={{0,96},{32,0},{64,32},{96,64},{1,97},{33,1},{65,33},{97,65},{2,98}... | collective-permute-start | bytes 245768 | tf_op jit(solution)/shard_map/ppermute | solution.py:375
  19.1 5.7 %collective-permute-start.5 = (f32[160,128]{1,0:T(8,128)S(1)}, f32[160,128]{1,0:T(8,128)S(1)}, u32[]{:S(2)}, u32[]{:S(2)}) collective-permute-start(f32[160,128]{1,0:T(8,128)S(1)} %get-tuple-element.43), channel_id=1, source_target_pairs={{0,32},{32,64},{64,96},{96,0},{1,33},{33,65},{65,97},{97,1},{2,34}... | collective-permute-start | bytes 245768 | tf_op jit(solution)/shard_map/ppermute | solution.py:376
  22.0 6.6 %copy-start.1 = (f32[1,32,1024]{2,1,0:T(8,128)S(1)}, f32[1,32,1024]{2,1,0:T(8,128)}, u32[]{:S(2)}) copy-start(f32[1,32,1024]{2,1,0:T(8,128)} %grad.4) | copy-start | bytes 393220
  26.5 4.2 %collective-permute-start.6 = (f32[112,128]{1,0:T(8,128)S(1)}, f32[112,128]{1,0:T(8,128)S(1)}, u32[]{:S(2)}, u32[]{:S(2)}) collective-permute-start(f32[112,128]{1,0:T(8,128)S(1)} %get-tuple-element.50), channel_id=1, source_target_pairs={{0,96},{32,0},{64,32},{96,64},{1,97},{33,1},{65,33},{97,65},{2,98}... | collective-permute-start | bytes 172040 | tf_op jit(solution)/shard_map/ppermute | solution.py:375
  27.2 5.4 %collective-permute-start.7 = (f32[112,128]{1,0:T(8,128)S(1)}, f32[112,128]{1,0:T(8,128)S(1)}, u32[]{:S(2)}, u32[]{:S(2)}) collective-permute-start(f32[112,128]{1,0:T(8,128)S(1)} %get-tuple-element.51), channel_id=1, source_target_pairs={{0,32},{32,64},{64,96},{96,0},{1,33},{33,65},{65,97},{97,1},{2,34}... | collective-permute-start | bytes 172040 | tf_op jit(solution)/shard_map/ppermute | solution.py:376
  32.6 19.6 %copy-start.3 = (s32[1,1,65536]{2,1,0:T(1,128)S(1)}, s32[1,1,65536]{2,1,0:T(1,128)}, u32[]{:S(2)}) copy-start(s32[1,1,65536]{2,1,0:T(1,128)} %param.13) | copy-start | bytes 786436
  32.6 31.8 %copy-start.2 = (f32[3,4,8192]{2,1,0:T(4,128)S(1)}, f32[3,4,8192]{2,1,0:T(4,128)}, u32[]{:S(2)}) copy-start(f32[3,4,8192]{2,1,0:T(4,128)} %grad.5) | copy-start | bytes 1179652
  32.6 31.8 %copy-start.4 = (s32[4,8192]{1,0:T(4,128)S(1)}, s32[4,8192]{1,0:T(4,128)}, u32[]{:S(2)}) copy-start(s32[4,8192]{1,0:T(4,128)} %nodes.1) | copy-start | bytes 393220
  56.9 4.0 %collective-permute-start.10 = (f32[64,128]{1,0:T(8,128)S(1)}, f32[64,128]{1,0:T(8,128)S(1)}, u32[]{:S(2)}, u32[]{:S(2)}) collective-permute-start(f32[64,128]{1,0:T(8,128)S(1)} %face_sums.1.part0), channel_id=1, source_target_pairs={{0,96},{32,0},{64,32},{96,64},{1,97},{33,1},{65,33},{97,65},{2,98}... | collective-permute-start | bytes 98312 | tf_op jit(solution)/shard_map/ppermute | solution.py:649
  57.0 5.5 %collective-permute-start.9 = (f32[64,128]{1,0:T(8,128)S(1)}, f32[64,128]{1,0:T(8,128)S(1)}, u32[]{:S(2)}, u32[]{:S(2)}) collective-permute-start(f32[64,128]{1,0:T(8,128)S(1)} %face_sums.1.part0), channel_id=1, source_target_pairs={{0,64},{32,96},{64,0},{96,32},{1,65},{33,97},{65,1},{97,33},{2,66}... | collective-permute-start | bytes 98312 | tf_op jit(solution)/shard_map/ppermute | solution.py:649
  59.2 5.1 %collective-permute-start.8 = (f32[64,128]{1,0:T(8,128)S(1)}, f32[64,128]{1,0:T(8,128)S(1)}, u32[]{:S(2)}, u32[]{:S(2)}) collective-permute-start(f32[64,128]{1,0:T(8,128)S(1)} %face_sums.1.part0), channel_id=1, source_target_pairs={{0,32},{32,64},{64,96},{96,0},{1,33},{33,65},{65,97},{97,1},{2,34}... | collective-permute-start | bytes 98312 | tf_op jit(solution)/shard_map/ppermute | solution.py:649
  68.1 8.2 %collective-permute-start.14 = (f32[3,32,128]{2,1,0:T(8,128)S(1)}, f32[3,32,128]{2,1,0:T(8,128)S(1)}, u32[]{:S(2)}, u32[]{:S(2)}) collective-permute-start(f32[3,32,128]{2,1,0:T(8,128)S(1)} %get-tuple-element.56), channel_id=1, source_target_pairs={{0,32},{1,33},{2,34},{3,35},{4,36},{5,37},{6,38},{7,39},{8,40},{9,... | collective-permute-start | bytes 147464 | tf_op jit(solution)/shard_map/ppermute | solution.py:653
  68.2 8.0 %collective-permute-start.13 = (f32[3,32,128]{2,1,0:T(8,128)S(1)}, f32[3,32,128]{2,1,0:T(8,128)S(1)}, u32[]{:S(2)}, u32[]{:S(2)}) collective-permute-start(f32[3,32,128]{2,1,0:T(8,128)S(1)} %get-tuple-element.56), channel_id=1, source_target_pairs={{0,64},{1,65},{2,66},{3,67},{4,68},{5,69},{6,70},{7,71},{8,72},{9,... | collective-permute-start | bytes 147464 | tf_op jit(solution)/shard_map/ppermute | solution.py:653
  70.5 8.5 %collective-permute-start.12 = (f32[3,32,128]{2,1,0:T(8,128)S(1)}, f32[3,32,128]{2,1,0:T(8,128)S(1)}, u32[]{:S(2)}, u32[]{:S(2)}) collective-permute-start(f32[3,32,128]{2,1,0:T(8,128)S(1)} %get-tuple-element.56), channel_id=1, source_target_pairs={{0,96},{1,97},{2,98},{3,99},{4,100},{5,101},{6,102},{7,103},{8,104... | collective-permute-start | bytes 147464 | tf_op jit(solution)/shard_map/ppermute | solution.py:653
  71.9 7.1 %collective-permute-start.11 = (f32[3,32,128]{2,1,0:T(8,128)S(1)}, f32[3,32,128]{2,1,0:T(8,128)S(1)}, u32[]{:S(2)}, u32[]{:S(2)}) collective-permute-start(f32[3,32,128]{2,1,0:T(8,128)S(1)} %get-tuple-element.56), channel_id=1, source_target_pairs={{0,0},{1,1},{2,2},{3,3},{4,4},{5,5},{6,6},{7,7},{8,8},{9,9},{10,10... | collective-permute-start | bytes 147464 | tf_op jit(solution)/shard_map/ppermute | solution.py:653

commit v6 on v5

--- a/solution.py
+++ b/solution.py
@@ -25,8 +25,8 @@
 PACKED = 2
 AT_RHS = NVAR * NVAR
 AT_COUPLING = AT_RHS + NVAR
-GIVEN_ROWS = AT_COUPLING + 8
-RAW_ROWS = 56
+GIVEN_ROWS = AT_COUPLING + 5
+RAW_ROWS = 48
 AT_RIM = 2 * NVAR * (TILES + 1)
 FIELD_ROWS = 112
 FIRST_ROWS = 160
@@ -125,8 +125,8 @@
 
 def given_rows(near, second):
     rows = [(0, (b, a), near) for b in range(NVAR) for a in range(NVAR)]
-    rows += [(1, (b,), near) for b in range(NVAR)]
-    return rows + [(2, (i,), row) for row in (near, second) for i in range(4)]
+    rows += [(1, (b,), near) for b in range(NVAR)] + [(2, (i,), near) for i in range(4)]
+    return rows + [(2, (1 if near < second else 0,), second)]
 
 
 def rim_kernel(field, after, before, rhs_rim, inverse_rim, coupling_rim, field_rim, low, high):
@@ -291,9 +291,8 @@
                 inverse_halo[b, a, :, at] = halo_tile(sides, given(b * NVAR + a))
             rhs_halo[b, :, at] = halo_tile(sides, given(AT_RHS + b))
         for i in range(4):
-            coupling_halo[i, :, at] = halo_tile(
-                sides, given(AT_COUPLING + i), given(AT_COUPLING + 4 + i)
-            )
+            second = given(AT_COUPLING + 4) if i < 2 else None
+            coupling_halo[i, :, at] = halo_tile(sides, given(AT_COUPLING + i), second)
     arrays = [
         strip_tiles(own_tiles(rhs, rhs_rim), rhs_halo),
         strip_tiles(own_tiles(inverse, inverse_rim), inverse_halo),

time: 80.3 us -> 80.3 us (level)
  no operation moved by 1% of the time
where the time goes in v6:
time: 80.3 us; the launch traced here: 79.7 us
  Pallas kernels  30.4 us (38%)
  starting transfers between devices  21.4 us (27%)
  waiting for transfers between devices  14.3 us (18%)
  blocking collectives  12.8 us (16%)
    pallas_call x8, Pallas kernels, call(): pl.pallas_call(kernel, out_shape=shapes, in_specs=in_specs or [VMEM] * le...  20.7 us
    all_to_all x1, blocking collectives, shards(): lax.all_to_all(slot_vals, 'dom', split_axis=0, concat_axis=0, tiled=True)  12.8 us
    ppermute x3, starting transfers between devices, to_span_neighbours(): above = lax.ppermute(low, 'span', shifted('span', N_SPAN, -1))  8.13 us
    ppermute x3, waiting for transfers between devices, shards(): lax.ppermute(face_part, 'span', shifted('span', N_SPAN, turn))  5.12 us
    ppermute x1, starting transfers between devices, relax_and_gather(): after = lax.ppermute(first, 'dom', shifted('dom', N_DOM, -1))  5.06 us
    pallas_call x1, Pallas kernels, face_sums(): pl.pallas_call(face_kernel, out_shape=f32(FACE_HI, LANES), in_specs=[VMEM...  4.77 us
    ppermute x4, starting transfers between devices, shards(): lax.ppermute(part, ('span', 'dom'), to_node_owners(turn))  4.49 us
    ppermute x3, waiting for transfers between devices, to_span_neighbours(): below = lax.ppermute(high, 'span', shifted('span', N_SPAN, 1))  4.48 us
  transfers between devices with their start and end apart: 15, of which 8 were waited for; matrix products, arithmetic and copies ran while one was open for 0% of the time, Pallas kernels for 13%

profile of v6, /device:TPU:0, one launch (start us, length us, event | category | flops | bytes accessed | tf_op | source)
XLA Modules:
  0.0 79.7 jit_solution(17916148954815563052)
XLA Ops:
  0.6 2.4 %pack_given.1 = (f32[2,32,128]{2,1,0:T(8,128)S(1)}, f32[2,32,128]{2,1,0:T(8,128)S(1)}, f32[48,1024]{1,0:T(8,128)S(1)}, f32[48,1024]{1,0:T(8,128)S(1)}) custom-call(f32[6,32,1024]{2,1,0:T(8,128)} %rhs.3, f32[6,6,32,1024]{3,2,1,0:T(8,128)} %inverse.3, f32[4,32,1024]{2,1,0:T(8,128)} %coupling.3), custom_call_target="tpu_custom_call" | custom-call | tf_op jit(solution)/shard_map/pack_given/pallas_call | solution.py:383
  3.1 0.0 copy-start
  3.1 4.2 %collective-permute-start.2 = (f32[48,1024]{1,0:T(8,128)S(1)}, f32[48,1024]{1,0:T(8,128)S(1)}, u32[]{:S(2)}, u32[]{:S(2)}) collective-permute-start(f32[48,1024]{1,0:T(8,128)S(1)} %get-tuple-element.40), channel_id=1, source_target_pairs={{0,96},{32,0},{64,32},{96,64},{1,97},{33,1},{65,33},{97,65},{2,98}... | collective-permute-start | bytes 589832 | tf_op jit(solution)/shard_map/ppermute | solution.py:374
  7.3 0.0 collective-permute-start.3
  7.3 0.0 collective-permute-start.1
  7.3 5.1 %collective-permute-start = (f32[2,32,128]{2,1,0:T(8,128)S(1)}, f32[2,32,128]{2,1,0:T(8,128)S(1)}, u32[]{:S(2)}, u32[]{:S(2)}) collective-permute-start(f32[2,32,128]{2,1,0:T(8,128)S(1)} %get-tuple-element.30.packed), channel_id=1, source_target_pairs={{0,31},{1,0},{2,1},{3,2},{4,3},{5,4},{6,5},{7,6},{8,7},{9,8},{10,9... | collective-permute-start | bytes 98312 | tf_op jit(solution)/shard_map/ppermute | solution.py:406
  12.3 2.9 %load_and_product.1 = (f32[6,32,1024]{2,1,0:T(8,128)S(1)}, f32[6,6,32,1024]{3,2,1,0:T(8,128)S(1)}, f32[4,32,1024]{2,1,0:T(8,128)S(1)}, f32[6,32,1024]{2,1,0:T(8,128)S(1)}) custom-call(f32[6,32,1024]{2,1,0:T(8,128)} %rhs.3, f32[6,6,32,1024]{3,2,1,0:T(8,128)} %inverse.3, f32[4,32,1024]{2,1,0:T(8,128)} %coupling.3, f32[2,32,128]{2,1,0:T(8,128)S(1)} %get-tuple-element.30.packed), custom_call_target="tpu_custom_call" | custom-call | flops 2359296 | bytes 13631488 | tf_op jit(solution)/shard_map/load_and_product/pallas_call | solution.py:383
  15.2 0.0 collective-permute-done.1.before
  15.2 0.0 collective-permute-done.after
  15.3 0.5 rim_product.1
  15.8 3.3 %collective-permute-start.4 = (f32[160,128]{1,0:T(8,128)S(1)}, f32[160,128]{1,0:T(8,128)S(1)}, u32[]{:S(2)}, u32[]{:S(2)}) collective-permute-start(f32[160,128]{1,0:T(8,128)S(1)} %get-tuple-element.42), channel_id=1, source_target_pairs={{0,96},{32,0},{64,32},{96,64},{1,97},{33,1},{65,33},{97,65},{2,98}... | collective-permute-start | bytes 245768 | tf_op jit(solution)/shard_map/ppermute | solution.py:374
  19.1 0.0 collective-permute-start.5
  19.1 0.0 copy-done
  19.1 0.5 live_rows.1.live.live_list
  19.6 2.4 %inner_1_2.1 = (f32[6,32,1152]{2,1,0:T(8,128)}, f32[6,32,1152]{2,1,0:T(8,128)S(1)}) custom-call(f32[6,32,1024]{2,1,0:T(8,128)S(1)} %get-tuple-element.31.rhs, f32[6,6,32,1024]{3,2,1,0:T(8,128)S(1)} %get-tuple-element.32.inverse, f32[4,32,1024]{2,1,0:T(8,128)S(1)} %get-tuple-element.33.coupling, f32[6,32,128]{2,1,0:T(8,128)S(1)} %get-tuple-element.36.rhs_rim, ...), custom_call_target="tpu_custom_call" | custom-call | flops 5898240 | bytes 8388608 | tf_op jit(solution)/shard_map/inner_1_2/pallas_call | solution.py:383
  22.0 0.0 copy-start.1
  22.1 0.0 collective-permute-done.4.above
  22.1 2.7 %collective-permute-done.5.below = f32[160,128]{1,0:T(8,128)S(1)} collective-permute-done((f32[160,128]{1,0:T(8,128)S(1)}, f32[160,128]{1,0:T(8,128)S(1)}, u32[]{:S(2)}, u32[]{:S(2)}) %collective-permute-start.5) | collective-permute-done | bytes 81952 | tf_op jit(solution)/shard_map/ppermute | solution.py:375
  24.8 0.0 collective-permute-done.2.raw_above
  24.8 0.0 collective-permute-done.3.raw_below
  24.8 1.8 %edges_1_2.1 = (f32[6,8,1152]{2,1,0:T(8,128)S(1)}, f32[6,6,8,1152]{3,2,1,0:T(8,128)S(1)}, f32[4,8,1152]{2,1,0:T(8,128)S(1)}, f32[6,32,1152]{2,1,0:T(8,128)S(1)},...) custom-call(f32[6,32,1024]{2,1,0:T(8,128)S(1)} %get-tuple-element.31.rhs, ...), custom_call_target="tpu_custom_call" | custom-call | tf_op jit(solution)/shard_map/edges_1_2/pallas_call | solution.py:383
  26.6 0.6 collective-permute-start.6
  27.2 1.5 %collective-permute-start.7 = (f32[112,128]{1,0:T(8,128)S(1)}, f32[112,128]{1,0:T(8,128)S(1)}, u32[]{:S(2)}, u32[]{:S(2)}) collective-permute-start(f32[112,128]{1,0:T(8,128)S(1)} %get-tuple-element.51), channel_id=1, source_target_pairs={{0,32},{32,64},{64,96},{96,0},{1,33},{33,65},{65,97},{97,1},{2,34}... | collective-permute-start | bytes 172040 | tf_op jit(solution)/shard_map/ppermute | solution.py:375
  28.7 0.0 copy-done.1
  28.7 1.8 %inner_3.1 = (f32[6,32,1152]{2,1,0:T(8,128)S(1)}, f32[32,1024]{1,0:T(8,128)S(1)}) custom-call(f32[6,32,1024]{2,1,0:T(8,128)S(1)} %get-tuple-element.31.rhs, f32[6,6,32,1024]{3,2,1,0:T(8,128)S(1)} %get-tuple-element.32.inverse, f32[4,32,1024]{2,1,0:T(8,128)S(1)} %get-tuple-element.33.coupling, f32[6,32,128]{2,1,0:T(8,128)S(1)} %get-tuple-element.36.rhs_rim, ...), custom_call_target="tpu_custom_call" | custom-call | flops 5898240 | bytes 8388608 | tf_op jit(solution)/shard_map/inner_3/pallas_call | solution.py:383
  30.5 0.3 collective-permute-done.6.above
  30.8 1.8 %collective-permute-done.7.below = f32[112,128]{1,0:T(8,128)S(1)} collective-permute-done((f32[112,128]{1,0:T(8,128)S(1)}, f32[112,128]{1,0:T(8,128)S(1)}, u32[]{:S(2)}, u32[]{:S(2)}) %collective-permute-start.7) | collective-permute-done | bytes 57376 | tf_op jit(solution)/shard_map/ppermute | solution.py:375
  32.6 6.8 %edges_3_and_gather.1 = (f32[512,128]{1,0:T(8,128)S(1)}, f32[6,24,1152]{2,1,0:T(8,128)S(1)}) custom-call(f32[6,32,1024]{2,1,0:T(8,128)S(1)} %get-tuple-element.31.rhs, f32[6,6,32,1024]{3,2,1,0:T(8,128)S(1)} %get-tuple-element.32.inverse, f32[4,32,1024]{2,1,0:T(8,128)S(1)} %get-tuple-element.33.coupling, f32[6,32,128]{2,1,0:T(8,128)S(1)} %get-tuple-element.36.rhs_rim, ...), custom_call_target="tpu_custom_call" | custom-call | tf_op jit(solution)/shard_map/edges_3_and_gather/pallas_call | solution.py:383
  39.4 12.8 %all_to_all.11 = f32[32,16,128]{2,1,0:T(8,128)S(1)} all-to-all(f32[32,16,128]{2,1,0:T(8,128)S(1)} %bitcast.9), channel_id=1, replica_groups=mesh['span'=4,'dom'=32] {'dom'}, dimensions={0} | all-to-all | bytes 524288 | tf_op jit(solution)/shard_map/all_to_all | solution.py:645
  52.2 0.0 copy-done.3
  52.2 4.8 %face_sums.1.part0 = f32[64,128]{1,0:T(8,128)S(1)} custom-call(f32[512,128]{1,0:T(8,128)S(1)} %bitcast.7, s32[512,128]{1,0:T(8,128)S(1)} %bitcast.8), custom_call_target="tpu_custom_call" | custom-call | tf_op jit(solution)/shard_map/face_sums/pallas_call | solution.py:559
  57.0 0.1 collective-permute-start.10
  57.0 2.2 %collective-permute-start.9 = (f32[64,128]{1,0:T(8,128)S(1)}, f32[64,128]{1,0:T(8,128)S(1)}, u32[]{:S(2)}, u32[]{:S(2)}) collective-permute-start(f32[64,128]{1,0:T(8,128)S(1)} %face_sums.1.part0), channel_id=1, source_target_pairs={{0,64},{32,96},{64,0},{96,32},{1,65},{33,97},{65,1},{97,33},{2,66}... | collective-permute-start | bytes 98312 | tf_op jit(solution)/shard_map/ppermute | solution.py:648
  59.2 0.0 collective-permute-start.8
  59.2 1.7 %collective-permute-done.10.part3 = f32[64,128]{1,0:T(8,128)S(1)} collective-permute-done((f32[64,128]{1,0:T(8,128)S(1)}, f32[64,128]{1,0:T(8,128)S(1)}, u32[]{:S(2)}, u32[]{:S(2)}) %collective-permute-start.10) | collective-permute-done | bytes 32800 | tf_op jit(solution)/shard_map/ppermute | solution.py:648
  60.9 1.6 %collective-permute-done.9.part2 = f32[64,128]{1,0:T(8,128)S(1)} collective-permute-done((f32[64,128]{1,0:T(8,128)S(1)}, f32[64,128]{1,0:T(8,128)S(1)}, u32[]{:S(2)}, u32[]{:S(2)}) %collective-permute-start.9) | collective-permute-done | bytes 32800 | tf_op jit(solution)/shard_map/ppermute | solution.py:648
  62.5 1.8 %collective-permute-done.8.part1 = f32[64,128]{1,0:T(8,128)S(1)} collective-permute-done((f32[64,128]{1,0:T(8,128)S(1)}, f32[64,128]{1,0:T(8,128)S(1)}, u32[]{:S(2)}, u32[]{:S(2)}) %collective-permute-start.8) | collective-permute-done | bytes 32800 | tf_op jit(solution)/shard_map/ppermute | solution.py:648
  64.4 3.7 %node_sums.1 = (f32[64,128]{1,0:T(8,128)}, f32[3,32,128]{2,1,0:T(8,128)S(1)}) custom-call(f32[64,128]{1,0:T(8,128)S(1)} %face_sums.1.part0, f32[64,128]{1,0:T(8,128)S(1)} %collective-permute-done.8.part1, f32[64,128]{1,0:T(8,128)S(1)} %collective-permute-done.9.part2, f32[64,128]{1,0:T(8,128)S(1)} %collective-permute-done.10.part3, ...), custom_call_target="tpu_custom_call" | custom-call | tf_op jit(solution)/shard_map/node_sums/pallas_call | solution.py:600
  68.1 0.2 collective-permute-start.14
  68.3 2.3 %collective-permute-start.13 = (f32[3,32,128]{2,1,0:T(8,128)S(1)}, f32[3,32,128]{2,1,0:T(8,128)S(1)}, u32[]{:S(2)}, u32[]{:S(2)}) collective-permute-start(f32[3,32,128]{2,1,0:T(8,128)S(1)} %get-tuple-element.56), channel_id=1, source_target_pairs={{0,64},{1,65},{2,66},{3,67},{4,68},{5,69},{6,70},{7,71},{8,72},{9,... | collective-permute-start | bytes 147464 | tf_op jit(solution)/shard_map/ppermute | solution.py:652
  70.5 1.4 %collective-permute-start.12 = (f32[3,32,128]{2,1,0:T(8,128)S(1)}, f32[3,32,128]{2,1,0:T(8,128)S(1)}, u32[]{:S(2)}, u32[]{:S(2)}) collective-permute-start(f32[3,32,128]{2,1,0:T(8,128)S(1)} %get-tuple-element.56), channel_id=1, source_target_pairs={{0,96},{1,97},{2,98},{3,99},{4,100},{5,101},{6,102},{7,103},{8,104... | collective-permute-start | bytes 147464 | tf_op jit(solution)/shard_map/ppermute | solution.py:652
  71.9 0.7 collective-permute-start.11
  72.6 2.1 %sweep_4.1 = f32[6,32,1024]{2,1,0:T(8,128)} custom-call(f32[6,32,1024]{2,1,0:T(8,128)S(1)} %get-tuple-element.31.rhs, f32[6,6,32,1024]{3,2,1,0:T(8,128)S(1)} %get-tuple-element.32.inverse, f32[4,32,1024]{2,1,0:T(8,128)S(1)} %get-tuple-element.33.coupling, f32[6,32,128]{2,1,0:T(8,128)S(1)} %get-tuple-element.36.rhs_rim, ...), custom_call_target="tpu_custom_call" | custom-call | tf_op jit(solution)/shard_map/sweep_4/pallas_call | solution.py:383
  74.6 1.6 %collective-permute-done.14.part3 = f32[3,32,128]{2,1,0:T(8,128)S(1)} collective-permute-done((f32[3,32,128]{2,1,0:T(8,128)S(1)}, f32[3,32,128]{2,1,0:T(8,128)S(1)}, u32[]{:S(2)}, u32[]{:S(2)}) %collective-permute-start.14) | collective-permute-done | bytes 49184 | tf_op jit(solution)/shard_map/ppermute | solution.py:652
  76.2 0.0 collective-permute-done.13.part2
  76.2 2.7 %collective-permute-done.12.part1 = f32[3,32,128]{2,1,0:T(8,128)S(1)} collective-permute-done((f32[3,32,128]{2,1,0:T(8,128)S(1)}, f32[3,32,128]{2,1,0:T(8,128)S(1)}, u32[]{:S(2)}, u32[]{:S(2)}) %collective-permute-start.12) | collective-permute-done | bytes 49184 | tf_op jit(solution)/shard_map/ppermute | solution.py:652
  79.0 0.0 collective-permute-done.11.part0
  79.0 0.7 add_parts.1
  (5 shorter events, 0.0 us)
Async XLA Ops:
  3.1 16.1 %copy-start = (s32[1,1,65536]{2,1,0:T(1,128)S(1)}, s32[1,1,65536]{2,1,0:T(1,128)}, u32[]{:S(2)}) copy-start(s32[1,1,65536]{2,1,0:T(1,128)} %param.12) | copy-start | bytes 786436
  3.1 21.7 %collective-permute-start.2 = (f32[48,1024]{1,0:T(8,128)S(1)}, f32[48,1024]{1,0:T(8,128)S(1)}, u32[]{:S(2)}, u32[]{:S(2)}) collective-permute-start(f32[48,1024]{1,0:T(8,128)S(1)} %get-tuple-element.40), channel_id=1, source_target_pairs={{0,96},{32,0},{64,32},{96,64},{1,97},{33,1},{65,33},{97,65},{2,98}... | collective-permute-start | bytes 589832 | tf_op jit(solution)/shard_map/ppermute | solution.py:374
  7.3 17.5 %collective-permute-start.3 = (f32[48,1024]{1,0:T(8,128)S(1)}, f32[48,1024]{1,0:T(8,128)S(1)}, u32[]{:S(2)}, u32[]{:S(2)}) collective-permute-start(f32[48,1024]{1,0:T(8,128)S(1)} %get-tuple-element.41), channel_id=1, source_target_pairs={{0,32},{32,64},{64,96},{96,0},{1,33},{33,65},{65,97},{97,1},{2,34}... | collective-permute-start | bytes 589832 | tf_op jit(solution)/shard_map/ppermute | solution.py:375
  7.3 8.0 %collective-permute-start.1 = (f32[2,32,128]{2,1,0:T(8,128)S(1)}, f32[2,32,128]{2,1,0:T(8,128)S(1)}, u32[]{:S(2)}, u32[]{:S(2)}) collective-permute-start(f32[2,32,128]{2,1,0:T(8,128)S(1)} %get-tuple-element.35), channel_id=1, source_target_pairs={{0,1},{1,2},{2,3},{3,4},{4,5},{5,6},{6,7},{7,8},{8,9},{9,10},{10,1... | collective-permute-start | bytes 98312 | tf_op jit(solution)/shard_map/ppermute | solution.py:407
  7.3 8.0 %collective-permute-start = (f32[2,32,128]{2,1,0:T(8,128)S(1)}, f32[2,32,128]{2,1,0:T(8,128)S(1)}, u32[]{:S(2)}, u32[]{:S(2)}) collective-permute-start(f32[2,32,128]{2,1,0:T(8,128)S(1)} %get-tuple-element.30.packed), channel_id=1, source_target_pairs={{0,31},{1,0},{2,1},{3,2},{4,3},{5,4},{6,5},{7,6},{8,7},{9,8},{10,9... | collective-permute-start | bytes 98312 | tf_op jit(solution)/shard_map/ppermute | solution.py:406
  15.8 6.3 %collective-permute-start.4 = (f32[160,128]{1,0:T(8,128)S(1)}, f32[160,128]{1,0:T(8,128)S(1)}, u32[]{:S(2)}, u32[]{:S(2)}) collective-permute-start(f32[160,128]{1,0:T(8,128)S(1)} %get-tuple-element.42), channel_id=1, source_target_pairs={{0,96},{32,0},{64,32},{96,64},{1,97},{33,1},{65,33},{97,65},{2,98}... | collective-permute-start | bytes 245768 | tf_op jit(solution)/shard_map/ppermute | solution.py:374
  19.1 5.7 %collective-permute-start.5 = (f32[160,128]{1,0:T(8,128)S(1)}, f32[160,128]{1,0:T(8,128)S(1)}, u32[]{:S(2)}, u32[]{:S(2)}) collective-permute-start(f32[160,128]{1,0:T(8,128)S(1)} %get-tuple-element.43), channel_id=1, source_target_pairs={{0,32},{32,64},{64,96},{96,0},{1,33},{33,65},{65,97},{97,1},{2,34}... | collective-permute-start | bytes 245768 | tf_op jit(solution)/shard_map/ppermute | solution.py:375
  22.0 6.6 %copy-start.1 = (f32[1,32,1024]{2,1,0:T(8,128)S(1)}, f32[1,32,1024]{2,1,0:T(8,128)}, u32[]{:S(2)}) copy-start(f32[1,32,1024]{2,1,0:T(8,128)} %grad.4) | copy-start | bytes 393220
  26.6 4.2 %collective-permute-start.6 = (f32[112,128]{1,0:T(8,128)S(1)}, f32[112,128]{1,0:T(8,128)S(1)}, u32[]{:S(2)}, u32[]{:S(2)}) collective-permute-start(f32[112,128]{1,0:T(8,128)S(1)} %get-tuple-element.50), channel_id=1, source_target_pairs={{0,96},{32,0},{64,32},{96,64},{1,97},{33,1},{65,33},{97,65},{2,98}... | collective-permute-start | bytes 172040 | tf_op jit(solution)/shard_map/ppermute | solution.py:374
  27.2 5.4 %collective-permute-start.7 = (f32[112,128]{1,0:T(8,128)S(1)}, f32[112,128]{1,0:T(8,128)S(1)}, u32[]{:S(2)}, u32[]{:S(2)}) collective-permute-start(f32[112,128]{1,0:T(8,128)S(1)} %get-tuple-element.51), channel_id=1, source_target_pairs={{0,32},{32,64},{64,96},{96,0},{1,33},{33,65},{65,97},{97,1},{2,34}... | collective-permute-start | bytes 172040 | tf_op jit(solution)/shard_map/ppermute | solution.py:375
  32.6 19.6 %copy-start.3 = (s32[1,1,65536]{2,1,0:T(1,128)S(1)}, s32[1,1,65536]{2,1,0:T(1,128)}, u32[]{:S(2)}) copy-start(s32[1,1,65536]{2,1,0:T(1,128)} %param.13) | copy-start | bytes 786436
  32.6 31.8 %copy-start.2 = (f32[3,4,8192]{2,1,0:T(4,128)S(1)}, f32[3,4,8192]{2,1,0:T(4,128)}, u32[]{:S(2)}) copy-start(f32[3,4,8192]{2,1,0:T(4,128)} %grad.5) | copy-start | bytes 1179652
  32.6 31.8 %copy-start.4 = (s32[4,8192]{1,0:T(4,128)S(1)}, s32[4,8192]{1,0:T(4,128)}, u32[]{:S(2)}) copy-start(s32[4,8192]{1,0:T(4,128)} %nodes.1) | copy-start | bytes 393220
  57.0 4.0 %collective-permute-start.10 = (f32[64,128]{1,0:T(8,128)S(1)}, f32[64,128]{1,0:T(8,128)S(1)}, u32[]{:S(2)}, u32[]{:S(2)}) collective-permute-start(f32[64,128]{1,0:T(8,128)S(1)} %face_sums.1.part0), channel_id=1, source_target_pairs={{0,96},{32,0},{64,32},{96,64},{1,97},{33,1},{65,33},{97,65},{2,98}... | collective-permute-start | bytes 98312 | tf_op jit(solution)/shard_map/ppermute | solution.py:648
  57.0 5.5 %collective-permute-start.9 = (f32[64,128]{1,0:T(8,128)S(1)}, f32[64,128]{1,0:T(8,128)S(1)}, u32[]{:S(2)}, u32[]{:S(2)}) collective-permute-start(f32[64,128]{1,0:T(8,128)S(1)} %face_sums.1.part0), channel_id=1, source_target_pairs={{0,64},{32,96},{64,0},{96,32},{1,65},{33,97},{65,1},{97,33},{2,66}... | collective-permute-start | bytes 98312 | tf_op jit(solution)/shard_map/ppermute | solution.py:648
  59.2 5.1 %collective-permute-start.8 = (f32[64,128]{1,0:T(8,128)S(1)}, f32[64,128]{1,0:T(8,128)S(1)}, u32[]{:S(2)}, u32[]{:S(2)}) collective-permute-start(f32[64,128]{1,0:T(8,128)S(1)} %face_sums.1.part0), channel_id=1, source_target_pairs={{0,32},{32,64},{64,96},{96,0},{1,33},{33,65},{65,97},{97,1},{2,34}... | collective-permute-start | bytes 98312 | tf_op jit(solution)/shard_map/ppermute | solution.py:648
  68.1 8.2 %collective-permute-start.14 = (f32[3,32,128]{2,1,0:T(8,128)S(1)}, f32[3,32,128]{2,1,0:T(8,128)S(1)}, u32[]{:S(2)}, u32[]{:S(2)}) collective-permute-start(f32[3,32,128]{2,1,0:T(8,128)S(1)} %get-tuple-element.56), channel_id=1, source_target_pairs={{0,32},{1,33},{2,34},{3,35},{4,36},{5,37},{6,38},{7,39},{8,40},{9,... | collective-permute-start | bytes 147464 | tf_op jit(solution)/shard_map/ppermute | solution.py:652
  68.3 8.0 %collective-permute-start.13 = (f32[3,32,128]{2,1,0:T(8,128)S(1)}, f32[3,32,128]{2,1,0:T(8,128)S(1)}, u32[]{:S(2)}, u32[]{:S(2)}) collective-permute-start(f32[3,32,128]{2,1,0:T(8,128)S(1)} %get-tuple-element.56), channel_id=1, source_target_pairs={{0,64},{1,65},{2,66},{3,67},{4,68},{5,69},{6,70},{7,71},{8,72},{9,... | collective-permute-start | bytes 147464 | tf_op jit(solution)/shard_map/ppermute | solution.py:652
  70.5 8.5 %collective-permute-start.12 = (f32[3,32,128]{2,1,0:T(8,128)S(1)}, f32[3,32,128]{2,1,0:T(8,128)S(1)}, u32[]{:S(2)}, u32[]{:S(2)}) collective-permute-start(f32[3,32,128]{2,1,0:T(8,128)S(1)} %get-tuple-element.56), channel_id=1, source_target_pairs={{0,96},{1,97},{2,98},{3,99},{4,100},{5,101},{6,102},{7,103},{8,104... | collective-permute-start | bytes 147464 | tf_op jit(solution)/shard_map/ppermute | solution.py:652
  71.9 7.1 %collective-permute-start.11 = (f32[3,32,128]{2,1,0:T(8,128)S(1)}, f32[3,32,128]{2,1,0:T(8,128)S(1)}, u32[]{:S(2)}, u32[]{:S(2)}) collective-permute-start(f32[3,32,128]{2,1,0:T(8,128)S(1)} %get-tuple-element.56), channel_id=1, source_target_pairs={{0,0},{1,1},{2,2},{3,3},{4,4},{5,5},{6,6},{7,7},{8,8},{9,9},{10,10... | collective-permute-start | bytes 147464 | tf_op jit(solution)/shard_map/ppermute | solution.py:652
